TPU v7x, 32 devices: a whole 2x2x4 slice. The times are simulated.
32 devices in a mesh: grp: 2 (over y), segment: 2 (over core), row: 4 (over z), col: 2 (over x).
Axes of the slice: x: 2, y: 2, z: 4, core: 2. Of those that a mesh axis runs over, the one named last changes fastest.
Arguments:
- latent: bfloat16 [4, 16, 128, 320], P('grp', 'row', 'col'), parts along dimension 0, may hold values from -6 to 6
- enc_first: bfloat16 [9, 320, 320], P(None, None, 'row'), may hold values from -0.15625 to 0.15625
- enc_first_bias: float32 [320], replicated, may hold values from -3 to 3
- enc_second: bfloat16 [9, 320, 320], P(None, None, 'row'), may hold values from -0.15625 to 0.15625
- enc_second_bias: float32 [320], replicated, may hold values from -3 to 3
- mid_weight: bfloat16 [9, 320, 640], P(None, None, 'row'), may hold values from -0.15625 to 0.15625
- mid_bias: float32 [640], replicated, may hold values from -3 to 3
- dec_first: bfloat16 [9, 960, 320], P(None, None, 'row'), may hold values from -0.09375 to 0.09375
- dec_first_bias: float32 [320], replicated, may hold values from -3 to 3
- dec_second: bfloat16 [9, 320, 320], P(None, None, 'row'), may hold values from -0.15625 to 0.15625
- dec_second_bias: float32 [320], replicated, may hold values from -3 to 3
Outputs:
- decoded: bfloat16 [4, 16, 128, 320], P(('grp', 'segment'), 'row', 'col'), parts along dimension 0
There are 2 independent parts, one for each index of `grp`. A program takes and returns all parts, laid end to end along the dimension named above; an argument that names none is the same for every part. Nothing has to cross between parts.
All inputs are finite; a program needn't handle non-finite values.
Results may differ from a plain program's by a relative error of at most 0.0075.
Values may be sent and summed in bfloat16 or wider, within the bound.
No kernel may reach another device: no remote copies, remote signals or barrier semaphores. Data moves between devices by JAX's collectives and lax.ppermute only.
A program may use at most 128 MiB of HBM per device.

v0:
```python
import jax
import jax.numpy as jnp
from jax import lax
from jax.sharding import PartitionSpec as P


def with_halo(block, sides, width):
    for axis, dim in sides:
        count = lax.axis_size(axis)
        forward = [(i, i + 1) for i in range(count - 1)]
        backward = [(target, source) for source, target in forward]
        low = lax.ppermute(
            lax.slice_in_dim(block, block.shape[dim] - width, None, axis=dim), axis, forward
        )
        high = lax.ppermute(lax.slice_in_dim(block, 0, width, axis=dim), axis, backward)
        block = jnp.concatenate([low, block, high], axis=dim)
    return block


def from_behind(value, axis, by):
    size = lax.axis_size(axis)
    pairs = [(i, i + by) for i in range(size) if 0 <= i + by < size]
    return lax.ppermute(value, axis, pairs)


def convolve(inputs, weight, bias, active):
    padded = with_halo(inputs, (("row", 1), ("col", 2)), 1)
    full_weight = lax.all_gather(weight, "row", axis=2, tiled=True)
    rows, cols = (inputs.shape[1], inputs.shape[2])
    out_shape = inputs.shape[:3] + (full_weight.shape[2],)

    def compute(operands):
        extended, weights = operands
        total = jnp.zeros(out_shape, jnp.float32)
        for tap in range(9):
            shift_row, shift_col = (tap // 3, tap % 3)
            window = extended[:, shift_row : shift_row + rows, shift_col : shift_col + cols, :]
            total = total + jnp.einsum(
                "brck,kn->brcn", window, weights[tap], preferred_element_type=jnp.float32
            )
        return jax.nn.silu(total + bias).astype(jnp.bfloat16)

    def skipped(operands):
        return jnp.zeros(out_shape, jnp.bfloat16)

    return lax.cond(active, compute, skipped, (padded, full_weight))


def pool_cells(inputs):
    batch, rows, cols, chans = inputs.shape
    blocks = inputs.astype(jnp.float32).reshape(batch, rows // 2, 2, cols // 2, 2, chans)
    return jnp.mean(blocks, axis=(2, 4)).astype(jnp.bfloat16)


def shards(
    latent,
    enc_first,
    enc_first_bias,
    enc_second,
    enc_second_bias,
    mid_weight,
    mid_bias,
    dec_first,
    dec_first_bias,
    dec_second,
    dec_second_bias,
):
    leading = lax.axis_index("segment") == 0
    trailing = jnp.logical_not(leading)
    hidden = convolve(latent, enc_first, enc_first_bias, leading)
    skips = convolve(hidden, enc_second, enc_second_bias, leading)
    pooled = pool_cells(skips)
    arrived = from_behind(pooled, "segment", 1)
    middle = convolve(arrived, mid_weight, mid_bias, trailing)
    returned = from_behind(middle, "segment", -1)
    upsampled = jnp.repeat(jnp.repeat(returned, 2, axis=1), 2, axis=2)
    joined = jnp.concatenate([skips, upsampled], axis=3)
    refined = convolve(joined, dec_first, dec_first_bias, leading)
    outputs = convolve(refined, dec_second, dec_second_bias, leading)
    shipped = from_behind(outputs[1:2], "segment", 1)
    result = jnp.where(leading, outputs[0:1], shipped)
    return result


def solution(mesh):
    placed = (
        P("grp", "row", "col", None),
        P(None, None, "row"),
        P(),
        P(None, None, "row"),
        P(),
        P(None, None, "row"),
        P(),
        P(None, None, "row"),
        P(),
        P(None, None, "row"),
        P(),
    )
    return jax.shard_map(
        shards,
        mesh=mesh,
        in_specs=placed,
        out_specs=P(("grp", "segment"), "row", "col", None),
        check_vma=False,
    )
```

profile of v0, /device:TPU:0, one launch (start us, length us, event | category | flops | bytes accessed | tf_op | source)
XLA Modules:
  0.0 374.6 jit_solution(9221154168002223844)
XLA Ops:
  9.4 4.9 %collective-permute-start = (bf16[2,1,64,320]{3,2,1,0:T(8,128)(2,1)S(1)}, bf16[2,1,64,320]{3,2,1,0:T(8,128)(2,1)S(1)}, u32[]{:S(2)}, u32[]{:S(2)}) collective-permute-start(bf16[2,1,64,320]{3,2,1,0:T(8,128)(2,1)S(1)} %get-tuple-element.143), channel_id=1, source_target_pairs={{0,2},{2,4},{4,6},{1,3},{3,5},{5,7},{8,10},{10,12},{12,14},{9,11},... | collective-permute-start | bytes 245768 | tf_op jit(solution)/shard_map/ppermute | solution.py:12
  16.6 4.2 %collective-permute-done.1 = bf16[2,1,64,320]{3,2,1,0:T(8,128)(2,1)S(1)} collective-permute-done((bf16[2,1,64,320]{3,2,1,0:T(8,128)(2,1)S(1)}, bf16[2,1,64,320]{3,2,1,0:T(8,128)(2,1)S(1)}, u32[]{:S(2)}, u32[]{:S(2)}) %collective-permute-start.1) | collective-permute-done | bytes 81952 | tf_op jit(solution)/shard_map/ppermute | solution.py:15
  20.9 3.4 collective-permute-start.2
  25.8 4.2 %collective-permute-done.3 = bf16[2,6,1,320]{3,2,1,0:T(2,128)(2,1)S(1)} collective-permute-done((bf16[2,6,1,320]{3,2,1,0:T(2,128)(2,1)S(1)}, bf16[2,6,1,320]{3,2,1,0:T(2,128)(2,1)S(1)}, u32[]{:S(2)}, u32[]{:S(2)}) %collective-permute-start.3) | collective-permute-done | bytes 7712 | tf_op jit(solution)/shard_map/ppermute | solution.py:15
  30.2 29.4 %all-gather.6.cloned.1.call-done = bf16[9,320,320]{1,2,0:T(8,128)(2,1)} async-done(((bf16[9,320,80]{1,2,0:T(8,128)(2,1)}), bf16[9,320,320]{1,2,0:T(8,128)(2,1)}) %all-gather.6.cloned.1.call-update) | async-done | bytes 1843216 | tf_op jit(solution)/shard_map/all_gather | solution.py:28
  59.7 6.7 %conditional.5 = (bf16[2,4,64,320]{3,2,1,0:T(8,128)(2,1)S(1)}) conditional(s32[]{:T(128)} %convert_element_type.31, () %tuple.42, (bf16[2,6,66,320]{3,2,1,0:T(8,128)(2,1)S(1)}, bf16[9,320,320]{1,2,0:T(8,128)(2,1)}, bf16[2,6,64,320]{3,2,1,0:T(8,128)(2,1)S(1)}, bf16[2,4,64,320]{3,2,1,0:T(8,128)(2,1)}, f32[320]{0:T(512)S(1)}) %tuple.86), branch_computations={%region_0.0_spmd, %region_1.2_spmd} | conditional | flops 946012160 | bytes 23005220 | solution.py:46
  59.7 3.0 copy.21
  69.7 2.7 collective-permute-done.4
  72.3 7.7 %collective-permute-done.5 = bf16[2,1,64,320]{3,2,1,0:T(8,128)(2,1)S(1)} collective-permute-done((bf16[2,1,64,320]{3,2,1,0:T(8,128)(2,1)S(1)}, bf16[2,1,64,320]{3,2,1,0:T(8,128)(2,1)S(1)}, u32[]{:S(2)}, u32[]{:S(2)}) %collective-permute-start.5) | collective-permute-done | bytes 81952 | tf_op jit(solution)/shard_map/ppermute | solution.py:15
  80.2 3.4 collective-permute-start.6
  85.1 4.2 %collective-permute-done.7 = bf16[2,6,1,320]{3,2,1,0:T(2,128)(2,1)S(1)} collective-permute-done((bf16[2,6,1,320]{3,2,1,0:T(2,128)(2,1)S(1)}, bf16[2,6,1,320]{3,2,1,0:T(2,128)(2,1)S(1)}, u32[]{:S(2)}, u32[]{:S(2)}) %collective-permute-start.7) | collective-permute-done | bytes 7712 | tf_op jit(solution)/shard_map/ppermute | solution.py:15
  89.5 19.6 %all-gather.8.cloned.1.call-done = bf16[9,320,320]{1,2,0:T(8,128)(2,1)} async-done(((bf16[9,320,80]{1,2,0:T(8,128)(2,1)}), bf16[9,320,320]{1,2,0:T(8,128)(2,1)}) %all-gather.8.cloned.1.call-update) | async-done | bytes 1843216 | tf_op jit(solution)/shard_map/all_gather | solution.py:28
  109.1 9.5 %conditional.6 = (bf16[2,4,64,320]{3,2,1,0:T(8,128)(2,1)}, f32[2,2,32,320]{3,2,1,0:T(8,128)S(1)}) conditional(s32[]{:T(128)} %convert_element_type.31, () %tuple.41, (bf16[2,6,66,320]{3,2,1,0:T(8,128)(2,1)S(1)}, bf16[9,320,320]{1,2,0:T(8,128)(2,1)}, bf16[2,6,64,320]{3,2,1,0:T(8,128)(2,1)}, bf16[2,4,64,320]{3,2,1,0:T(8,128)(2,1)S(1)}, ...), branch_computations={%region_2.3_spmd, %region_3.0_spmd} | conditional | flops 946135040 | bytes 25462832 | solution.py:46
  109.1 3.0 copy.22
  125.9 5.4 %collective-permute-done.10 = bf16[2,1,32,320]{3,2,1,0:T(8,128)(2,1)S(1)} collective-permute-done((bf16[2,1,32,320]{3,2,1,0:T(8,128)(2,1)S(1)}, bf16[2,1,32,320]{3,2,1,0:T(8,128)(2,1)S(1)}, u32[]{:S(2)}, u32[]{:S(2)}) %collective-permute-start.10) | collective-permute-done | bytes 40992 | tf_op jit(solution)/shard_map/ppermute | solution.py:15
  131.3 3.4 collective-permute-start.11
  136.0 4.2 %collective-permute-done.12 = bf16[2,4,1,320]{3,2,1,0:T(2,128)(2,1)S(1)} collective-permute-done((bf16[2,4,1,320]{3,2,1,0:T(2,128)(2,1)S(1)}, bf16[2,4,1,320]{3,2,1,0:T(2,128)(2,1)S(1)}, u32[]{:S(2)}, u32[]{:S(2)}) %collective-permute-start.12) | collective-permute-done | bytes 5152 | tf_op jit(solution)/shard_map/ppermute | solution.py:15
  140.3 54.9 %all-gather.10.cloned.1.call-done = bf16[9,320,640]{1,2,0:T(8,128)(2,1)} async-done(((bf16[9,320,160]{1,2,0:T(8,128)(2,1)}), bf16[9,320,640]{1,2,0:T(8,128)(2,1)}) %all-gather.10.cloned.1.call-update) | async-done | bytes 3686416 | tf_op jit(solution)/shard_map/all_gather | solution.py:28
  196.7 15.1 %collective-permute-done.13 = bf16[2,2,32,640]{3,2,1,0:T(8,128)(2,1)S(1)} collective-permute-done((bf16[2,2,32,640]{3,2,1,0:T(8,128)(2,1)S(1)}, bf16[2,2,32,640]{3,2,1,0:T(8,128)(2,1)S(1)}, u32[]{:S(2)}, u32[]{:S(2)}) %collective-permute-start.13) | collective-permute-done | bytes 163872 | tf_op jit(solution)/shard_map/ppermute | solution.py:23
  216.3 10.8 %collective-permute-done.14 = bf16[2,1,64,960]{3,2,1,0:T(8,128)(2,1)S(1)} collective-permute-done((bf16[2,1,64,960]{3,2,1,0:T(8,128)(2,1)S(1)}, bf16[2,1,64,960]{3,2,1,0:T(8,128)(2,1)S(1)}, u32[]{:S(2)}, u32[]{:S(2)}) %collective-permute-start.14) | collective-permute-done | bytes 245792 | tf_op jit(solution)/shard_map/ppermute | solution.py:12
  227.0 12.2 %collective-permute-done.15 = bf16[2,1,64,960]{3,2,1,0:T(8,128)(2,1)S(1)} collective-permute-done((bf16[2,1,64,960]{3,2,1,0:T(8,128)(2,1)S(1)}, bf16[2,1,64,960]{3,2,1,0:T(8,128)(2,1)S(1)}, u32[]{:S(2)}, u32[]{:S(2)}) %collective-permute-start.15) | collective-permute-done | bytes 245792 | tf_op jit(solution)/shard_map/ppermute | solution.py:15
  240.8 3.4 collective-permute-start.16
  250.2 3.3 pad_maximum_fusion
  253.5 56.1 %all-gather.12.cloned.1.call-done = bf16[9,960,320]{1,2,0:T(8,128)(2,1)} async-done(((bf16[9,960,80]{1,2,0:T(8,128)(2,1)}), bf16[9,960,320]{1,2,0:T(8,128)(2,1)}) %all-gather.12.cloned.1.call-update) | async-done | bytes 5529616 | tf_op jit(solution)/shard_map/all_gather | solution.py:28
  309.6 11.2 %conditional.8 = (bf16[2,4,64,320]{3,2,1,0:T(8,128)(2,1)S(1)}) conditional(s32[]{:T(128)} %convert_element_type.31, () %tuple.40, (bf16[2,6,66,960]{3,2,1,0:T(8,128)(2,1)}, bf16[9,960,320]{1,2,0:T(8,128)(2,1)}, bf16[2,6,64,960]{3,2,1,0:T(8,128)(2,1)S(1)}, bf16[2,4,64,960]{3,2,1,0:T(8,128)(2,1)}, f32[320]{0:T(512)S(1)}) %tuple.88), branch_computations={%region_7.8_spmd, %region_8.9_spmd} | conditional | flops 2833448960 | bytes 60381276 | solution.py:46
  323.6 2.7 collective-permute-done.18
  326.3 6.3 %collective-permute-done.19 = bf16[2,1,64,320]{3,2,1,0:T(8,128)(2,1)S(1)} collective-permute-done((bf16[2,1,64,320]{3,2,1,0:T(8,128)(2,1)S(1)}, bf16[2,1,64,320]{3,2,1,0:T(8,128)(2,1)S(1)}, u32[]{:S(2)}, u32[]{:S(2)}) %collective-permute-start.19) | collective-permute-done | bytes 81952 | tf_op jit(solution)/shard_map/ppermute | solution.py:15
  332.8 3.4 collective-permute-start.20
  337.6 4.2 %collective-permute-done.21 = bf16[2,6,1,320]{3,2,1,0:T(2,128)(2,1)S(1)} collective-permute-done((bf16[2,6,1,320]{3,2,1,0:T(2,128)(2,1)S(1)}, bf16[2,6,1,320]{3,2,1,0:T(2,128)(2,1)S(1)}, u32[]{:S(2)}, u32[]{:S(2)}) %collective-permute-start.21) | collective-permute-done | bytes 7712 | tf_op jit(solution)/shard_map/ppermute | solution.py:15
  342.1 16.2 %all-gather.14.cloned.1.call-done = bf16[9,320,320]{1,2,0:T(8,128)(2,1)} async-done(((bf16[9,320,80]{1,2,0:T(8,128)(2,1)}), bf16[9,320,320]{1,2,0:T(8,128)(2,1)}) %all-gather.14.cloned.1.call-update) | async-done | bytes 1843216 | tf_op jit(solution)/shard_map/all_gather | solution.py:28
  358.3 6.7 %conditional.9 = (bf16[2,4,64,320]{3,2,1,0:T(8,128)(2,1)S(1)}) conditional(s32[]{:T(128)} %convert_element_type.31, () %tuple.39, (bf16[2,6,66,320]{3,2,1,0:T(8,128)(2,1)S(1)}, bf16[9,320,320]{1,2,0:T(8,128)(2,1)}, bf16[2,6,64,320]{3,2,1,0:T(8,128)(2,1)}, bf16[2,4,64,320]{3,2,1,0:T(8,128)(2,1)S(1)}, f32[320]{0:T(512)S(1)}) %tuple.89), branch_computations={%region_9.10_spmd, %region_10.11_spmd} | conditional | flops 946012160 | bytes 23660580 | solution.py:46
  358.3 3.0 copy.24
  (135 shorter events, 66.6 us)
Async XLA Ops:
  6.5 53.1 %all-gather.6.cloned.1.call-start = ((), (), s32[]{:S(2)}) async-start(), calls=%async_computation | async-start | bytes 2764800 | tf_op jit(solution)/shard_map/all_gather | solution.py:28
  7.3 101.9 %all-gather.8.cloned.1.call-start = ((), (), s32[]{:S(2)}) async-start(), calls=%async_computation.1 | async-start | bytes 2764800 | tf_op jit(solution)/shard_map/all_gather | solution.py:28
  8.0 187.2 %all-gather.10.cloned.1.call-start = ((), (), s32[]{:S(2)}) async-start(), calls=%async_computation.2 | async-start | bytes 5529600 | tf_op jit(solution)/shard_map/all_gather | solution.py:28
  8.7 50.9 %copy-start.11 = (f32[320]{0:T(512)S(1)}, f32[320]{0:T(512)}, u32[]{:S(2)}) copy-start(f32[320]{0:T(512)} %param.23) | copy-start | bytes 3844
  8.8 300.8 %all-gather.12.cloned.1.call-start = ((), (), s32[]{:S(2)}) async-start(), calls=%async_computation.3 | async-start | bytes 7372800 | tf_op jit(solution)/shard_map/all_gather | solution.py:28
  9.3 348.9 %all-gather.14.cloned.1.call-start = ((), (), s32[]{:S(2)}) async-start(), calls=%async_computation.4 | async-start | bytes 2764800 | tf_op jit(solution)/shard_map/all_gather | solution.py:28
  9.4 7.1 %collective-permute-start = (bf16[2,1,64,320]{3,2,1,0:T(8,128)(2,1)S(1)}, bf16[2,1,64,320]{3,2,1,0:T(8,128)(2,1)S(1)}, u32[]{:S(2)}, u32[]{:S(2)}) collective-permute-start(bf16[2,1,64,320]{3,2,1,0:T(8,128)(2,1)S(1)} %get-tuple-element.143), channel_id=1, source_target_pairs={{0,2},{2,4},{4,6},{1,3},{3,5},{5,7},{8,10},{10,12},{12,14},{9,11},... | collective-permute-start | bytes 245768 | tf_op jit(solution)/shard_map/ppermute | solution.py:12
  14.4 6.5 %collective-permute-start.1 = (bf16[2,1,64,320]{3,2,1,0:T(8,128)(2,1)S(1)}, bf16[2,1,64,320]{3,2,1,0:T(8,128)(2,1)S(1)}, u32[]{:S(2)}, u32[]{:S(2)}) collective-permute-start(bf16[2,1,64,320]{3,2,1,0:T(8,128)(2,1)S(1)} %get-tuple-element.142), channel_id=1, source_target_pairs={{2,0},{4,2},{6,4},{3,1},{5,3},{7,5},{10,8},{12,10},{14,12},{11,9},... | collective-permute-start | bytes 245768 | tf_op jit(solution)/shard_map/ppermute | solution.py:15
  20.9 4.8 %collective-permute-start.2 = (bf16[2,6,1,320]{3,2,1,0:T(2,128)(2,1)S(1)}, bf16[2,6,1,320]{3,2,1,0:T(2,128)(2,1)S(1)}, u32[]{:S(2)}, u32[]{:S(2)}) collective-permute-start(bf16[2,6,1,320]{3,2,1,0:T(2,128)(2,1)S(1)} %get-tuple-element.136), channel_id=1, source_target_pairs={{0,1},{2,3},{4,5},{6,7},{8,9},{10,11},{12,13},{14,15},{16,17},{18,... | collective-permute-start | bytes 23048 | tf_op jit(solution)/shard_map/ppermute | solution.py:12
  24.3 5.7 %collective-permute-start.3 = (bf16[2,6,1,320]{3,2,1,0:T(2,128)(2,1)S(1)}, bf16[2,6,1,320]{3,2,1,0:T(2,128)(2,1)S(1)}, u32[]{:S(2)}, u32[]{:S(2)}) collective-permute-start(bf16[2,6,1,320]{3,2,1,0:T(2,128)(2,1)S(1)} %get-tuple-element.137), channel_id=1, source_target_pairs={{1,0},{3,2},{5,4},{7,6},{9,8},{11,10},{13,12},{15,14},{17,16},{19,... | collective-permute-start | bytes 23048 | tf_op jit(solution)/shard_map/ppermute | solution.py:15
  66.4 42.7 %copy-start.12 = (f32[320]{0:T(512)S(1)}, f32[320]{0:T(512)}, u32[]{:S(2)}) copy-start(f32[320]{0:T(512)} %param.25) | copy-start | bytes 3844
  66.5 5.9 %collective-permute-start.4 = (bf16[2,1,64,320]{3,2,1,0:T(8,128)(2,1)S(1)}, bf16[2,1,64,320]{3,2,1,0:T(8,128)(2,1)S(1)}, u32[]{:S(2)}, u32[]{:S(2)}) collective-permute-start(bf16[2,1,64,320]{3,2,1,0:T(8,128)(2,1)S(1)} %get-tuple-element.140), channel_id=1, source_target_pairs={{0,2},{2,4},{4,6},{1,3},{3,5},{5,7},{8,10},{10,12},{12,14},{9,11},... | collective-permute-start | bytes 245768 | tf_op jit(solution)/shard_map/ppermute | solution.py:12
  68.4 11.6 %collective-permute-start.5 = (bf16[2,1,64,320]{3,2,1,0:T(8,128)(2,1)S(1)}, bf16[2,1,64,320]{3,2,1,0:T(8,128)(2,1)S(1)}, u32[]{:S(2)}, u32[]{:S(2)}) collective-permute-start(bf16[2,1,64,320]{3,2,1,0:T(8,128)(2,1)S(1)} %get-tuple-element.141), channel_id=1, source_target_pairs={{2,0},{4,2},{6,4},{3,1},{5,3},{7,5},{10,8},{12,10},{14,12},{11,9},... | collective-permute-start | bytes 245768 | tf_op jit(solution)/shard_map/ppermute | solution.py:15
  80.2 4.8 %collective-permute-start.6 = (bf16[2,6,1,320]{3,2,1,0:T(2,128)(2,1)S(1)}, bf16[2,6,1,320]{3,2,1,0:T(2,128)(2,1)S(1)}, u32[]{:S(2)}, u32[]{:S(2)}) collective-permute-start(bf16[2,6,1,320]{3,2,1,0:T(2,128)(2,1)S(1)} %get-tuple-element.134), channel_id=1, source_target_pairs={{0,1},{2,3},{4,5},{6,7},{8,9},{10,11},{12,13},{14,15},{16,17},{18,... | collective-permute-start | bytes 23048 | tf_op jit(solution)/shard_map/ppermute | solution.py:12
  83.6 5.7 %collective-permute-start.7 = (bf16[2,6,1,320]{3,2,1,0:T(2,128)(2,1)S(1)}, bf16[2,6,1,320]{3,2,1,0:T(2,128)(2,1)S(1)}, u32[]{:S(2)}, u32[]{:S(2)}) collective-permute-start(bf16[2,6,1,320]{3,2,1,0:T(2,128)(2,1)S(1)} %get-tuple-element.135), channel_id=1, source_target_pairs={{1,0},{3,2},{5,4},{7,6},{9,8},{11,10},{13,12},{15,14},{17,16},{19,... | collective-permute-start | bytes 23048 | tf_op jit(solution)/shard_map/ppermute | solution.py:15
  109.1 86.1 %copy-start.10 = (f32[640]{0:T(1024)S(1)}, f32[640]{0:T(1024)}, u32[]{:S(2)}) copy-start(f32[640]{0:T(1024)} %param.27) | copy-start | bytes 7684
  118.7 2.2 collective-permute-start.8
  120.9 4.9 %collective-permute-start.9 = (bf16[2,1,32,320]{3,2,1,0:T(8,128)(2,1)S(1)}, bf16[2,1,32,320]{3,2,1,0:T(8,128)(2,1)S(1)}, u32[]{:S(2)}, u32[]{:S(2)}) collective-permute-start(bf16[2,1,32,320]{3,2,1,0:T(8,128)(2,1)S(1)} %get-tuple-element.147), channel_id=1, source_target_pairs={{0,2},{2,4},{4,6},{1,3},{3,5},{5,7},{8,10},{10,12},{12,14},{9,11},... | collective-permute-start | bytes 122888 | tf_op jit(solution)/shard_map/ppermute | solution.py:12
  122.9 8.3 %collective-permute-start.10 = (bf16[2,1,32,320]{3,2,1,0:T(8,128)(2,1)S(1)}, bf16[2,1,32,320]{3,2,1,0:T(8,128)(2,1)S(1)}, u32[]{:S(2)}, u32[]{:S(2)}) collective-permute-start(bf16[2,1,32,320]{3,2,1,0:T(8,128)(2,1)S(1)} %get-tuple-element.146), channel_id=1, source_target_pairs={{2,0},{4,2},{6,4},{3,1},{5,3},{7,5},{10,8},{12,10},{14,12},{11,9},... | collective-permute-start | bytes 122888 | tf_op jit(solution)/shard_map/ppermute | solution.py:15
  131.3 4.7 %collective-permute-start.11 = (bf16[2,4,1,320]{3,2,1,0:T(2,128)(2,1)S(1)}, bf16[2,4,1,320]{3,2,1,0:T(2,128)(2,1)S(1)}, u32[]{:S(2)}, u32[]{:S(2)}) collective-permute-start(bf16[2,4,1,320]{3,2,1,0:T(2,128)(2,1)S(1)} %get-tuple-element.144), channel_id=1, source_target_pairs={{0,1},{2,3},{4,5},{6,7},{8,9},{10,11},{12,13},{14,15},{16,17},{18,... | collective-permute-start | bytes 15368 | tf_op jit(solution)/shard_map/ppermute | solution.py:12
  134.7 5.6 %collective-permute-start.12 = (bf16[2,4,1,320]{3,2,1,0:T(2,128)(2,1)S(1)}, bf16[2,4,1,320]{3,2,1,0:T(2,128)(2,1)S(1)}, u32[]{:S(2)}, u32[]{:S(2)}) collective-permute-start(bf16[2,4,1,320]{3,2,1,0:T(2,128)(2,1)S(1)} %get-tuple-element.145), channel_id=1, source_target_pairs={{1,0},{3,2},{5,4},{7,6},{9,8},{11,10},{13,12},{15,14},{17,16},{19,... | collective-permute-start | bytes 15368 | tf_op jit(solution)/shard_map/ppermute | solution.py:15
  195.4 16.4 %collective-permute-start.13 = (bf16[2,2,32,640]{3,2,1,0:T(8,128)(2,1)S(1)}, bf16[2,2,32,640]{3,2,1,0:T(8,128)(2,1)S(1)}, u32[]{:S(2)}, u32[]{:S(2)}) collective-permute-start(bf16[2,2,32,640]{3,2,1,0:T(8,128)(2,1)S(1)} %get-tuple-element.153), channel_id=1, source_target_pairs={{8,0},{9,1},{10,2},{11,3},{12,4},{13,5},{14,6},{15,7},{24,16},{25,... | collective-permute-start | bytes 491528 | tf_op jit(solution)/shard_map/ppermute | solution.py:23
  213.6 13.4 %collective-permute-start.14 = (bf16[2,1,64,960]{3,2,1,0:T(8,128)(2,1)S(1)}, bf16[2,1,64,960]{3,2,1,0:T(8,128)(2,1)S(1)}, u32[]{:S(2)}, u32[]{:S(2)}) collective-permute-start(bf16[2,1,64,960]{3,2,1,0:T(8,128)(2,1)S(1)} %get-tuple-element.130), channel_id=1, source_target_pairs={{0,2},{2,4},{4,6},{1,3},{3,5},{5,7},{8,10},{10,12},{12,14},{9,11},... | collective-permute-start | bytes 737288 | tf_op jit(solution)/shard_map/ppermute | solution.py:12
  215.0 24.3 %collective-permute-start.15 = (bf16[2,1,64,960]{3,2,1,0:T(8,128)(2,1)S(1)}, bf16[2,1,64,960]{3,2,1,0:T(8,128)(2,1)S(1)}, u32[]{:S(2)}, u32[]{:S(2)}) collective-permute-start(bf16[2,1,64,960]{3,2,1,0:T(8,128)(2,1)S(1)} %get-tuple-element.131), channel_id=1, source_target_pairs={{2,0},{4,2},{6,4},{3,1},{5,3},{7,5},{10,8},{12,10},{14,12},{11,9},... | collective-permute-start | bytes 737288 | tf_op jit(solution)/shard_map/ppermute | solution.py:15
  240.8 7.2 %collective-permute-start.16 = (bf16[2,6,1,960]{3,2,1,0:T(2,128)(2,1)S(1)}, bf16[2,6,1,960]{3,2,1,0:T(2,128)(2,1)S(1)}, u32[]{:S(2)}, u32[]{:S(2)}) collective-permute-start(bf16[2,6,1,960]{3,2,1,0:T(2,128)(2,1)S(1)} %get-tuple-element.128), channel_id=1, source_target_pairs={{0,1},{2,3},{4,5},{6,7},{8,9},{10,11},{12,13},{14,15},{16,17},{18,... | collective-permute-start | bytes 69128 | tf_op jit(solution)/shard_map/ppermute | solution.py:12
  244.2 6.0 %collective-permute-start.17 = (bf16[2,6,1,960]{3,2,1,0:T(2,128)(2,1)S(1)}, bf16[2,6,1,960]{3,2,1,0:T(2,128)(2,1)S(1)}, u32[]{:S(2)}, u32[]{:S(2)}) collective-permute-start(bf16[2,6,1,960]{3,2,1,0:T(2,128)(2,1)S(1)} %get-tuple-element.129), channel_id=1, source_target_pairs={{1,0},{3,2},{5,4},{7,6},{9,8},{11,10},{13,12},{15,14},{17,16},{19,... | collective-permute-start | bytes 69128 | tf_op jit(solution)/shard_map/ppermute | solution.py:15
  248.0 61.6 %copy-start.13 = (f32[320]{0:T(512)S(1)}, f32[320]{0:T(512)}, u32[]{:S(2)}) copy-start(f32[320]{0:T(512)} %param.29) | copy-start | bytes 3844
  320.8 5.5 %collective-permute-start.18 = (bf16[2,1,64,320]{3,2,1,0:T(8,128)(2,1)S(1)}, bf16[2,1,64,320]{3,2,1,0:T(8,128)(2,1)S(1)}, u32[]{:S(2)}, u32[]{:S(2)}) collective-permute-start(bf16[2,1,64,320]{3,2,1,0:T(8,128)(2,1)S(1)} %get-tuple-element.138), channel_id=1, source_target_pairs={{0,2},{2,4},{4,6},{1,3},{3,5},{5,7},{8,10},{10,12},{12,14},{9,11},... | collective-permute-start | bytes 245768 | tf_op jit(solution)/shard_map/ppermute | solution.py:12
  322.1 10.5 %collective-permute-start.19 = (bf16[2,1,64,320]{3,2,1,0:T(8,128)(2,1)S(1)}, bf16[2,1,64,320]{3,2,1,0:T(8,128)(2,1)S(1)}, u32[]{:S(2)}, u32[]{:S(2)}) collective-permute-start(bf16[2,1,64,320]{3,2,1,0:T(8,128)(2,1)S(1)} %get-tuple-element.139), channel_id=1, source_target_pairs={{2,0},{4,2},{6,4},{3,1},{5,3},{7,5},{10,8},{12,10},{14,12},{11,9},... | collective-permute-start | bytes 245768 | tf_op jit(solution)/shard_map/ppermute | solution.py:15
  332.8 4.8 %collective-permute-start.20 = (bf16[2,6,1,320]{3,2,1,0:T(2,128)(2,1)S(1)}, bf16[2,6,1,320]{3,2,1,0:T(2,128)(2,1)S(1)}, u32[]{:S(2)}, u32[]{:S(2)}) collective-permute-start(bf16[2,6,1,320]{3,2,1,0:T(2,128)(2,1)S(1)} %get-tuple-element.132), channel_id=1, source_target_pairs={{0,1},{2,3},{4,5},{6,7},{8,9},{10,11},{12,13},{14,15},{16,17},{18,... | collective-permute-start | bytes 23048 | tf_op jit(solution)/shard_map/ppermute | solution.py:12
  336.1 5.7 %collective-permute-start.21 = (bf16[2,6,1,320]{3,2,1,0:T(2,128)(2,1)S(1)}, bf16[2,6,1,320]{3,2,1,0:T(2,128)(2,1)S(1)}, u32[]{:S(2)}, u32[]{:S(2)}) collective-permute-start(bf16[2,6,1,320]{3,2,1,0:T(2,128)(2,1)S(1)} %get-tuple-element.133), channel_id=1, source_target_pairs={{1,0},{3,2},{5,4},{7,6},{9,8},{11,10},{13,12},{15,14},{17,16},{19,... | collective-permute-start | bytes 23048 | tf_op jit(solution)/shard_map/ppermute | solution.py:15
  365.1 2.4 collective-permute-start.22
  (10 other events, 61.1 us)
Sparse Core Ops, SparseCore 0:
  8.9 50.7 all-gather.5
  61.2 47.8 all-gather.7
  110.7 84.4 all-gather.9
  196.6 112.8 all-gather.11
  311.0 47.2 all-gather.13
where the time goes:
time: 376 us; the launch traced here: 375 us
  waiting for transfers between devices  270 us (72%)
  starting transfers between devices  45.5 us (12%)
  matrix products  22.3 us (6%)
  between operations  13.6 us (4%)
  local copies, waits for them, and re-layouts  12.1 us (3%)
  other arithmetic  10.8 us (3%)
    all_gather x5, waiting for transfers between devices, convolve(): full_weight = lax.all_gather(weight, 'row', axis=2, tiled=True)  176 us
    ppermute x10, waiting for transfers between devices, with_halo(): lax.ppermute(lax.slice_in_dim(block, 0, width, axis=dim), axis, backward)  54.9 us
    ppermute x10, starting transfers between devices, with_halo(): lax.ppermute(lax.slice_in_dim(block, block.shape[dim] - width, None, axis...  28.3 us
    dot_general x36, matrix products, compute(): jnp.einsum('brck,kn->brcn', window, weights[tap], preferred_element_type=...  22.3 us
    ppermute x10, waiting for transfers between devices, with_halo(): lax.ppermute(lax.slice_in_dim(block, block.shape[dim] - width, None, axis...  19.1 us
    ppermute x3, waiting for transfers between devices, from_behind(): return lax.ppermute(value, axis, pairs)  17 us
    ppermute x10, starting transfers between devices, with_halo(): lax.ppermute(lax.slice_in_dim(block, 0, width, axis=dim), axis, backward)  13.1 us
    another operation x4, local copies, waits for them, and re-layouts  8.95 us
  transfers between devices with their start and end apart: 28, of which 27 were waited for; matrix products, arithmetic and copies ran while one was open for 10% of the time, Pallas kernels for 0%

commit v1 on v0

v1 whole, which is shorter than its diff:
```python
import functools

import jax
import jax.numpy as jnp
from jax import lax
from jax.experimental import pallas as pl
from jax.experimental.pallas import tpu as pltpu
from jax.sharding import PartitionSpec as P

BF = jnp.bfloat16
F32 = jnp.float32
LANES = 128
SIDE = 8
AXES = ("grp", "segment", "row", "col")
PIECES = 8
SHARDS = 4
VMEM = pl.BlockSpec(memory_space=pltpu.VMEM)
HBM = pl.BlockSpec(memory_space=pl.ANY)
SMEM = pl.BlockSpec(memory_space=pltpu.SMEM)


def params():
    return pltpu.CompilerParams(vmem_limit_bytes=52 * 1024 * 1024)


def plain_chunks(base):
    chunks = [[(tap, base + half * LANES, LANES)] for tap in range(9) for half in range(2)]
    rest = [(tap, base + 256, 64) for tap in range(9)]
    for at in range(0, 9, 2):
        chunks.append(rest[at : at + 2])
    return chunks


def joined_chunks():
    chunks = plain_chunks(0)
    for tap in range(9):
        for shard in range(4):
            chunks.append([(tap, 320 + shard * 160, LANES)])
        chunks.append([(tap, 320 + shard * 160 + LANES, 32) for shard in range(4)])
    return chunks


def padded_count(chunks):
    return -(-len(chunks) // PIECES) * PIECES


def pack_body(layouts, *refs):
    count = len(layouts)
    for chunks, source, target in zip(layouts, refs[:count], refs[count:]):
        channels = source.shape[2]
        for index in range(target.shape[0]):
            if index < len(chunks):
                parts = [source[tap, pl.ds(first, size), :] for tap, first, size in chunks[index]]
                have = sum(part.shape[0] for part in parts)
                if have < LANES:
                    parts.append(jnp.zeros((LANES - have, channels), BF))
                block = parts[0] if len(parts) == 1 else jnp.concatenate(parts, axis=0)
                target[index] = block.T
            else:
                target[index] = jnp.zeros((channels, LANES), BF)


def pack(layouts, weights):
    shapes = [
        jax.ShapeDtypeStruct((padded_count(chunks), weight.shape[2], LANES), BF)
        for chunks, weight in zip(layouts, weights)
    ]
    return pl.pallas_call(
        functools.partial(pack_body, layouts),
        out_shape=shapes,
        in_specs=[VMEM] * len(weights),
        out_specs=[VMEM] * len(weights),
        compiler_params=params(),
        name="pack_weights",
    )(*weights)


def device_pairs(mesh_shape, move):
    grps, segs, rows, cols = mesh_shape
    place = lambda g, s, r, c: ((g * segs + s) * rows + r) * cols + c
    return [
        (place(g, s, r, c), place(*move(g, s, r, c)))
        for g in range(grps)
        for s in range(segs)
        for r in range(rows)
        for c in range(cols)
    ]


def cyclic(count, by):
    return [(i, (i + by) % count) for i in range(count)]


def gather_planes(packed, piece, count):
    size = packed.shape[0] // PIECES
    mine = lax.dynamic_slice_in_dim(packed, piece * size, size, axis=0)
    return jnp.concatenate(
        [lax.ppermute(mine, "row", cyclic(count, by)) for by in range(1, count)], axis=0
    )


def gather_plane(block, mesh_shape):
    first = device_pairs(
        mesh_shape, lambda g, s, r, c: (g, s, r, 1 - c) if s == 0 else (1 - g, s, r, c)
    )
    second = device_pairs(
        mesh_shape, lambda g, s, r, c: (1 - g, s, r, c) if s == 0 else (g, s, r, 1 - c)
    )
    block = jnp.concatenate([block, lax.ppermute(block, AXES, first)], axis=0)
    block = jnp.concatenate([block, lax.ppermute(block, AXES, second)], axis=0)
    return block, lax.ppermute(block, "segment", [(0, 1), (1, 0)])


def load_weights(place, sources, target, sem):
    if len(sources) == 1:
        return [pltpu.make_async_copy(sources[0], target, sem)]
    own, near, far = sources
    grp, seg, row, col = (place[i] for i in range(4))
    size = own.shape[0] // PIECES
    copies = [pltpu.make_async_copy(own, target.at[:, row], sem)]
    for part, core in ((near, seg), (far, 1 - seg)):
        for slot in range(4):
            low, high = slot % 2, slot // 2
            flip_col = jnp.where(core == 0, low, high)
            flip_grp = jnp.where(core == 0, high, low)
            owner_grp = jnp.where(flip_grp == 1, 1 - grp, grp)
            owner_col = jnp.where(flip_col == 1, 1 - col, col)
            piece = (owner_grp * 2 + core) * 2 + owner_col
            for by in range(1, SHARDS):
                shard = lax.rem(row - by + SHARDS, SHARDS)
                source = part.at[pl.ds((slot * 3 + by - 1) * size, size)]
                copies.append(
                    pltpu.make_async_copy(source, target.at[pl.ds(piece * size, size), shard], sem)
                )
    return copies


def silu(value):
    return value / (1.0 + jnp.exp(-value))


def spread(value, shifted):
    cells = value.shape[0]
    shifted[0, :cells] = pltpu.roll(value, 1, 0).astype(BF)
    shifted[1, :cells] = value.astype(BF)
    shifted[2, :cells] = pltpu.roll(value, cells - 1, 0).astype(BF)


def weight_pair(weights, low, high):
    parts = []
    for index in (low, high):
        if index is not None:
            block = weights[index]
            parts.append(block.reshape(block.shape[0] * block.shape[1], LANES))
    return parts[0] if len(parts) == 1 else jnp.concatenate(parts, axis=1)


def product(left, right):
    return lax.dot_general(left, right, (((1,), (1,)), ((), ())), preferred_element_type=F32)


def add_plain(shifted, weights, rows, wide, acc, bias):
    cells = rows * wide

    def window(tap, first, size):
        at = (tap // 3) * wide
        return shifted[tap % 3, pl.ds(at, cells), pl.ds(first, size)]

    def rest(at):
        low = window(2 * at, 256, LANES)
        if at == 4:
            return low
        high = window(2 * at + 1, 256, LANES)
        lane = lax.broadcasted_iota(jnp.int32, (cells, LANES), 1)
        return jnp.where(lane < 64, low, high)

    acc[:cells] = product(window(0, 0, 256), weight_pair(weights, 0, 1)) + bias
    for tap in range(1, 9):
        acc[:cells] += product(window(tap, 0, 256), weight_pair(weights, 2 * tap, 2 * tap + 1))
    for at in range(0, 4, 2):
        left = jnp.concatenate([rest(at), rest(at + 1)], axis=1)
        acc[:cells] += product(left, weight_pair(weights, 18 + at, 19 + at))
    acc[:cells] += product(rest(4), weight_pair(weights, 22, None))


def inside(place, rows, wide, first_row, first_col, size):
    tile_rows, tile_cols, row_count, col_count = size
    row = lax.broadcasted_iota(jnp.int32, (rows, wide, 1), 0) + (place[2] * tile_rows + first_row)
    col = lax.broadcasted_iota(jnp.int32, (rows, wide, 1), 1) + (place[3] * tile_cols + first_col)
    return (row >= 0) & (row < tile_rows * row_count) & (col >= 0) & (col < tile_cols * col_count)


def activated(acc, rows, wide, keep):
    value = silu(acc[: rows * wide]).reshape(rows, wide, acc.shape[1])
    value = jnp.where(keep, value, 0.0).reshape(rows * wide, acc.shape[1])
    value = value.astype(BF).astype(F32)
    return jnp.concatenate([value, value[:, 256:320]], axis=1)


def encoder_body(size, sets, place, cells, bias1, bias2, *refs):
    tile_rows, tile_cols = size[:2]
    wide = tile_cols + 2 * SIDE
    sources1, refs = refs[:sets], refs[sets:]
    sources2, refs = refs[:sets], refs[sets:]
    skip, pooled, w1, w2, shifted, acc, sems = refs
    copies1 = load_weights(place, sources1, w1, sems.at[0])
    copies2 = load_weights(place, sources2, w2, sems.at[1])
    for copy in copies1 + copies2:
        copy.start()
    spread(cells[...].astype(F32), shifted)
    for copy in copies1:
        copy.wait()
    rows = tile_rows + 6
    add_plain(shifted, w1, rows, wide, acc, bias1[...])
    hidden = activated(acc, rows, wide, inside(place, rows, wide, -3, -SIDE, size))
    spread(hidden, shifted)
    for copy in copies2:
        copy.wait()
    rows = tile_rows + 4
    add_plain(shifted, w2, rows, wide, acc, bias2[...])
    value = activated(acc, rows, wide, inside(place, rows, wide, -2, -SIDE, size)).astype(BF)
    skip[...] = value
    half = pooled.shape[1]
    cell = lax.broadcasted_iota(jnp.int32, (half, 2 * wide), 1)
    cell = jnp.where(cell >= wide, cell - wide, cell)
    target = lax.broadcasted_iota(jnp.int32, (half, 2 * wide), 0)
    mean = jnp.where(cell // 2 == target, 0.25, 0.0).astype(BF)
    for row in range(tile_rows // 2):
        at = (2 + 2 * row) * wide
        block = value[at : at + 2 * wide]
        pooled[row] = jnp.dot(mean, block, preferred_element_type=F32).astype(BF)


def middle_body(size, place, own, *refs):
    tile_rows, tile_cols, row_count, col_count = size
    others, refs = refs[: row_count - 1], refs[row_count - 1 :]
    weights, bias = refs[:2]
    outs, refs = refs[2 : 2 + row_count], refs[2 + row_count :]
    field, shifted, acc, result = refs
    row = place[2]
    tall, half = tile_rows // 2, own.shape[1]
    rows = tall * row_count
    flat = (rows + 2) * half
    field[0] = jnp.zeros_like(field[0])
    field[rows + 1] = jnp.zeros_like(field[0])
    for by in range(row_count):
        source = own if by == 0 else others[by - 1]
        at = lax.rem(row - by + row_count, row_count)
        field[pl.ds(1 + tall * at, tall)] = source[...].astype(F32)
    spread(field[...].reshape(flat, field.shape[2]), shifted)
    cells = rows * half
    channels = weights.shape[2]
    acc[...] = jnp.zeros_like(acc)
    for tap in range(9):
        at = (tap // 3) * half
        left = shifted[tap % 3, pl.ds(at, cells), :]
        part = jnp.dot(left[:, :256], weights[tap, :256, :], preferred_element_type=F32)
        part += jnp.dot(left[:, 256:320], weights[tap, 256:320, :], preferred_element_type=F32)
        if tap == 0:
            part += bias[...]
        acc[:, :channels] += part
    col = lax.broadcasted_iota(jnp.int32, (rows, half, 1), 1)
    col = col + (place[3] * (tile_cols // 2) - SIDE // 2)
    keep = (col >= 0) & (col < tile_cols // 2 * col_count)
    value = silu(acc[...]).reshape(rows, half, 2 * LANES)
    value = jnp.where(keep, value, 0.0).reshape(cells, 2 * LANES)
    tail = pltpu.roll(value[:, LANES:], row * 32, 1)
    value = jnp.concatenate([value[:, :LANES], tail], axis=1).astype(BF)
    result[0] = jnp.zeros_like(result[0])
    result[rows + 1] = jnp.zeros_like(result[0])
    result[1 : rows + 1] = value.reshape(rows, half, 2 * LANES)
    for by in range(row_count):
        at = lax.rem(row + by, row_count)
        outs[by][...] = result[pl.ds(tall * at, tall + 2)]


def decoder_body(size, sets, place, skip, bias1, bias2, *refs):
    tile_rows, tile_cols = size[:2]
    wide = tile_cols + 2 * SIDE
    mids, refs = refs[:SHARDS], refs[SHARDS:]
    sources1, refs = refs[:sets], refs[sets:]
    sources2, refs = refs[:sets], refs[sets:]
    out, w1, w2, shifted, raised, field, acc, sems = refs
    copies1 = load_weights(place, sources1, w1, sems.at[0])
    copies2 = load_weights(place, sources2, w2, sems.at[1])
    for copy in copies1 + copies2:
        copy.start()
    spread(skip[...].astype(F32), shifted)
    half = mids[0].shape[1]
    tall = tile_rows // 2 + 2
    tail = mids[0][:, :, LANES:]
    for mid in mids[1:]:
        tail = tail + mid[:, :, LANES:]
    field[4] = tail
    for by in range(SHARDS):
        shard = lax.rem(place[2] - by + SHARDS, SHARDS) if sets == 3 else by
        field[shard] = mids[by][:, :, :LANES]
    cell = lax.broadcasted_iota(jnp.int32, (3 * wide, half), 0)
    move = jnp.where(cell >= 2 * wide, 1 - 2 * wide, jnp.where(cell >= wide, -wide, -1))
    source = lax.broadcasted_iota(jnp.int32, (3 * wide, half), 1)
    place_of = cell + move
    raise_by = jnp.where((place_of >= 2 * source) & (place_of < 2 * source + 2), 1.0, 0.0).astype(BF)
    for row in range(tall):
        block = jnp.concatenate([field[chunk, row] for chunk in range(5)], axis=1)
        up = jnp.dot(raise_by, block, preferred_element_type=F32).astype(BF)
        for dx in range(3):
            for twice in range(2):
                at = (2 * row + twice) * wide
                raised[dx, at : at + wide] = up[dx * wide : (dx + 1) * wide]
    for copy in copies1:
        copy.wait()
    rows = tile_rows + 2
    cells = rows * wide
    add_plain(shifted, w1, rows, wide, acc, bias1[...])

    def window(tap, first, count):
        return raised[tap % 3, pl.ds((tap // 3) * wide, cells), pl.ds(first, count)]

    for tap in range(9):
        at = 23 + 5 * tap
        for pair in range(2):
            left = window(tap, 256 * pair, 256)
            acc[:cells] += product(left, weight_pair(w1, at + 2 * pair, at + 2 * pair + 1))
        if tap % 2 == 1:
            left = jnp.concatenate([window(tap - 1, 512, LANES), window(tap, 512, LANES)], axis=1)
            acc[:cells] += product(left, weight_pair(w1, at - 1, at + 4))
        elif tap == 8:
            acc[:cells] += product(window(tap, 512, LANES), weight_pair(w1, at + 4, None))
    refined = activated(acc, rows, wide, inside(place, rows, wide, -1, -SIDE, size))
    spread(refined, shifted)
    for copy in copies2:
        copy.wait()
    add_plain(shifted, w2, tile_rows, wide, acc, bias2[...])
    value = silu(acc[: tile_rows * wide]).reshape(tile_rows, wide, acc.shape[1])
    out[0] = value[:, SIDE : SIDE + tile_cols, :].astype(BF)


def shards(mesh_shape, latent, enc_first, enc_first_bias, enc_second, enc_second_bias, mid_weight, mid_bias,
           dec_first, dec_first_bias, dec_second, dec_second_bias):
    grps, segs, row_count, col_count = mesh_shape
    grp, seg, row, col = (lax.axis_index(axis) for axis in AXES)
    place = jnp.stack([grp, seg, row, col]).astype(jnp.int32)
    piece = (grp * 2 + seg) * 2 + col
    tile_rows, tile_cols, channels = latent.shape[1:]
    size = (tile_rows, tile_cols, row_count, col_count)
    wide = tile_cols + 2 * SIDE
    half = -(-(wide // 2) // 16) * 16
    spread_out = row_count == SHARDS and col_count == 2 and grps == 2 and segs == 2
    plain, joined = plain_chunks(0), joined_chunks()

    if spread_out:
        (own1,) = pack((plain,), (enc_first,))
        (own2,) = pack((plain,), (enc_second,))
        own3, own4 = pack((joined, plain), (dec_first, dec_second))
        sets = 3
        weights = []
        for own in (own1, own2, own3, own4):
            block = gather_planes(own, piece, row_count)
            weights.append((own,) + gather_plane(block, mesh_shape))
    else:
        sets = 1
        weights = []
        for chunks, weight in ((plain, enc_first), (plain, enc_second), (joined, dec_first), (plain, dec_second)):
            full = lax.all_gather(weight, "row", axis=2, tiled=True)
            (own,) = pack((chunks,), (full,))
            weights.append((own.reshape(own.shape[0], SHARDS, -1, LANES),))

    tile = lax.dynamic_index_in_dim(latent, seg, 0, keepdims=False)
    down = [(i, i + 1) for i in range(row_count - 1)]
    above = lax.ppermute(tile, "row", down)
    below = lax.ppermute(tile, "row", [(b, a) for a, b in down])
    tile = jnp.concatenate([above, tile, below], axis=0)
    left_edge, right_edge = tile[:, :SIDE], tile[:, tile_cols - SIDE :]
    if col_count == 2:
        edge = lax.ppermute(jnp.where(col == 0, right_edge, left_edge), "col", [(0, 1), (1, 0)])
        blank = jnp.zeros_like(edge)
        left, right = jnp.where(col == 0, blank, edge), jnp.where(col == 0, edge, blank)
    else:
        along = [(i, i + 1) for i in range(col_count - 1)]
        left = lax.ppermute(right_edge, "col", along)
        right = lax.ppermute(left_edge, "col", [(b, a) for a, b in along])
    tile = jnp.concatenate([left, tile, right], axis=1)
    cells = jnp.concatenate([tile, tile[:, :, 256:]], axis=2).reshape(-1, 3 * LANES)

    scratch = lambda *shape: pltpu.VMEM(shape, BF)
    lines = lambda bias: bias.reshape(1, -1)
    skip, pooled = pl.pallas_call(
        functools.partial(encoder_body, size, sets),
        out_shape=[
            jax.ShapeDtypeStruct(((tile_rows + 4) * wide, 3 * LANES), BF),
            jax.ShapeDtypeStruct((tile_rows // 2, half, 3 * LANES), BF),
        ],
        in_specs=[SMEM, VMEM, VMEM, VMEM] + [HBM] * (2 * sets),
        out_specs=[VMEM, VMEM],
        scratch_shapes=[
            scratch(24, SHARDS, channels // SHARDS, LANES),
            scratch(24, SHARDS, channels // SHARDS, LANES),
            scratch(3, 3 * tile_rows * wide, 3 * LANES),
            pltpu.VMEM(((tile_rows + 6) * wide, channels), F32),
            pltpu.SemaphoreType.DMA((2,)),
        ],
        compiler_params=params(),
        name="encoder",
    )(place, cells, lines(enc_first_bias), lines(enc_second_bias), *weights[0], *weights[1])

    tall = tile_rows // 2
    if spread_out:
        others = [lax.ppermute(pooled, "row", cyclic(row_count, by)) for by in range(1, row_count)]
        part = mid_weight.shape[2]
        bias = lax.dynamic_slice_in_dim(mid_bias, row * part, part, 0)
        rows = tall * row_count
        sent = pl.pallas_call(
            functools.partial(middle_body, size),
            out_shape=[jax.ShapeDtypeStruct((tall + 2, half, 2 * LANES), BF)] * row_count,
            in_specs=[SMEM] + [VMEM] * (row_count + 2),
            out_specs=[VMEM] * row_count,
            scratch_shapes=[
                pltpu.VMEM((rows + 2, half, 3 * LANES), F32),
                scratch(3, (rows + 2) * half, 3 * LANES),
                pltpu.VMEM((rows * half, 2 * LANES), F32),
                scratch(rows + 2, half, 2 * LANES),
            ],
            compiler_params=params(),
            name="middle",
        )(place, pooled, *others, mid_weight, lines(bias))
        mids = [sent[0]] + [
            lax.ppermute(sent[by], "row", cyclic(row_count, by)) for by in range(1, row_count)
        ]
    else:
        full = lax.all_gather(mid_weight, "row", axis=2, tiled=True)
        field = jnp.concatenate(
            [lax.ppermute(pooled, "row", down), pooled, lax.ppermute(pooled, "row", [(b, a) for a, b in down])]
        )[:, :, :channels]
        field = jnp.pad(field, ((0, 0), (1, 1), (0, 0)))
        total = jnp.zeros((tall + 2, half, full.shape[2]), F32)
        first = field.shape[0] // 2 - tall // 2 - 2
        for tap in range(9):
            dy, dx = tap // 3, tap % 3
            window = field[first + dy : first + dy + tall + 2, dx : dx + half]
            total += jnp.einsum("rck,kn->rcn", window, full[tap], preferred_element_type=F32)
        at_row = jnp.arange(tall + 2)[:, None, None] - 1 + row * tall
        at_col = jnp.arange(half)[None, :, None] - SIDE // 2 + col * (tile_cols // 2)
        keep = (at_row >= 0) & (at_row < tall * row_count) & (at_col >= 0) & (at_col < tile_cols // 2 * col_count)
        middle = jnp.where(keep, jax.nn.silu(total + mid_bias), 0.0).astype(BF)
        mids = []
        for shard in range(SHARDS):
            block = middle[:, :, 160 * shard : 160 * (shard + 1)]
            tail = jnp.pad(block[:, :, LANES:], ((0, 0), (0, 0), (32 * shard, 96 - 32 * shard)))
            mids.append(jnp.concatenate([block[:, :, :LANES], tail], axis=2))

    return pl.pallas_call(
        functools.partial(decoder_body, size, sets),
        out_shape=jax.ShapeDtypeStruct((1, tile_rows, tile_cols, channels), BF),
        in_specs=[SMEM, VMEM, VMEM, VMEM] + [VMEM] * SHARDS + [HBM] * (2 * sets),
        out_specs=VMEM,
        scratch_shapes=[
            scratch(padded_count(joined), SHARDS, channels // SHARDS, LANES),
            scratch(24, SHARDS, channels // SHARDS, LANES),
            scratch(3, (tile_rows + 4) * wide, 3 * LANES),
            scratch(3, (tile_rows + 4) * wide, 5 * LANES),
            scratch(5, tall + 2, half, LANES),
            pltpu.VMEM(((tile_rows + 2) * wide, channels), F32),
            pltpu.SemaphoreType.DMA((2,)),
        ],
        compiler_params=params(),
        name="decoder",
    )(place, skip, lines(dec_first_bias), lines(dec_second_bias), *mids, *weights[2], *weights[3])


def solution(mesh):
    placed = (
        P("grp", "row", "col", None),
        P(None, None, "row"),
        P(),
        P(None, None, "row"),
        P(),
        P(None, None, "row"),
        P(),
        P(None, None, "row"),
        P(),
        P(None, None, "row"),
        P(),
    )
    mesh_shape = tuple(mesh.shape[axis] for axis in AXES)
    return jax.shard_map(
        functools.partial(shards, mesh_shape),
        mesh=mesh,
        in_specs=placed,
        out_specs=P(("grp", "segment"), "row", "col", None),
        check_vma=False,
    )
```

time: 376 us -> 130 us (0.35)
  waiting for transfers between devices: 270 us -> 30.6 us
  Pallas kernels: 0 us -> 25.1 us
  matrix products: 22.3 us -> 0 us
  between operations: 13.6 us -> 0.45 us
  local copies, waits for them, and re-layouts: 12.1 us -> 19.9 us
  other arithmetic: 10.8 us -> 3.57 us
  starting transfers between devices: 45.5 us -> 49.4 us
    all_gather x5 -> x0, waiting for transfers between devices: 176 us -> none  [convolve(): full_weight = lax.all_gather(weight, 'row', axis=2, tiled=True)]
    ppermute x23 -> x33, waiting for transfers between devices: 91 us -> 30.6 us  [the longest x12 13.5 us: gather_planes(): lax.ppermute(mine, 'row', cyclic(count, by))]
    pallas_call x0 -> x6, Pallas kernels: none -> 25.1 us  [the longest x1 10 us: shards(): pl.pallas_call(functools.partial(decoder_body, size, sets), out_shape=jax...]
    dot_general x36 -> x0, matrix products: 22.3 us -> none  [compute(): jnp.einsum('brck,kn->brcn', window, weights[tap], preferred_element_type=...]
    unnamed x20 -> x43, local copies, waits for them, and re-layouts: 0.13 us -> 16.1 us
    another operation x4 -> x0, local copies, waits for them, and re-layouts: 8.95 us -> none
    concatenate x10 -> x9, other arithmetic: 9.46 us -> 2.65 us  [the longest x1 2.28 us: shards(): jnp.concatenate([tile, tile[:, :, 256:]], axis=2).reshape(-1, 3 * LANES)]
    ppermute x23 -> x33, starting transfers between devices: 45.3 us -> 49.4 us  [the longest x12 18.9 us: gather_planes(): lax.ppermute(mine, 'row', cyclic(count, by))]
  transfers between devices with their start and end apart: 28 -> 33, of which waited for: 27 -> 18; matrix products, arithmetic and copies ran while one was open for 10% -> 13% of each run, Pallas kernels for 0% -> 9%
where the time goes in v1:
time: 130 us; the launch traced here: 129 us
  starting transfers between devices  49.4 us (38%)
  waiting for transfers between devices  30.6 us (24%)
  Pallas kernels  25.1 us (19%)
  local copies, waits for them, and re-layouts  19.9 us (15%)
  other arithmetic  3.57 us (3%)
    ppermute x12, starting transfers between devices, gather_planes(): lax.ppermute(mine, 'row', cyclic(count, by))  18.9 us
    unnamed x43, local copies, waits for them, and re-layouts  16.1 us
    ppermute x12, waiting for transfers between devices, gather_planes(): lax.ppermute(mine, 'row', cyclic(count, by))  13.5 us
    pallas_call x1, Pallas kernels, shards(): pl.pallas_call(functools.partial(decoder_body, size, sets), out_shape=jax...  10 us
    pallas_call x1, Pallas kernels, shards(): pl.pallas_call(functools.partial(encoder_body, size, sets), out_shape=[ja...  8.37 us
    ppermute x4, waiting for transfers between devices, gather_plane(): block = jnp.concatenate([block, lax.ppermute(block, AXES, second)], axis=0)  7.91 us
    ppermute x4, starting transfers between devices, gather_plane(): block = jnp.concatenate([block, lax.ppermute(block, AXES, first)], axis=0)  7.09 us
    ppermute x4, starting transfers between devices, gather_plane(): block = jnp.concatenate([block, lax.ppermute(block, AXES, second)], axis=0)  6.35 us
  transfers between devices with their start and end apart: 33, of which 18 were waited for; matrix products, arithmetic and copies ran while one was open for 13% of the time, Pallas kernels for 9%

profile of v1, /device:TPU:0, one launch (start us, length us, event | category | flops | bytes accessed | tf_op | source)
XLA Modules:
  0.0 129.0 jit_solution(12533646065709203241)
XLA Ops:
  0.0 3.9 %copy.15.refs_0_ = bf16[9,960,80]{2,1,0:T(8,128)(2,1)} copy(bf16[9,960,80]{1,2,0:T(8,128)(2,1)} %param.18) | data formatting | bytes 2764800 | tf_op args[7]
  4.3 3.4 %pack_weights.5 = (bf16[72,80,128]{2,1,0:T(8,128)(2,1)}, bf16[24,80,128]{2,1,0:T(8,128)(2,1)S(1)}) custom-call(bf16[9,960,80]{2,1,0:T(8,128)(2,1)} %copy.15.refs_0_, bf16[9,320,80]{2,1,0:T(8,128)(2,1)S(1)} %copy.16.refs_1_), custom_call_target="tpu_custom_call" | custom-call | tf_op jit(solution)/shard_map/pack_weights/pallas_call | solution.py:68
  8.7 3.1 %collective-permute-start.21 = (bf16[9,80,128]{2,1,0:T(8,128)(2,1)S(1)}, bf16[9,80,128]{2,1,0:T(8,128)(2,1)S(1)}, u32[]{:S(2)}, u32[]{:S(2)}) collective-permute-start(bf16[9,80,128]{2,1,0:T(8,128)(2,1)S(1)} %constant_dynamic-slice_fusion.1), channel_id=1, source_target_pairs={{0,2},{2,4},{4,6},{6,0},{1,3},{3,5},{5,7},{7,1},{8,10},{10,12},{12... | collective-permute-start | bytes 552968 | tf_op jit(solution)/shard_map/ppermute | solution.py:98
  11.8 2.6 %collective-permute-start.22 = (bf16[9,80,128]{2,1,0:T(8,128)(2,1)S(1)}, bf16[9,80,128]{2,1,0:T(8,128)(2,1)S(1)}, u32[]{:S(2)}, u32[]{:S(2)}) collective-permute-start(bf16[9,80,128]{2,1,0:T(8,128)(2,1)S(1)} %constant_dynamic-slice_fusion.1), channel_id=1, source_target_pairs={{0,4},{2,6},{4,0},{6,2},{1,5},{3,7},{5,1},{7,3},{8,12},{10,14},{12... | collective-permute-start | bytes 552968 | tf_op jit(solution)/shard_map/ppermute | solution.py:98
  17.0 5.2 %collective-permute-start = (bf16[4,64,320]{2,1,0:T(8,128)(2,1)S(1)}, bf16[4,64,320]{2,1,0:T(8,128)(2,1)}, u32[]{:S(2)}, u32[]{:S(2)}) collective-permute-start(bf16[4,64,320]{2,1,0:T(8,128)(2,1)S(1)} %dynamic-slice_bitcast_fusion), channel_id=1, source_target_pairs={{0,2},{2,4},{4,6},{1,3},{3,5},{5,7},{8,10},{10,12},{12,14},{9,11},... | collective-permute-start | bytes 491528 | tf_op jit(solution)/shard_map/ppermute | solution.py:370
  26.5 1.8 %collective-permute-start.4 = (bf16[3,80,128]{2,1,0:T(8,128)(2,1)S(1)}, bf16[3,80,128]{2,1,0:T(8,128)(2,1)S(1)}, u32[]{:S(2)}, u32[]{:S(2)}) collective-permute-start(bf16[3,80,128]{2,1,0:T(8,128)(2,1)S(1)} %constant_dynamic-slice_fusion.3), channel_id=1, source_target_pairs={{0,4},{2,6},{4,0},{6,2},{1,5},{3,7},{5,1},{7,3},{8,12},{10,14},{12... | collective-permute-start | bytes 184328 | tf_op jit(solution)/shard_map/ppermute | solution.py:98
  29.9 2.2 %collective-permute-done.3 = bf16[3,80,128]{2,1,0:T(8,128)(2,1)S(1)} collective-permute-done((bf16[3,80,128]{2,1,0:T(8,128)(2,1)S(1)}, bf16[3,80,128]{2,1,0:T(8,128)(2,1)S(1)}, u32[]{:S(2)}, u32[]{:S(2)}) %collective-permute-start.3) | collective-permute-done | bytes 61472 | tf_op jit(solution)/shard_map/ppermute | solution.py:98
  32.1 3.9 %collective-permute-start.5 = (bf16[3,80,128]{2,1,0:T(8,128)(2,1)S(1)}, bf16[3,80,128]{2,1,0:T(8,128)(2,1)S(1)}, u32[]{:S(2)}, u32[]{:S(2)}) collective-permute-start(bf16[3,80,128]{2,1,0:T(8,128)(2,1)S(1)} %constant_dynamic-slice_fusion.3), channel_id=1, source_target_pairs={{0,6},{2,0},{4,2},{6,4},{1,7},{3,1},{5,3},{7,5},{8,14},{10,8},{12,... | collective-permute-start | bytes 184328 | tf_op jit(solution)/shard_map/ppermute | solution.py:98
  36.0 2.6 %collective-permute-done.4 = bf16[3,80,128]{2,1,0:T(8,128)(2,1)S(1)} collective-permute-done((bf16[3,80,128]{2,1,0:T(8,128)(2,1)S(1)}, bf16[3,80,128]{2,1,0:T(8,128)(2,1)S(1)}, u32[]{:S(2)}, u32[]{:S(2)}) %collective-permute-start.4) | collective-permute-done | bytes 61472 | tf_op jit(solution)/shard_map/ppermute | solution.py:98
  39.1 3.6 %collective-permute-start.10 = (bf16[3,80,128]{2,1,0:T(8,128)(2,1)S(1)}, bf16[3,80,128]{2,1,0:T(8,128)(2,1)S(1)}, u32[]{:S(2)}, u32[]{:S(2)}) collective-permute-start(bf16[3,80,128]{2,1,0:T(8,128)(2,1)S(1)} %constant_dynamic-slice_fusion.2), channel_id=1, source_target_pairs={{0,4},{2,6},{4,0},{6,2},{1,5},{3,7},{5,1},{7,3},{8,12},{10,14},{12... | collective-permute-start | bytes 184328 | tf_op jit(solution)/shard_map/ppermute | solution.py:98
  42.9 1.6 %collective-permute-start.25 = (bf16[54,80,128]{2,1,0:T(8,128)(2,1)S(1)}, bf16[54,80,128]{2,1,0:T(8,128)(2,1)S(1)}, u32[]{:S(2)}, u32[]{:S(2)}) collective-permute-start(bf16[54,80,128]{2,1,0:T(8,128)(2,1)S(1)} %pad_maximum_fusion), channel_id=1, source_target_pairs={{0,16},{1,17},{2,18},{3,19},{4,20},{5,21},{6,22},{7,23},{8,9},{9,8... | collective-permute-start | bytes 3317768 | tf_op jit(solution)/shard_map/ppermute | solution.py:110
  47.1 2.4 %collective-permute-done.11 = bf16[3,80,128]{2,1,0:T(8,128)(2,1)S(1)} collective-permute-done((bf16[3,80,128]{2,1,0:T(8,128)(2,1)S(1)}, bf16[3,80,128]{2,1,0:T(8,128)(2,1)S(1)}, u32[]{:S(2)}, u32[]{:S(2)}) %collective-permute-start.11) | collective-permute-done | bytes 61472 | tf_op jit(solution)/shard_map/ppermute | solution.py:98
  49.5 2.6 %collective-permute-done.27 = bf16[3,80,128]{2,1,0:T(8,128)(2,1)S(1)} collective-permute-done((bf16[3,80,128]{2,1,0:T(8,128)(2,1)S(1)}, bf16[3,80,128]{2,1,0:T(8,128)(2,1)S(1)}, u32[]{:S(2)}, u32[]{:S(2)}) %collective-permute-start.27) | collective-permute-done | bytes 61472 | tf_op jit(solution)/shard_map/ppermute | solution.py:98
  53.4 1.9 %collective-permute-done.28 = bf16[3,80,128]{2,1,0:T(8,128)(2,1)S(1)} collective-permute-done((bf16[3,80,128]{2,1,0:T(8,128)(2,1)S(1)}, bf16[3,80,128]{2,1,0:T(8,128)(2,1)S(1)}, u32[]{:S(2)}, u32[]{:S(2)}) %collective-permute-start.28) | collective-permute-done | bytes 61472 | tf_op jit(solution)/shard_map/ppermute | solution.py:98
  55.3 1.6 %collective-permute-start.6 = (bf16[9,80,128]{2,1,0:T(8,128)(2,1)S(1)}, bf16[9,80,128]{2,1,0:T(8,128)(2,1)S(1)}, u32[]{:S(2)}, u32[]{:S(2)}) collective-permute-start(bf16[9,80,128]{2,1,0:T(8,128)(2,1)S(1)} %pad_maximum_fusion.5), channel_id=1, source_target_pairs={{0,1},{1,0},{2,3},{3,2},{4,5},{5,4},{6,7},{7,6},{8,24},{9,25},{10,... | collective-permute-start | bytes 552968 | tf_op jit(solution)/shard_map/ppermute | solution.py:109
  56.8 2.1 %collective-permute-start.12 = (bf16[9,80,128]{2,1,0:T(8,128)(2,1)S(1)}, bf16[9,80,128]{2,1,0:T(8,128)(2,1)S(1)}, u32[]{:S(2)}, u32[]{:S(2)}) collective-permute-start(bf16[9,80,128]{2,1,0:T(8,128)(2,1)S(1)} %pad_maximum_fusion.6), channel_id=1, source_target_pairs={{0,1},{1,0},{2,3},{3,2},{4,5},{5,4},{6,7},{7,6},{8,24},{9,25},{10,... | collective-permute-start | bytes 552968 | tf_op jit(solution)/shard_map/ppermute | solution.py:109
  64.3 1.9 %collective-permute-start.30 = (bf16[9,80,128]{2,1,0:T(8,128)(2,1)S(1)}, bf16[9,80,128]{2,1,0:T(8,128)(2,1)S(1)}, u32[]{:S(2)}, u32[]{:S(2)}) collective-permute-start(bf16[9,80,128]{2,1,0:T(8,128)(2,1)S(1)} %pad_maximum_fusion.7), channel_id=1, source_target_pairs={{0,1},{1,0},{2,3},{3,2},{4,5},{5,4},{6,7},{7,6},{8,24},{9,25},{10,... | collective-permute-start | bytes 552968 | tf_op jit(solution)/shard_map/ppermute | solution.py:109
  67.3 1.6 %collective-permute-start.7 = (bf16[18,80,128]{2,1,0:T(8,128)(2,1)S(1)}, bf16[18,80,128]{2,1,0:T(8,128)(2,1)S(1)}, u32[]{:S(2)}, u32[]{:S(2)}) collective-permute-start(bf16[18,80,128]{2,1,0:T(8,128)(2,1)S(1)} %pad_maximum_fusion.2), channel_id=1, source_target_pairs={{0,16},{1,17},{2,18},{3,19},{4,20},{5,21},{6,22},{7,23},{8,9},{9,8... | collective-permute-start | bytes 1105928 | tf_op jit(solution)/shard_map/ppermute | solution.py:110
  70.0 2.6 %collective-permute-start.31 = (bf16[18,80,128]{2,1,0:T(8,128)(2,1)S(1)}, bf16[18,80,128]{2,1,0:T(8,128)(2,1)S(1)}, u32[]{:S(2)}, u32[]{:S(2)}) collective-permute-start(bf16[18,80,128]{2,1,0:T(8,128)(2,1)S(1)} %pad_maximum_fusion.4), channel_id=1, source_target_pairs={{0,16},{1,17},{2,18},{3,19},{4,20},{5,21},{6,22},{7,23},{8,9},{9,8... | collective-permute-start | bytes 1105928 | tf_op jit(solution)/shard_map/ppermute | solution.py:110
  72.7 2.2 %collective-permute-done.7 = bf16[18,80,128]{2,1,0:T(8,128)(2,1)S(1)} collective-permute-done((bf16[18,80,128]{2,1,0:T(8,128)(2,1)S(1)}, bf16[18,80,128]{2,1,0:T(8,128)(2,1)S(1)}, u32[]{:S(2)}, u32[]{:S(2)}) %collective-permute-start.7) | collective-permute-done | bytes 368672 | tf_op jit(solution)/shard_map/ppermute | solution.py:110
  75.6 3.2 %collective-permute-done.13 = bf16[18,80,128]{2,1,0:T(8,128)(2,1)S(1)} collective-permute-done((bf16[18,80,128]{2,1,0:T(8,128)(2,1)S(1)}, bf16[18,80,128]{2,1,0:T(8,128)(2,1)S(1)}, u32[]{:S(2)}, u32[]{:S(2)}) %collective-permute-start.13) | collective-permute-done | bytes 368672 | tf_op jit(solution)/shard_map/ppermute | solution.py:110
  80.3 2.5 %collective-permute-done.31 = bf16[18,80,128]{2,1,0:T(8,128)(2,1)S(1)} collective-permute-done((bf16[18,80,128]{2,1,0:T(8,128)(2,1)S(1)}, bf16[18,80,128]{2,1,0:T(8,128)(2,1)S(1)}, u32[]{:S(2)}, u32[]{:S(2)}) %collective-permute-start.31) | collective-permute-done | bytes 368672 | tf_op jit(solution)/shard_map/ppermute | solution.py:110
  84.0 2.3 %fusion.7 = bf16[12,80,384]{2,1,0:T(8,128)(2,1)} fusion(bf16[12,8,320]{2,1,0:T(8,128)(2,1)S(1)} %get-tuple-element.22, bf16[12,8,320]{2,1,0:T(8,128)(2,1)S(1)} %get-tuple-element.21, bf16[4,64,320]{2,1,0:T(8,128)(2,1)} %collective-permute-done.1, bf16[4,64,320]{2,1,0:T(8,128)(2,1)S(1)} %dynamic-slice_bitcast_fusion, bf16[4,64,320]{2,1,0:T(8,128)(2,1)} %collective-permute-done), kind=kLoop, calls=%fused_computation.9 | loop fusion | flops 9584640 | bytes 1351680 | tf_op jit(solution)/shard_map/concatenate | solution.py:383
  87.4 8.4 %encoder.1 = (bf16[640,384]{1,0:T(8,128)(2,1)S(1)}, bf16[2,48,384]{2,1,0:T(8,128)(2,1)S(1)}) custom-call(s32[4]{0:T(128)S(1)} %pad_add_fusion.place, bf16[960,384]{1,0:T(8,128)(2,1)} %bitcast.9, f32[1,320]{1,0:T(1,128)S(1)} %reshape.19.bias1, f32[1,320]{1,0:T(1,128)S(1)} %reshape.20.bias2, bf16[24,80,128]{2,1,0:T(8,128)(2,1)S(1)} %pack_weights.3.refs_0_, ...), custom_call_target="tpu_custom_call" | custom-call | tf_op jit(solution)/shard_map/encoder/pallas_call | solution.py:387
  98.1 1.7 %collective-permute-start.17 = (bf16[2,48,384]{2,1,0:T(8,128)(2,1)S(1)}, bf16[2,48,384]{2,1,0:T(8,128)(2,1)S(1)}, u32[]{:S(2)}, u32[]{:S(2)}) collective-permute-start(bf16[2,48,384]{2,1,0:T(8,128)(2,1)S(1)} %get-tuple-element.14.own), channel_id=1, source_target_pairs={{0,6},{2,0},{4,2},{6,4},{1,7},{3,1},{5,3},{7,5},{8,14},{10,8},{12,... | collective-permute-start | bytes 221192 | tf_op jit(solution)/shard_map/ppermute | solution.py:408
  99.8 2.2 %copy.14.refs_3_ = bf16[9,320,160]{2,1,0:T(8,128)(2,1)} copy(bf16[9,320,160]{1,2,0:T(8,128)(2,1)S(1)} %copy-done.1) | data formatting | bytes 1843200 | tf_op args[5]
  102.9 2.4 %collective-permute-done.16.refs_1_ = bf16[2,48,384]{2,1,0:T(8,128)(2,1)S(1)} collective-permute-done((bf16[2,48,384]{2,1,0:T(8,128)(2,1)S(1)}, bf16[2,48,384]{2,1,0:T(8,128)(2,1)S(1)}, u32[]{:S(2)}, u32[]{:S(2)}) %collective-permute-start.16) | collective-permute-done | bytes 73760 | tf_op jit(solution)/shard_map/ppermute | solution.py:408
  105.2 2.8 %middle.1 = (bf16[4,48,256]{2,1,0:T(8,128)(2,1)S(1)}, bf16[4,48,256]{2,1,0:T(8,128)(2,1)S(1)}, bf16[4,48,256]{2,1,0:T(8,128)(2,1)S(1)}, bf16[4,48,256]{2,1,0:T(8,128)(2,1)S(1)}) custom-call(s32[4]{0:T(128)S(1)} %pad_add_fusion.place, bf16[2,48,384]{2,1,0:T(8,128)(2,1)S(1)} %get-tuple-element.14.own, bf16[2,48,384]{2,1,0:T(8,128)(2,1)S(1)} %collective-permute-done.15.refs_0_, ...), custom_call_target="tpu_custom_call" | custom-call | tf_op jit(solution)/shard_map/middle/pallas_call | solution.py:412
  108.0 2.1 %collective-permute-start.18 = (bf16[4,48,256]{2,1,0:T(8,128)(2,1)S(1)}, bf16[4,48,256]{2,1,0:T(8,128)(2,1)S(1)}, u32[]{:S(2)}, u32[]{:S(2)}) collective-permute-start(bf16[4,48,256]{2,1,0:T(8,128)(2,1)S(1)} %get-tuple-element.16), channel_id=1, source_target_pairs={{0,2},{2,4},{4,6},{6,0},{1,3},{3,5},{5,7},{7,1},{8,10},{10,12},{12... | collective-permute-start | bytes 294920 | tf_op jit(solution)/shard_map/ppermute | solution.py:427
  112.6 3.1 %collective-permute-done.18.refs_1_ = bf16[4,48,256]{2,1,0:T(8,128)(2,1)S(1)} collective-permute-done((bf16[4,48,256]{2,1,0:T(8,128)(2,1)S(1)}, bf16[4,48,256]{2,1,0:T(8,128)(2,1)S(1)}, u32[]{:S(2)}, u32[]{:S(2)}) %collective-permute-start.18) | collective-permute-done | bytes 98336 | tf_op jit(solution)/shard_map/ppermute | solution.py:427
  115.6 3.2 %collective-permute-done.19.refs_2_ = bf16[4,48,256]{2,1,0:T(8,128)(2,1)S(1)} collective-permute-done((bf16[4,48,256]{2,1,0:T(8,128)(2,1)S(1)}, bf16[4,48,256]{2,1,0:T(8,128)(2,1)S(1)}, u32[]{:S(2)}, u32[]{:S(2)}) %collective-permute-start.19) | collective-permute-done | bytes 98336 | tf_op jit(solution)/shard_map/ppermute | solution.py:427
  118.8 10.0 %decoder.1 = bf16[1,4,64,320]{3,2,1,0:T(8,128)(2,1)} custom-call(s32[4]{0:T(128)S(1)} %pad_add_fusion.place, bf16[640,384]{1,0:T(8,128)(2,1)S(1)} %get-tuple-element.13.skip, f32[1,320]{1,0:T(1,128)S(1)} %reshape.21.bias1, f32[1,320]{1,0:T(1,128)S(1)} %reshape.22.bias2, bf16[4,48,256]{2,1,0:T(8,128)(2,1)S(1)} %get-tuple-element.15.refs_0_, ...), custom_call_target="tpu_custom_call" | custom-call | tf_op jit(solution)/shard_map/decoder/pallas_call | solution.py:451
  (109 shorter events, 32.3 us)
Async XLA Ops:
  8.7 17.0 %collective-permute-start.21 = (bf16[9,80,128]{2,1,0:T(8,128)(2,1)S(1)}, bf16[9,80,128]{2,1,0:T(8,128)(2,1)S(1)}, u32[]{:S(2)}, u32[]{:S(2)}) collective-permute-start(bf16[9,80,128]{2,1,0:T(8,128)(2,1)S(1)} %constant_dynamic-slice_fusion.1), channel_id=1, source_target_pairs={{0,2},{2,4},{4,6},{6,0},{1,3},{3,5},{5,7},{7,1},{8,10},{10,12},{12... | collective-permute-start | bytes 552968 | tf_op jit(solution)/shard_map/ppermute | solution.py:98
  11.8 14.7 %collective-permute-start.22 = (bf16[9,80,128]{2,1,0:T(8,128)(2,1)S(1)}, bf16[9,80,128]{2,1,0:T(8,128)(2,1)S(1)}, u32[]{:S(2)}, u32[]{:S(2)}) collective-permute-start(bf16[9,80,128]{2,1,0:T(8,128)(2,1)S(1)} %constant_dynamic-slice_fusion.1), channel_id=1, source_target_pairs={{0,4},{2,6},{4,0},{6,2},{1,5},{3,7},{5,1},{7,3},{8,12},{10,14},{12... | collective-permute-start | bytes 552968 | tf_op jit(solution)/shard_map/ppermute | solution.py:98
  14.4 13.9 %collective-permute-start.23 = (bf16[9,80,128]{2,1,0:T(8,128)(2,1)S(1)}, bf16[9,80,128]{2,1,0:T(8,128)(2,1)S(1)}, u32[]{:S(2)}, u32[]{:S(2)}) collective-permute-start(bf16[9,80,128]{2,1,0:T(8,128)(2,1)S(1)} %constant_dynamic-slice_fusion.1), channel_id=1, source_target_pairs={{0,6},{2,0},{4,2},{6,4},{1,7},{3,1},{5,3},{7,5},{8,14},{10,8},{12,... | collective-permute-start | bytes 552968 | tf_op jit(solution)/shard_map/ppermute | solution.py:98
  15.7 48.6 %collective-permute-start.1 = (bf16[4,64,320]{2,1,0:T(8,128)(2,1)S(1)}, bf16[4,64,320]{2,1,0:T(8,128)(2,1)}, u32[]{:S(2)}, u32[]{:S(2)}) collective-permute-start(bf16[4,64,320]{2,1,0:T(8,128)(2,1)S(1)} %dynamic-slice_bitcast_fusion), channel_id=1, source_target_pairs={{2,0},{4,2},{6,4},{3,1},{5,3},{7,5},{10,8},{12,10},{14,12},{11,9},... | collective-permute-start | bytes 491528 | tf_op jit(solution)/shard_map/ppermute | solution.py:371
  17.0 49.2 %collective-permute-start = (bf16[4,64,320]{2,1,0:T(8,128)(2,1)S(1)}, bf16[4,64,320]{2,1,0:T(8,128)(2,1)}, u32[]{:S(2)}, u32[]{:S(2)}) collective-permute-start(bf16[4,64,320]{2,1,0:T(8,128)(2,1)S(1)} %dynamic-slice_bitcast_fusion), channel_id=1, source_target_pairs={{0,2},{2,4},{4,6},{1,3},{3,5},{5,7},{8,10},{10,12},{12,14},{9,11},... | collective-permute-start | bytes 491528 | tf_op jit(solution)/shard_map/ppermute | solution.py:370
  25.7 6.4 %collective-permute-start.3 = (bf16[3,80,128]{2,1,0:T(8,128)(2,1)S(1)}, bf16[3,80,128]{2,1,0:T(8,128)(2,1)S(1)}, u32[]{:S(2)}, u32[]{:S(2)}) collective-permute-start(bf16[3,80,128]{2,1,0:T(8,128)(2,1)S(1)} %constant_dynamic-slice_fusion.3), channel_id=1, source_target_pairs={{0,2},{2,4},{4,6},{6,0},{1,3},{3,5},{5,7},{7,1},{8,10},{10,12},{12... | collective-permute-start | bytes 184328 | tf_op jit(solution)/shard_map/ppermute | solution.py:98
  26.5 12.1 %collective-permute-start.4 = (bf16[3,80,128]{2,1,0:T(8,128)(2,1)S(1)}, bf16[3,80,128]{2,1,0:T(8,128)(2,1)S(1)}, u32[]{:S(2)}, u32[]{:S(2)}) collective-permute-start(bf16[3,80,128]{2,1,0:T(8,128)(2,1)S(1)} %constant_dynamic-slice_fusion.3), channel_id=1, source_target_pairs={{0,4},{2,6},{4,0},{6,2},{1,5},{3,7},{5,1},{7,3},{8,12},{10,14},{12... | collective-permute-start | bytes 184328 | tf_op jit(solution)/shard_map/ppermute | solution.py:98
  28.3 14.5 %collective-permute-start.24 = (bf16[27,80,128]{2,1,0:T(8,128)(2,1)S(1)}, bf16[27,80,128]{2,1,0:T(8,128)(2,1)S(1)}, u32[]{:S(2)}, u32[]{:S(2)}) collective-permute-start(bf16[27,80,128]{2,1,0:T(8,128)(2,1)S(1)} %pad_maximum_fusion.1), channel_id=1, source_target_pairs={{0,1},{1,0},{2,3},{3,2},{4,5},{5,4},{6,7},{7,6},{8,24},{9,25},{10,... | collective-permute-start | bytes 1658888 | tf_op jit(solution)/shard_map/ppermute | solution.py:109
  32.1 7.1 %collective-permute-start.5 = (bf16[3,80,128]{2,1,0:T(8,128)(2,1)S(1)}, bf16[3,80,128]{2,1,0:T(8,128)(2,1)S(1)}, u32[]{:S(2)}, u32[]{:S(2)}) collective-permute-start(bf16[3,80,128]{2,1,0:T(8,128)(2,1)S(1)} %constant_dynamic-slice_fusion.3), channel_id=1, source_target_pairs={{0,6},{2,0},{4,2},{6,4},{1,7},{3,1},{5,3},{7,5},{8,14},{10,8},{12,... | collective-permute-start | bytes 184328 | tf_op jit(solution)/shard_map/ppermute | solution.py:98
  38.6 6.4 %collective-permute-start.9 = (bf16[3,80,128]{2,1,0:T(8,128)(2,1)S(1)}, bf16[3,80,128]{2,1,0:T(8,128)(2,1)S(1)}, u32[]{:S(2)}, u32[]{:S(2)}) collective-permute-start(bf16[3,80,128]{2,1,0:T(8,128)(2,1)S(1)} %constant_dynamic-slice_fusion.2), channel_id=1, source_target_pairs={{0,2},{2,4},{4,6},{6,0},{1,3},{3,5},{5,7},{7,1},{8,10},{10,12},{12... | collective-permute-start | bytes 184328 | tf_op jit(solution)/shard_map/ppermute | solution.py:98
  39.1 6.7 %collective-permute-start.10 = (bf16[3,80,128]{2,1,0:T(8,128)(2,1)S(1)}, bf16[3,80,128]{2,1,0:T(8,128)(2,1)S(1)}, u32[]{:S(2)}, u32[]{:S(2)}) collective-permute-start(bf16[3,80,128]{2,1,0:T(8,128)(2,1)S(1)} %constant_dynamic-slice_fusion.2), channel_id=1, source_target_pairs={{0,4},{2,6},{4,0},{6,2},{1,5},{3,7},{5,1},{7,3},{8,12},{10,14},{12... | collective-permute-start | bytes 184328 | tf_op jit(solution)/shard_map/ppermute | solution.py:98
  42.9 19.0 %collective-permute-start.25 = (bf16[54,80,128]{2,1,0:T(8,128)(2,1)S(1)}, bf16[54,80,128]{2,1,0:T(8,128)(2,1)S(1)}, u32[]{:S(2)}, u32[]{:S(2)}) collective-permute-start(bf16[54,80,128]{2,1,0:T(8,128)(2,1)S(1)} %pad_maximum_fusion), channel_id=1, source_target_pairs={{0,16},{1,17},{2,18},{3,19},{4,20},{5,21},{6,22},{7,23},{8,9},{9,8... | collective-permute-start | bytes 3317768 | tf_op jit(solution)/shard_map/ppermute | solution.py:110
  45.8 6.3 %collective-permute-start.27 = (bf16[3,80,128]{2,1,0:T(8,128)(2,1)S(1)}, bf16[3,80,128]{2,1,0:T(8,128)(2,1)S(1)}, u32[]{:S(2)}, u32[]{:S(2)}) collective-permute-start(bf16[3,80,128]{2,1,0:T(8,128)(2,1)S(1)} %constant_dynamic-slice_fusion), channel_id=1, source_target_pairs={{0,2},{2,4},{4,6},{6,0},{1,3},{3,5},{5,7},{7,1},{8,10},{10,12},{12... | collective-permute-start | bytes 184328 | tf_op jit(solution)/shard_map/ppermute | solution.py:98
  49.5 5.8 %collective-permute-start.28 = (bf16[3,80,128]{2,1,0:T(8,128)(2,1)S(1)}, bf16[3,80,128]{2,1,0:T(8,128)(2,1)S(1)}, u32[]{:S(2)}, u32[]{:S(2)}) collective-permute-start(bf16[3,80,128]{2,1,0:T(8,128)(2,1)S(1)} %constant_dynamic-slice_fusion), channel_id=1, source_target_pairs={{0,4},{2,6},{4,0},{6,2},{1,5},{3,7},{5,1},{7,3},{8,12},{10,14},{12... | collective-permute-start | bytes 184328 | tf_op jit(solution)/shard_map/ppermute | solution.py:98
  52.1 4.7 %collective-permute-start.29 = (bf16[3,80,128]{2,1,0:T(8,128)(2,1)S(1)}, bf16[3,80,128]{2,1,0:T(8,128)(2,1)S(1)}, u32[]{:S(2)}, u32[]{:S(2)}) collective-permute-start(bf16[3,80,128]{2,1,0:T(8,128)(2,1)S(1)} %constant_dynamic-slice_fusion), channel_id=1, source_target_pairs={{0,6},{2,0},{4,2},{6,4},{1,7},{3,1},{5,3},{7,5},{8,14},{10,8},{12,... | collective-permute-start | bytes 184328 | tf_op jit(solution)/shard_map/ppermute | solution.py:98
  55.3 12.0 %collective-permute-start.6 = (bf16[9,80,128]{2,1,0:T(8,128)(2,1)S(1)}, bf16[9,80,128]{2,1,0:T(8,128)(2,1)S(1)}, u32[]{:S(2)}, u32[]{:S(2)}) collective-permute-start(bf16[9,80,128]{2,1,0:T(8,128)(2,1)S(1)} %pad_maximum_fusion.5), channel_id=1, source_target_pairs={{0,1},{1,0},{2,3},{3,2},{4,5},{5,4},{6,7},{7,6},{8,24},{9,25},{10,... | collective-permute-start | bytes 552968 | tf_op jit(solution)/shard_map/ppermute | solution.py:109
  56.8 12.0 %collective-permute-start.12 = (bf16[9,80,128]{2,1,0:T(8,128)(2,1)S(1)}, bf16[9,80,128]{2,1,0:T(8,128)(2,1)S(1)}, u32[]{:S(2)}, u32[]{:S(2)}) collective-permute-start(bf16[9,80,128]{2,1,0:T(8,128)(2,1)S(1)} %pad_maximum_fusion.6), channel_id=1, source_target_pairs={{0,1},{1,0},{2,3},{3,2},{4,5},{5,4},{6,7},{7,6},{8,24},{9,25},{10,... | collective-permute-start | bytes 552968 | tf_op jit(solution)/shard_map/ppermute | solution.py:109
  63.0 55.8 %collective-permute-start.26 = (bf16[108,80,128]{2,1,0:T(8,128)(2,1)}, bf16[108,80,128]{2,1,0:T(8,128)(2,1)}, u32[]{:S(2)}, u32[]{:S(2)}) collective-permute-start(bf16[108,80,128]{2,1,0:T(8,128)(2,1)} %constant_dynamic-update-slice_fusion.10.refs_5_), channel_id=1, source_target_pairs={{0,8},{8,0},{1,9},{9,1},{2,10},{10,2},{3,11},{11,3},{4,12},{12,4},... | collective-permute-start | bytes 6635528 | tf_op jit(solution)/shard_map/ppermute | solution.py:111
  64.3 5.6 %collective-permute-start.30 = (bf16[9,80,128]{2,1,0:T(8,128)(2,1)S(1)}, bf16[9,80,128]{2,1,0:T(8,128)(2,1)S(1)}, u32[]{:S(2)}, u32[]{:S(2)}) collective-permute-start(bf16[9,80,128]{2,1,0:T(8,128)(2,1)S(1)} %pad_maximum_fusion.7), channel_id=1, source_target_pairs={{0,1},{1,0},{2,3},{3,2},{4,5},{5,4},{6,7},{7,6},{8,24},{9,25},{10,... | collective-permute-start | bytes 552968 | tf_op jit(solution)/shard_map/ppermute | solution.py:109
  67.0 17.0 %collective-permute-start.2 = (bf16[12,8,320]{2,1,0:T(8,128)(2,1)S(1)}, bf16[12,8,320]{2,1,0:T(8,128)(2,1)S(1)}, u32[]{:S(2)}, u32[]{:S(2)}) collective-permute-start(bf16[12,8,320]{2,1,0:T(8,128)(2,1)S(1)} %fusion.10), channel_id=1, source_target_pairs={{0,1},{1,0},{2,3},{3,2},{4,5},{5,4},{6,7},{7,6},{8,9},{9,8},{10,11... | collective-permute-start | bytes 184328 | tf_op jit(solution)/shard_map/ppermute | solution.py:375
  67.3 7.6 %collective-permute-start.7 = (bf16[18,80,128]{2,1,0:T(8,128)(2,1)S(1)}, bf16[18,80,128]{2,1,0:T(8,128)(2,1)S(1)}, u32[]{:S(2)}, u32[]{:S(2)}) collective-permute-start(bf16[18,80,128]{2,1,0:T(8,128)(2,1)S(1)} %pad_maximum_fusion.2), channel_id=1, source_target_pairs={{0,16},{1,17},{2,18},{3,19},{4,20},{5,21},{6,22},{7,23},{8,9},{9,8... | collective-permute-start | bytes 1105928 | tf_op jit(solution)/shard_map/ppermute | solution.py:110
  68.9 9.9 %collective-permute-start.13 = (bf16[18,80,128]{2,1,0:T(8,128)(2,1)S(1)}, bf16[18,80,128]{2,1,0:T(8,128)(2,1)S(1)}, u32[]{:S(2)}, u32[]{:S(2)}) collective-permute-start(bf16[18,80,128]{2,1,0:T(8,128)(2,1)S(1)} %pad_maximum_fusion.3), channel_id=1, source_target_pairs={{0,16},{1,17},{2,18},{3,19},{4,20},{5,21},{6,22},{7,23},{8,9},{9,8... | collective-permute-start | bytes 1105928 | tf_op jit(solution)/shard_map/ppermute | solution.py:110
  70.0 12.8 %collective-permute-start.31 = (bf16[18,80,128]{2,1,0:T(8,128)(2,1)S(1)}, bf16[18,80,128]{2,1,0:T(8,128)(2,1)S(1)}, u32[]{:S(2)}, u32[]{:S(2)}) collective-permute-start(bf16[18,80,128]{2,1,0:T(8,128)(2,1)S(1)} %pad_maximum_fusion.4), channel_id=1, source_target_pairs={{0,16},{1,17},{2,18},{3,19},{4,20},{5,21},{6,22},{7,23},{8,9},{9,8... | collective-permute-start | bytes 1105928 | tf_op jit(solution)/shard_map/ppermute | solution.py:110
  74.9 11.4 %collective-permute-start.8 = (bf16[36,80,128]{2,1,0:T(8,128)(2,1)S(1)}, bf16[36,80,128]{2,1,0:T(8,128)(2,1)S(1)}, u32[]{:S(2)}, u32[]{:S(2)}) collective-permute-start(bf16[36,80,128]{2,1,0:T(8,128)(2,1)S(1)} %constant_dynamic-update-slice_fusion.refs_1_), channel_id=1, source_target_pairs={{0,8},{8,0},{1,9},{9,1},{2,10},{10,2},{3,11},{11,3},{4,12},{12,4},... | collective-permute-start | bytes 2211848 | tf_op jit(solution)/shard_map/ppermute | solution.py:111
  78.9 7.4 %collective-permute-start.14 = (bf16[36,80,128]{2,1,0:T(8,128)(2,1)S(1)}, bf16[36,80,128]{2,1,0:T(8,128)(2,1)S(1)}, u32[]{:S(2)}, u32[]{:S(2)}) collective-permute-start(bf16[36,80,128]{2,1,0:T(8,128)(2,1)S(1)} %constant_dynamic-update-slice_fusion.5.refs_4_), channel_id=1, source_target_pairs={{0,8},{8,0},{1,9},{9,1},{2,10},{10,2},{3,11},{11,3},{4,12},{12,4},... | collective-permute-start | bytes 2211848 | tf_op jit(solution)/shard_map/ppermute | solution.py:111
  83.5 29.0 %collective-permute-start.32 = (bf16[36,80,128]{2,1,0:T(8,128)(2,1)}, bf16[36,80,128]{2,1,0:T(8,128)(2,1)}, u32[]{:S(2)}, u32[]{:S(2)}) collective-permute-start(bf16[36,80,128]{2,1,0:T(8,128)(2,1)} %constant_dynamic-update-slice_fusion.15.refs_8_), channel_id=1, source_target_pairs={{0,8},{8,0},{1,9},{9,1},{2,10},{10,2},{3,11},{11,3},{4,12},{12,4},... | collective-permute-start | bytes 2211848 | tf_op jit(solution)/shard_map/ppermute | solution.py:111
  95.8 7.1 %collective-permute-start.15 = (bf16[2,48,384]{2,1,0:T(8,128)(2,1)S(1)}, bf16[2,48,384]{2,1,0:T(8,128)(2,1)S(1)}, u32[]{:S(2)}, u32[]{:S(2)}) collective-permute-start(bf16[2,48,384]{2,1,0:T(8,128)(2,1)S(1)} %get-tuple-element.14.own), channel_id=1, source_target_pairs={{0,2},{2,4},{4,6},{6,0},{1,3},{3,5},{5,7},{7,1},{8,10},{10,12},{12... | collective-permute-start | bytes 221192 | tf_op jit(solution)/shard_map/ppermute | solution.py:408
  97.4 7.9 %collective-permute-start.16 = (bf16[2,48,384]{2,1,0:T(8,128)(2,1)S(1)}, bf16[2,48,384]{2,1,0:T(8,128)(2,1)S(1)}, u32[]{:S(2)}, u32[]{:S(2)}) collective-permute-start(bf16[2,48,384]{2,1,0:T(8,128)(2,1)S(1)} %get-tuple-element.14.own), channel_id=1, source_target_pairs={{0,4},{2,6},{4,0},{6,2},{1,5},{3,7},{5,1},{7,3},{8,12},{10,14},{12... | collective-permute-start | bytes 221192 | tf_op jit(solution)/shard_map/ppermute | solution.py:408
  98.1 7.1 %collective-permute-start.17 = (bf16[2,48,384]{2,1,0:T(8,128)(2,1)S(1)}, bf16[2,48,384]{2,1,0:T(8,128)(2,1)S(1)}, u32[]{:S(2)}, u32[]{:S(2)}) collective-permute-start(bf16[2,48,384]{2,1,0:T(8,128)(2,1)S(1)} %get-tuple-element.14.own), channel_id=1, source_target_pairs={{0,6},{2,0},{4,2},{6,4},{1,7},{3,1},{5,3},{7,5},{8,14},{10,8},{12,... | collective-permute-start | bytes 221192 | tf_op jit(solution)/shard_map/ppermute | solution.py:408
  108.0 7.6 %collective-permute-start.18 = (bf16[4,48,256]{2,1,0:T(8,128)(2,1)S(1)}, bf16[4,48,256]{2,1,0:T(8,128)(2,1)S(1)}, u32[]{:S(2)}, u32[]{:S(2)}) collective-permute-start(bf16[4,48,256]{2,1,0:T(8,128)(2,1)S(1)} %get-tuple-element.16), channel_id=1, source_target_pairs={{0,2},{2,4},{4,6},{6,0},{1,3},{3,5},{5,7},{7,1},{8,10},{10,12},{12... | collective-permute-start | bytes 294920 | tf_op jit(solution)/shard_map/ppermute | solution.py:427
  110.1 8.7 %collective-permute-start.19 = (bf16[4,48,256]{2,1,0:T(8,128)(2,1)S(1)}, bf16[4,48,256]{2,1,0:T(8,128)(2,1)S(1)}, u32[]{:S(2)}, u32[]{:S(2)}) collective-permute-start(bf16[4,48,256]{2,1,0:T(8,128)(2,1)S(1)} %get-tuple-element.17), channel_id=1, source_target_pairs={{0,4},{2,6},{4,0},{6,2},{1,5},{3,7},{5,1},{7,3},{8,12},{10,14},{12... | collective-permute-start | bytes 294920 | tf_op jit(solution)/shard_map/ppermute | solution.py:427
  111.0 7.8 %collective-permute-start.20 = (bf16[4,48,256]{2,1,0:T(8,128)(2,1)S(1)}, bf16[4,48,256]{2,1,0:T(8,128)(2,1)S(1)}, u32[]{:S(2)}, u32[]{:S(2)}) collective-permute-start(bf16[4,48,256]{2,1,0:T(8,128)(2,1)S(1)} %get-tuple-element.18), channel_id=1, source_target_pairs={{0,6},{2,0},{4,2},{6,4},{1,7},{3,1},{5,3},{7,5},{8,14},{10,8},{12,... | collective-permute-start | bytes 294920 | tf_op jit(solution)/shard_map/ppermute | solution.py:427
  (12 other events, 114.4 us)

commit v2 on v1

--- a/solution.py
+++ b/solution.py
@@ -23,6 +23,10 @@
     return pltpu.CompilerParams(vmem_limit_bytes=52 * 1024 * 1024)
 
 
+def cost(cells):
+    return pl.CostEstimate(flops=cells * 9 * 320 * 640 * 2, bytes_accessed=1 << 20, transcendentals=0)
+
+
 def plain_chunks(base):
     chunks = [[(tap, base + half * LANES, LANES)] for tap in range(9) for half in range(2)]
     rest = [(tap, base + 256, 64) for tap in range(9)]
@@ -44,35 +48,41 @@
     return -(-len(chunks) // PIECES) * PIECES
 
 
-def pack_body(layouts, *refs):
+def pack_body(layouts, parts, place, *refs):
     count = len(layouts)
-    for chunks, source, target in zip(layouts, refs[:count], refs[count:]):
-        channels = source.shape[2]
-        for index in range(target.shape[0]):
-            if index < len(chunks):
-                parts = [source[tap, pl.ds(first, size), :] for tap, first, size in chunks[index]]
-                have = sum(part.shape[0] for part in parts)
-                if have < LANES:
-                    parts.append(jnp.zeros((LANES - have, channels), BF))
-                block = parts[0] if len(parts) == 1 else jnp.concatenate(parts, axis=0)
-                target[index] = block.T
-            else:
-                target[index] = jnp.zeros((channels, LANES), BF)
-
-
-def pack(layouts, weights):
-    shapes = [
-        jax.ShapeDtypeStruct((padded_count(chunks), weight.shape[2], LANES), BF)
-        for chunks, weight in zip(layouts, weights)
-    ]
+    own, mine = refs[count:]
+    index = 0
+    for chunks, source in zip(layouts, refs):
+        channels = source.shape[1]
+        for chunk in chunks:
+            parts = [source[tap, :, pl.ds(first, size)] for tap, first, size in chunk]
+            have = sum(part.shape[1] for part in parts)
+            if have < LANES:
+                parts.append(jnp.zeros((channels, LANES - have), BF))
+            own[index] = parts[0] if len(parts) == 1 else jnp.concatenate(parts, axis=1)
+            index += 1
+    while index < own.shape[0]:
+        own[index] = jnp.zeros(own.shape[1:], BF)
+        index += 1
+    size = mine.shape[0]
+    mine[...] = own[pl.ds(owner_piece(place, parts, place[1], 0) * size, size)]
+
+
+def pack(layouts, parts, place, weights):
+    total = padded_count([chunk for chunks in layouts for chunk in chunks])
+    weights = [jnp.swapaxes(weight, 1, 2) for weight in weights]
+    channels = weights[0].shape[1]
     return pl.pallas_call(
-        functools.partial(pack_body, layouts),
-        out_shape=shapes,
-        in_specs=[VMEM] * len(weights),
-        out_specs=[VMEM] * len(weights),
+        functools.partial(pack_body, layouts, parts),
+        out_shape=[
+            jax.ShapeDtypeStruct((total, channels, LANES), BF),
+            jax.ShapeDtypeStruct((total // parts, channels, LANES), BF),
+        ],
+        in_specs=[SMEM] + [VMEM] * len(weights),
+        out_specs=[VMEM, VMEM],
         compiler_params=params(),
         name="pack_weights",
-    )(*weights)
+    )(place, *weights)
 
 
 def device_pairs(mesh_shape, move):
@@ -91,44 +101,87 @@
     return [(i, (i + by) % count) for i in range(count)]
 
 
-def gather_planes(packed, piece, count):
-    size = packed.shape[0] // PIECES
-    mine = lax.dynamic_slice_in_dim(packed, piece * size, size, axis=0)
-    return jnp.concatenate(
-        [lax.ppermute(mine, "row", cyclic(count, by)) for by in range(1, count)], axis=0
-    )
-
-
-def gather_plane(block, mesh_shape):
+def after(value, *others):
+    return lax.optimization_barrier((value,) + others)[0]
+
+
+def laid_body(cuts, *refs):
+    count = len(cuts)
+    sources, target, sems = refs[:count], refs[count], refs[count + 1]
+    copies, at = [], 0
+    for index, (source, (first, size)) in enumerate(zip(sources, cuts)):
+        copies.append(
+            pltpu.make_async_copy(
+                source.at[pl.ds(first, size)], target.at[pl.ds(at, size)], sems.at[index]
+            )
+        )
+        at += size
+    for copy in copies:
+        copy.start()
+    for copy in copies:
+        copy.wait()
+
+
+def laid(*parts, cut=None):
+    cuts = tuple(cut or (0, part.shape[0]) for part in parts)
+    return pl.pallas_call(
+        functools.partial(laid_body, cuts),
+        out_shape=jax.ShapeDtypeStruct((sum(size for _, size in cuts),) + parts[0].shape[1:], BF),
+        in_specs=[HBM] * len(parts),
+        out_specs=VMEM,
+        scratch_shapes=[pltpu.SemaphoreType.DMA((len(parts),))],
+        compiler_params=params(),
+        cost_estimate=pl.CostEstimate(flops=0, bytes_accessed=1 << 21, transcendentals=0),
+        name="laid",
+    )(*parts)
+
+
+def from_planes(mine, count):
+    return [lax.ppermute(mine, "row", cyclic(count, by)) for by in range(1, count)]
+
+
+def plane_moves(mesh_shape):
     first = device_pairs(
         mesh_shape, lambda g, s, r, c: (g, s, r, 1 - c) if s == 0 else (1 - g, s, r, c)
     )
     second = device_pairs(
         mesh_shape, lambda g, s, r, c: (1 - g, s, r, c) if s == 0 else (g, s, r, 1 - c)
     )
-    block = jnp.concatenate([block, lax.ppermute(block, AXES, first)], axis=0)
-    block = jnp.concatenate([block, lax.ppermute(block, AXES, second)], axis=0)
-    return block, lax.ppermute(block, "segment", [(0, 1), (1, 0)])
-
-
-def load_weights(place, sources, target, sem):
+    return first, second
+
+
+def swap_cores(block):
+    return lax.ppermute(block, "segment", [(0, 1), (1, 0)])
+
+
+def owner_piece(place, parts, core, slot):
+    grp, col = place[0], place[3]
+    low, high = slot % 2, slot // 2
+    if parts == 4:
+        col, grp = (1 - col, 1 - grp) if low else (col, grp)
+        return jnp.where(core == 0, col, 2 + grp)
+    flip_col = jnp.where(core == 0, low, high)
+    flip_grp = jnp.where(core == 0, high, low)
+    grp = jnp.where(flip_grp == 1, 1 - grp, grp)
+    col = jnp.where(flip_col == 1, 1 - col, col)
+    return (grp * 2 + core) * 2 + col
+
+
+def load_weights(place, parts, sources, target, sem):
     if len(sources) == 1:
         return [pltpu.make_async_copy(sources[0], target, sem)]
-    own, near, far = sources
-    grp, seg, row, col = (place[i] for i in range(4))
-    size = own.shape[0] // PIECES
+    own, near0, near1, far0, far1 = sources
+    seg, row = place[1], place[2]
+    size = own.shape[0] // parts
+    each = parts // 4
     copies = [pltpu.make_async_copy(own, target.at[:, row], sem)]
-    for part, core in ((near, seg), (far, 1 - seg)):
-        for slot in range(4):
-            low, high = slot % 2, slot // 2
-            flip_col = jnp.where(core == 0, low, high)
-            flip_grp = jnp.where(core == 0, high, low)
-            owner_grp = jnp.where(flip_grp == 1, 1 - grp, grp)
-            owner_col = jnp.where(flip_col == 1, 1 - col, col)
-            piece = (owner_grp * 2 + core) * 2 + owner_col
+    for pair, core in (((near0, near1), seg), ((far0, far1), 1 - seg)):
+        for slot in range(2 * each):
+            array = pair[slot // each]
+            piece = owner_piece(place, parts, core, slot)
             for by in range(1, SHARDS):
                 shard = lax.rem(row - by + SHARDS, SHARDS)
-                source = part.at[pl.ds((slot * 3 + by - 1) * size, size)]
+                source = array.at[pl.ds(((slot % each) * 3 + by - 1) * size, size)]
                 copies.append(
                     pltpu.make_async_copy(source, target.at[pl.ds(piece * size, size), shard], sem)
                 )
@@ -159,7 +212,7 @@
     return lax.dot_general(left, right, (((1,), (1,)), ((), ())), preferred_element_type=F32)
 
 
-def add_plain(shifted, weights, rows, wide, acc, bias):
+def add_plain(shifted, weights, base, rows, wide, acc, bias):
     cells = rows * wide
 
     def window(tap, first, size):
@@ -174,13 +227,13 @@
         lane = lax.broadcasted_iota(jnp.int32, (cells, LANES), 1)
         return jnp.where(lane < 64, low, high)
 
-    acc[:cells] = product(window(0, 0, 256), weight_pair(weights, 0, 1)) + bias
+    acc[:cells] = product(window(0, 0, 256), weight_pair(weights, base, base + 1)) + bias
     for tap in range(1, 9):
-        acc[:cells] += product(window(tap, 0, 256), weight_pair(weights, 2 * tap, 2 * tap + 1))
+        acc[:cells] += product(window(tap, 0, 256), weight_pair(weights, base + 2 * tap, base + 2 * tap + 1))
     for at in range(0, 4, 2):
         left = jnp.concatenate([rest(at), rest(at + 1)], axis=1)
-        acc[:cells] += product(left, weight_pair(weights, 18 + at, 19 + at))
-    acc[:cells] += product(rest(4), weight_pair(weights, 22, None))
+        acc[:cells] += product(left, weight_pair(weights, base + 18 + at, base + 19 + at))
+    acc[:cells] += product(rest(4), weight_pair(weights, base + 22, None))
 
 
 def inside(place, rows, wide, first_row, first_col, size):
@@ -197,27 +250,23 @@
     return jnp.concatenate([value, value[:, 256:320]], axis=1)
 
 
-def encoder_body(size, sets, place, cells, bias1, bias2, *refs):
+def encoder_body(size, sets, parts, place, cells, bias1, bias2, *refs):
     tile_rows, tile_cols = size[:2]
     wide = tile_cols + 2 * SIDE
-    sources1, refs = refs[:sets], refs[sets:]
-    sources2, refs = refs[:sets], refs[sets:]
-    skip, pooled, w1, w2, shifted, acc, sems = refs
-    copies1 = load_weights(place, sources1, w1, sems.at[0])
-    copies2 = load_weights(place, sources2, w2, sems.at[1])
-    for copy in copies1 + copies2:
+    sources, refs = refs[:sets], refs[sets:]
+    skip, pooled, weights, shifted, acc, sem = refs
+    copies = load_weights(place, parts, sources, weights, sem)
+    for copy in copies:
         copy.start()
     spread(cells[...].astype(F32), shifted)
-    for copy in copies1:
+    for copy in copies:
         copy.wait()
     rows = tile_rows + 6
-    add_plain(shifted, w1, rows, wide, acc, bias1[...])
+    add_plain(shifted, weights, 0, rows, wide, acc, bias1[...])
     hidden = activated(acc, rows, wide, inside(place, rows, wide, -3, -SIDE, size))
     spread(hidden, shifted)
-    for copy in copies2:
-        copy.wait()
     rows = tile_rows + 4
-    add_plain(shifted, w2, rows, wide, acc, bias2[...])
+    add_plain(shifted, weights, 23, rows, wide, acc, bias2[...])
     value = activated(acc, rows, wide, inside(place, rows, wide, -2, -SIDE, size)).astype(BF)
     skip[...] = value
     half = pooled.shape[1]
@@ -249,13 +298,13 @@
         field[pl.ds(1 + tall * at, tall)] = source[...].astype(F32)
     spread(field[...].reshape(flat, field.shape[2]), shifted)
     cells = rows * half
-    channels = weights.shape[2]
+    channels = weights.shape[1]
     acc[...] = jnp.zeros_like(acc)
     for tap in range(9):
         at = (tap // 3) * half
         left = shifted[tap % 3, pl.ds(at, cells), :]
-        part = jnp.dot(left[:, :256], weights[tap, :256, :], preferred_element_type=F32)
-        part += jnp.dot(left[:, 256:320], weights[tap, 256:320, :], preferred_element_type=F32)
+        part = product(left[:, :256], weights[tap, :, :256])
+        part += product(left[:, 256:320], weights[tap, :, 256:320])
         if tap == 0:
             part += bias[...]
         acc[:, :channels] += part
@@ -274,16 +323,14 @@
         outs[by][...] = result[pl.ds(tall * at, tall + 2)]
 
 
-def decoder_body(size, sets, place, skip, bias1, bias2, *refs):
+def joined_body(size, sets, parts, place, skip, bias, *refs):
     tile_rows, tile_cols = size[:2]
     wide = tile_cols + 2 * SIDE
     mids, refs = refs[:SHARDS], refs[SHARDS:]
-    sources1, refs = refs[:sets], refs[sets:]
-    sources2, refs = refs[:sets], refs[sets:]
-    out, w1, w2, shifted, raised, field, acc, sems = refs
-    copies1 = load_weights(place, sources1, w1, sems.at[0])
-    copies2 = load_weights(place, sources2, w2, sems.at[1])
-    for copy in copies1 + copies2:
+    sources, refs = refs[:sets], refs[sets:]
+    out, weights, shifted, raised, field, acc, sem = refs
+    copies = load_weights(place, parts, sources, weights, sem)
+    for copy in copies:
         copy.start()
     spread(skip[...].astype(F32), shifted)
     half = mids[0].shape[1]
@@ -293,7 +340,7 @@
         tail = tail + mid[:, :, LANES:]
     field[4] = tail
     for by in range(SHARDS):
-        shard = lax.rem(place[2] - by + SHARDS, SHARDS) if sets == 3 else by
+        shard = lax.rem(place[2] - by + SHARDS, SHARDS) if sets > 1 else by
         field[shard] = mids[by][:, :, :LANES]
     cell = lax.broadcasted_iota(jnp.int32, (3 * wide, half), 0)
     move = jnp.where(cell >= 2 * wide, 1 - 2 * wide, jnp.where(cell >= wide, -wide, -1))
@@ -307,11 +354,11 @@
             for twice in range(2):
                 at = (2 * row + twice) * wide
                 raised[dx, at : at + wide] = up[dx * wide : (dx + 1) * wide]
-    for copy in copies1:
+    for copy in copies:
         copy.wait()
     rows = tile_rows + 2
     cells = rows * wide
-    add_plain(shifted, w1, rows, wide, acc, bias1[...])
+    add_plain(shifted, weights, 0, rows, wide, acc, bias[...])
 
     def window(tap, first, count):
         return raised[tap % 3, pl.ds((tap // 3) * wide, cells), pl.ds(first, count)]
@@ -320,18 +367,28 @@
         at = 23 + 5 * tap
         for pair in range(2):
             left = window(tap, 256 * pair, 256)
-            acc[:cells] += product(left, weight_pair(w1, at + 2 * pair, at + 2 * pair + 1))
+            acc[:cells] += product(left, weight_pair(weights, at + 2 * pair, at + 2 * pair + 1))
         if tap % 2 == 1:
             left = jnp.concatenate([window(tap - 1, 512, LANES), window(tap, 512, LANES)], axis=1)
-            acc[:cells] += product(left, weight_pair(w1, at - 1, at + 4))
+            acc[:cells] += product(left, weight_pair(weights, at - 1, at + 4))
         elif tap == 8:
-            acc[:cells] += product(window(tap, 512, LANES), weight_pair(w1, at + 4, None))
-    refined = activated(acc, rows, wide, inside(place, rows, wide, -1, -SIDE, size))
-    spread(refined, shifted)
-    for copy in copies2:
+            acc[:cells] += product(window(tap, 512, LANES), weight_pair(weights, at + 4, None))
+    out[...] = activated(acc, rows, wide, inside(place, rows, wide, -1, -SIDE, size)).astype(BF)
+
+
+def last_body(size, sets, parts, place, refined, bias, *refs):
+    tile_rows, tile_cols = size[:2]
+    wide = tile_cols + 2 * SIDE
+    sources, refs = refs[:sets], refs[sets:]
+    out, weights, shifted, acc, sem = refs
+    copies = load_weights(place, parts, sources, weights, sem)
+    for copy in copies:
+        copy.start()
+    spread(refined[...].astype(F32), shifted)
+    for copy in copies:
         copy.wait()
-    add_plain(shifted, w2, tile_rows, wide, acc, bias2[...])
-    value = silu(acc[: tile_rows * wide]).reshape(tile_rows, wide, acc.shape[1])
+    add_plain(shifted, weights, 0, tile_rows, wide, acc, bias[...])
+    value = silu(acc[...]).reshape(tile_rows, wide, acc.shape[1])
     out[0] = value[:, SIDE : SIDE + tile_cols, :].astype(BF)
 
 
@@ -340,7 +397,6 @@
     grps, segs, row_count, col_count = mesh_shape
     grp, seg, row, col = (lax.axis_index(axis) for axis in AXES)
     place = jnp.stack([grp, seg, row, col]).astype(jnp.int32)
-    piece = (grp * 2 + seg) * 2 + col
     tile_rows, tile_cols, channels = latent.shape[1:]
     size = (tile_rows, tile_cols, row_count, col_count)
     wide = tile_cols + 2 * SIDE
@@ -348,24 +404,19 @@
     spread_out = row_count == SHARDS and col_count == 2 and grps == 2 and segs == 2
     plain, joined = plain_chunks(0), joined_chunks()
 
+    groups = (
+        ((plain, plain), 8, (enc_first, enc_second)),
+        ((joined,), 8, (dec_first,)),
+        ((plain,), 8, (dec_second,)),
+    )
     if spread_out:
-        (own1,) = pack((plain,), (enc_first,))
-        (own2,) = pack((plain,), (enc_second,))
-        own3, own4 = pack((joined, plain), (dec_first, dec_second))
-        sets = 3
-        weights = []
-        for own in (own1, own2, own3, own4):
-            block = gather_planes(own, piece, row_count)
-            weights.append((own,) + gather_plane(block, mesh_shape))
-    else:
-        sets = 1
-        weights = []
-        for chunks, weight in ((plain, enc_first), (plain, enc_second), (joined, dec_first), (plain, dec_second)):
-            full = lax.all_gather(weight, "row", axis=2, tiled=True)
-            (own,) = pack((chunks,), (full,))
-            weights.append((own.reshape(own.shape[0], SHARDS, -1, LANES),))
+        (own0, mine0), (own1, mine1), (own2, mine2) = (
+            pack(layouts, parts, place, group) for layouts, parts, group in groups
+        )
 
     tile = lax.dynamic_index_in_dim(latent, seg, 0, keepdims=False)
+    if spread_out:
+        tile = after(tile, mine0)
     down = [(i, i + 1) for i in range(row_count - 1)]
     above = lax.ppermute(tile, "row", down)
     below = lax.ppermute(tile, "row", [(b, a) for a, b in down])
@@ -379,33 +430,63 @@
         along = [(i, i + 1) for i in range(col_count - 1)]
         left = lax.ppermute(right_edge, "col", along)
         right = lax.ppermute(left_edge, "col", [(b, a) for a, b in along])
+        edge = left
     tile = jnp.concatenate([left, tile, right], axis=1)
     cells = jnp.concatenate([tile, tile[:, :, 256:]], axis=2).reshape(-1, 3 * LANES)
 
+    sets = 5 if spread_out else 1
+    weights = []
+    if spread_out:
+        first, second = plane_moves(mesh_shape)
+        across = lambda block, pairs: lax.ppermute(block, AXES, pairs)
+        here0 = from_planes(mine0, row_count)
+        here1 = from_planes(laid(mine1, mine2), row_count)
+        block0 = laid(*here0)
+        block0 = laid(block0, across(block0, first))
+        block0 = after(block0, here1[0], above, below)
+        far0 = swap_cores(block0)
+        next0 = after(across(block0, second), edge, here1[1], here1[2])
+        held0 = (block0, next0, far0, swap_cores(next0))
+        part1, part2 = mine1.shape[0], mine2.shape[0]
+        block1 = laid(*here1, cut=(0, part1))
+        weights = [(own0,) + held0]
+    else:
+        for layouts, parts, group in groups:
+            full = [lax.all_gather(weight, "row", axis=2, tiled=True) for weight in group]
+            own = pack(layouts, parts, place, full)[0]
+            weights.append((own.reshape(own.shape[0], SHARDS, -1, LANES),))
+
     scratch = lambda *shape: pltpu.VMEM(shape, BF)
     lines = lambda bias: bias.reshape(1, -1)
+    packed = lambda source: scratch(source[0].shape[0], SHARDS, channels // SHARDS, LANES)
     skip, pooled = pl.pallas_call(
-        functools.partial(encoder_body, size, sets),
+        functools.partial(encoder_body, size, sets, groups[0][1]),
         out_shape=[
             jax.ShapeDtypeStruct(((tile_rows + 4) * wide, 3 * LANES), BF),
             jax.ShapeDtypeStruct((tile_rows // 2, half, 3 * LANES), BF),
         ],
-        in_specs=[SMEM, VMEM, VMEM, VMEM] + [HBM] * (2 * sets),
+        in_specs=[SMEM, VMEM, VMEM, VMEM] + [HBM] * sets,
         out_specs=[VMEM, VMEM],
         scratch_shapes=[
-            scratch(24, SHARDS, channels // SHARDS, LANES),
-            scratch(24, SHARDS, channels // SHARDS, LANES),
+            packed(weights[0]),
             scratch(3, 3 * tile_rows * wide, 3 * LANES),
             pltpu.VMEM(((tile_rows + 6) * wide, channels), F32),
-            pltpu.SemaphoreType.DMA((2,)),
+            pltpu.SemaphoreType.DMA,
         ],
         compiler_params=params(),
+        cost_estimate=cost(4 * (2 * tile_rows + 10) * wide),
         name="encoder",
-    )(place, cells, lines(enc_first_bias), lines(enc_second_bias), *weights[0], *weights[1])
+    )(place, cells, lines(enc_first_bias), lines(enc_second_bias), *weights[0])
 
     tall = tile_rows // 2
     if spread_out:
         others = [lax.ppermute(pooled, "row", cyclic(row_count, by)) for by in range(1, row_count)]
+        block1 = laid(block1, after(across(block1, first), pooled))
+        far1 = swap_cores(block1)
+        next1 = across(block1, second)
+        block2 = laid(*here1, cut=(part1, part2))
+        block2 = laid(block2, after(across(block2, first), pooled))
+        others = after(others, block2)
         part = mid_weight.shape[2]
         bias = lax.dynamic_slice_in_dim(mid_bias, row * part, part, 0)
         rows = tall * row_count
@@ -421,11 +502,17 @@
                 scratch(rows + 2, half, 2 * LANES),
             ],
             compiler_params=params(),
+            cost_estimate=cost(4 * tile_rows * wide),
             name="middle",
-        )(place, pooled, *others, mid_weight, lines(bias))
+        )(place, pooled, *others, jnp.swapaxes(mid_weight, 1, 2), lines(bias))
         mids = [sent[0]] + [
             lax.ppermute(sent[by], "row", cyclic(row_count, by)) for by in range(1, row_count)
         ]
+        next1 = after(next1, sent[0])
+        held1 = (block1, next1, far1, swap_cores(next1))
+        next2 = after(across(after(block2, sent[0]), second), *mids)
+        held2 = (block2, next2, swap_cores(block2), swap_cores(next2))
+        weights += [(own1,) + held1, (own2,) + held2]
     else:
         full = lax.all_gather(mid_weight, "row", axis=2, tiled=True)
         field = jnp.concatenate(
@@ -448,23 +535,38 @@
             tail = jnp.pad(block[:, :, LANES:], ((0, 0), (0, 0), (32 * shard, 96 - 32 * shard)))
             mids.append(jnp.concatenate([block[:, :, :LANES], tail], axis=2))
 
-    return pl.pallas_call(
-        functools.partial(decoder_body, size, sets),
-        out_shape=jax.ShapeDtypeStruct((1, tile_rows, tile_cols, channels), BF),
-        in_specs=[SMEM, VMEM, VMEM, VMEM] + [VMEM] * SHARDS + [HBM] * (2 * sets),
+    refined = pl.pallas_call(
+        functools.partial(joined_body, size, sets, groups[1][1]),
+        out_shape=jax.ShapeDtypeStruct(((tile_rows + 2) * wide, 3 * LANES), BF),
+        in_specs=[SMEM, VMEM, VMEM] + [VMEM] * SHARDS + [HBM] * sets,
         out_specs=VMEM,
         scratch_shapes=[
-            scratch(padded_count(joined), SHARDS, channels // SHARDS, LANES),
-            scratch(24, SHARDS, channels // SHARDS, LANES),
+            packed(weights[1]),
             scratch(3, (tile_rows + 4) * wide, 3 * LANES),
             scratch(3, (tile_rows + 4) * wide, 5 * LANES),
             scratch(5, tall + 2, half, LANES),
             pltpu.VMEM(((tile_rows + 2) * wide, channels), F32),
-            pltpu.SemaphoreType.DMA((2,)),
+            pltpu.SemaphoreType.DMA,
         ],
         compiler_params=params(),
-        name="decoder",
-    )(place, skip, lines(dec_first_bias), lines(dec_second_bias), *mids, *weights[2], *weights[3])
+        cost_estimate=cost(6 * (tile_rows + 2) * wide),
+        name="joined",
+    )(place, skip, lines(dec_first_bias), *mids, *weights[1])
+    return pl.pallas_call(
+        functools.partial(last_body, size, sets, groups[2][1]),
+        out_shape=jax.ShapeDtypeStruct((1, tile_rows, tile_cols, channels), BF),
+        in_specs=[SMEM, VMEM, VMEM] + [HBM] * sets,
+        out_specs=VMEM,
+        scratch_shapes=[
+            packed(weights[2]),
+            scratch(3, (tile_rows + 2) * wide, 3 * LANES),
+            pltpu.VMEM((tile_rows * wide, channels), F32),
+            pltpu.SemaphoreType.DMA,
+        ],
+        compiler_params=params(),
+        cost_estimate=cost(2 * tile_rows * wide),
+        name="last",
+    )(place, refined, lines(dec_second_bias), *weights[2])
 
 
 def solution(mesh):

time: 130 us -> 114 us (0.88)
  local copies, waits for them, and re-layouts: 19.9 us -> 6.92 us
  starting transfers between devices: 49.4 us -> 40.4 us
  Pallas kernels: 25.1 us -> 30.5 us
  waiting for transfers between devices: 30.6 us -> 35.1 us
  other arithmetic: 3.57 us -> 0.3 us
    ppermute x24 -> x18, starting transfers between devices: 34.2 us -> 19.1 us  [the longest x6 14.4 us: from_planes(): lax.ppermute(mine, 'row', cyclic(count, by))]
    unnamed x43 -> x34, local copies, waits for them, and re-layouts: 16.1 us -> 6.1 us
    ppermute x24 -> x18, waiting for transfers between devices: 21.9 us -> 14.9 us  [the longest x6 12 us: from_planes(): lax.ppermute(mine, 'row', cyclic(count, by))]
    pallas_call x5 -> x13, Pallas kernels: 22.3 us -> 28.5 us  [the longest x1 8.64 us: shards(): pl.pallas_call(functools.partial(joined_body, size, sets, groups[1][1]),...]
    ppermute x1, waiting for transfers between devices: 0.01 us -> 5.72 us  [shards(): above = lax.ppermute(tile, 'row', down)]
    ppermute x3, starting transfers between devices: 4.54 us -> 10 us  [shards(): lax.ppermute(sent[by], 'row', cyclic(row_count, by))]
    ppermute x1, waiting for transfers between devices: 0.01 us -> 4.62 us  [shards(): lax.ppermute(jnp.where(col == 0, right_edge, left_edge), 'col', [(0, 1),...]
    ppermute x3, starting transfers between devices: 4 us -> 7.4 us  [shards(): lax.ppermute(pooled, 'row', cyclic(row_count, by))]
  transfers between devices with their start and end apart: 33 -> 27, of which waited for: 18 -> 13; matrix products, arithmetic and copies ran while one was open for 13% -> 1% of each run, Pallas kernels for 9% -> 21%
where the time goes in v2:
time: 114 us
  starting transfers between devices  40.4 us (35%)
  waiting for transfers between devices  35.1 us (31%)
  Pallas kernels  30.5 us (27%)
  local copies, waits for them, and re-layouts  6.92 us (6%)
    ppermute x6, starting transfers between devices, from_planes(): lax.ppermute(mine, 'row', cyclic(count, by))  14.4 us
    ppermute x6, waiting for transfers between devices, from_planes(): lax.ppermute(mine, 'row', cyclic(count, by))  12 us
    ppermute x3, starting transfers between devices, shards(): lax.ppermute(sent[by], 'row', cyclic(row_count, by))  10 us
    pallas_call x1, Pallas kernels, shards(): pl.pallas_call(functools.partial(joined_body, size, sets, groups[1][1]),...  8.64 us
    pallas_call x1, Pallas kernels, shards(): pl.pallas_call(functools.partial(encoder_body, size, sets, groups[0][1]),...  8.25 us
    ppermute x3, starting transfers between devices, shards(): lax.ppermute(pooled, 'row', cyclic(row_count, by))  7.4 us
    unnamed x34, local copies, waits for them, and re-layouts  6.1 us
    ppermute x1, waiting for transfers between devices, shards(): above = lax.ppermute(tile, 'row', down)  5.72 us
  transfers between devices with their start and end apart: 27, of which 13 were waited for; matrix products, arithmetic and copies ran while one was open for 1% of the time, Pallas kernels for 21%

profile of v2, /device:TPU:0, one launch (start us, length us, event | category | flops | bytes accessed | tf_op | source)
XLA Modules:
  0.0 113.8 jit_solution(5817995829659786406)
XLA Ops:
  2.2 1.7 %pack_weights.3 = (bf16[48,80,128]{2,1,0:T(8,128)(2,1)}, bf16[6,80,128]{2,1,0:T(8,128)(2,1)S(1)}) custom-call(s32[4]{0:T(128)S(1)} %pad_add_fusion.place, bf16[9,80,320]{2,1,0:T(8,128)(2,1)S(1)} %bitcast.15, bf16[9,80,320]{2,1,0:T(8,128)(2,1)S(1)} %bitcast.16), custom_call_target="tpu_custom_call" | custom-call | tf_op jit(solution)/shard_map/pack_weights/pallas_call | solution.py:75
  3.9 3.0 %collective-permute-start.3 = (bf16[6,80,128]{2,1,0:T(8,128)(2,1)S(1)}, bf16[6,80,128]{2,1,0:T(8,128)(2,1)S(1)}, u32[]{:S(2)}, u32[]{:S(2)}) collective-permute-start(bf16[6,80,128]{2,1,0:T(8,128)(2,1)S(1)} %get-tuple-element.28), channel_id=1, source_target_pairs={{0,2},{2,4},{4,6},{6,0},{1,3},{3,5},{5,7},{7,1},{8,10},{10,12},{12... | collective-permute-start | bytes 368648 | tf_op jit(solution)/shard_map/ppermute | solution.py:140
  6.9 2.6 %collective-permute-start.4 = (bf16[6,80,128]{2,1,0:T(8,128)(2,1)S(1)}, bf16[6,80,128]{2,1,0:T(8,128)(2,1)S(1)}, u32[]{:S(2)}, u32[]{:S(2)}) collective-permute-start(bf16[6,80,128]{2,1,0:T(8,128)(2,1)S(1)} %get-tuple-element.28), channel_id=1, source_target_pairs={{0,4},{2,6},{4,0},{6,2},{1,5},{3,7},{5,1},{7,3},{8,12},{10,14},{12... | collective-permute-start | bytes 368648 | tf_op jit(solution)/shard_map/ppermute | solution.py:140
  9.5 1.3 %collective-permute-start.5 = (bf16[6,80,128]{2,1,0:T(8,128)(2,1)S(1)}, bf16[6,80,128]{2,1,0:T(8,128)(2,1)S(1)}, u32[]{:S(2)}, u32[]{:S(2)}) collective-permute-start(bf16[6,80,128]{2,1,0:T(8,128)(2,1)S(1)} %get-tuple-element.28), channel_id=1, source_target_pairs={{0,6},{2,0},{4,2},{6,4},{1,7},{3,1},{5,3},{7,5},{8,14},{10,8},{12,... | collective-permute-start | bytes 368648 | tf_op jit(solution)/shard_map/ppermute | solution.py:140
  10.9 2.3 %collective-permute-done.3.refs_0_ = bf16[6,80,128]{2,1,0:T(8,128)(2,1)S(1)} collective-permute-done((bf16[6,80,128]{2,1,0:T(8,128)(2,1)S(1)}, bf16[6,80,128]{2,1,0:T(8,128)(2,1)S(1)}, u32[]{:S(2)}, u32[]{:S(2)}) %collective-permute-start.3) | collective-permute-done | bytes 122912 | tf_op jit(solution)/shard_map/ppermute | solution.py:140
  13.2 4.4 %collective-permute-done.4.refs_1_ = bf16[6,80,128]{2,1,0:T(8,128)(2,1)S(1)} collective-permute-done((bf16[6,80,128]{2,1,0:T(8,128)(2,1)S(1)}, bf16[6,80,128]{2,1,0:T(8,128)(2,1)S(1)}, u32[]{:S(2)}, u32[]{:S(2)}) %collective-permute-start.4) | collective-permute-done | bytes 122912 | tf_op jit(solution)/shard_map/ppermute | solution.py:140
  18.1 1.6 %collective-permute-start.6 = (bf16[18,80,128]{2,1,0:T(8,128)(2,1)S(1)}, bf16[18,80,128]{2,1,0:T(8,128)(2,1)S(1)}, u32[]{:S(2)}, u32[]{:S(2)}) collective-permute-start(bf16[18,80,128]{2,1,0:T(8,128)(2,1)S(1)} %laid.7.refs_0_), channel_id=1, source_target_pairs={{0,1},{1,0},{2,3},{3,2},{4,5},{5,4},{6,7},{7,6},{8,24},{9,25},{10,... | collective-permute-start | bytes 1105928 | tf_op jit(solution)/shard_map/ppermute | solution.py:441
  19.7 2.0 %pack_weights.4 = (bf16[72,80,128]{2,1,0:T(8,128)(2,1)S(1)}, bf16[9,80,128]{2,1,0:T(8,128)(2,1)S(1)}) custom-call(s32[4]{0:T(128)S(1)} %pad_add_fusion.place, bf16[9,80,960]{2,1,0:T(8,128)(2,1)} %bitcast.19), custom_call_target="tpu_custom_call" | custom-call | tf_op jit(solution)/shard_map/pack_weights/pallas_call | solution.py:75
  21.7 1.1 %copy-done.5 = bf16[72,80,128]{2,1,0:T(8,128)(2,1)} copy-done((bf16[72,80,128]{2,1,0:T(8,128)(2,1)}, bf16[72,80,128]{2,1,0:T(8,128)(2,1)S(1)}, u32[]{:S(2)}) %copy-start.5) | copy-done | bytes 1474584
  24.3 3.1 %collective-permute-start.7 = (bf16[12,80,128]{2,1,0:T(8,128)(2,1)S(1)}, bf16[12,80,128]{2,1,0:T(8,128)(2,1)S(1)}, u32[]{:S(2)}, u32[]{:S(2)}) collective-permute-start(bf16[12,80,128]{2,1,0:T(8,128)(2,1)S(1)} %laid.9), channel_id=1, source_target_pairs={{0,2},{2,4},{4,6},{6,0},{1,3},{3,5},{5,7},{7,1},{8,10},{10,12},{12... | collective-permute-start | bytes 737288 | tf_op jit(solution)/shard_map/ppermute | solution.py:140
  27.4 1.9 %collective-permute-start = (bf16[4,64,320]{2,1,0:T(8,128)(2,1)S(1)}, bf16[4,64,320]{2,1,0:T(8,128)(2,1)S(1)}, u32[]{:S(2)}, u32[]{:S(2)}) collective-permute-start(bf16[4,64,320]{2,1,0:T(8,128)(2,1)S(1)} %dynamic-slice_bitcast_fusion), channel_id=1, source_target_pairs={{0,2},{2,4},{4,6},{1,3},{3,5},{5,7},{8,10},{10,12},{12,14},{9,11},... | collective-permute-start | bytes 491528 | tf_op jit(solution)/shard_map/ppermute | solution.py:421
  29.3 1.3 %collective-permute-start.1 = (bf16[4,64,320]{2,1,0:T(8,128)(2,1)S(1)}, bf16[4,64,320]{2,1,0:T(8,128)(2,1)S(1)}, u32[]{:S(2)}, u32[]{:S(2)}) collective-permute-start(bf16[4,64,320]{2,1,0:T(8,128)(2,1)S(1)} %dynamic-slice_bitcast_fusion), channel_id=1, source_target_pairs={{2,0},{4,2},{6,4},{3,1},{5,3},{7,5},{10,8},{12,10},{14,12},{11,9},... | collective-permute-start | bytes 491528 | tf_op jit(solution)/shard_map/ppermute | solution.py:422
  31.0 5.7 %collective-permute-done = bf16[4,64,320]{2,1,0:T(8,128)(2,1)S(1)} collective-permute-done((bf16[4,64,320]{2,1,0:T(8,128)(2,1)S(1)}, bf16[4,64,320]{2,1,0:T(8,128)(2,1)S(1)}, u32[]{:S(2)}, u32[]{:S(2)}) %collective-permute-start) | collective-permute-done | bytes 163872 | tf_op jit(solution)/shard_map/ppermute | solution.py:421
  38.6 1.5 %collective-permute-start.9 = (bf16[12,80,128]{2,1,0:T(8,128)(2,1)S(1)}, bf16[12,80,128]{2,1,0:T(8,128)(2,1)S(1)}, u32[]{:S(2)}, u32[]{:S(2)}) collective-permute-start(bf16[12,80,128]{2,1,0:T(8,128)(2,1)S(1)} %laid.9), channel_id=1, source_target_pairs={{0,4},{2,6},{4,0},{6,2},{1,5},{3,7},{5,1},{7,3},{8,12},{10,14},{12... | collective-permute-start | bytes 737288 | tf_op jit(solution)/shard_map/ppermute | solution.py:140
  40.1 2.9 %collective-permute-start.10 = (bf16[12,80,128]{2,1,0:T(8,128)(2,1)S(1)}, bf16[12,80,128]{2,1,0:T(8,128)(2,1)S(1)}, u32[]{:S(2)}, u32[]{:S(2)}) collective-permute-start(bf16[12,80,128]{2,1,0:T(8,128)(2,1)S(1)} %laid.9), channel_id=1, source_target_pairs={{0,6},{2,0},{4,2},{6,4},{1,7},{3,1},{5,3},{7,5},{8,14},{10,8},{12,... | collective-permute-start | bytes 737288 | tf_op jit(solution)/shard_map/ppermute | solution.py:140
  43.8 4.6 %collective-permute-done.2 = bf16[12,8,320]{2,1,0:T(8,128)(2,1)S(1)} collective-permute-done((bf16[12,8,320]{2,1,0:T(8,128)(2,1)S(1)}, bf16[12,8,320]{2,1,0:T(8,128)(2,1)S(1)}, u32[]{:S(2)}, u32[]{:S(2)}) %collective-permute-start.2) | collective-permute-done | bytes 61472 | tf_op jit(solution)/shard_map/ppermute | solution.py:426
  48.4 5.2 %collective-permute-done.9.refs_1_ = bf16[12,80,128]{2,1,0:T(8,128)(2,1)S(1)} collective-permute-done((bf16[12,80,128]{2,1,0:T(8,128)(2,1)S(1)}, bf16[12,80,128]{2,1,0:T(8,128)(2,1)S(1)}, u32[]{:S(2)}, u32[]{:S(2)}) %collective-permute-start.9) | collective-permute-done | bytes 245792 | tf_op jit(solution)/shard_map/ppermute | solution.py:140
  56.9 8.3 %encoder.1 = (bf16[640,384]{1,0:T(8,128)(2,1)S(1)}, bf16[2,48,384]{2,1,0:T(8,128)(2,1)S(1)}) custom-call(s32[4]{0:T(128)S(1)} %pad_add_fusion.place, bf16[960,384]{1,0:T(8,128)(2,1)S(1)} %bitcast.13, f32[1,320]{1,0:T(1,128)S(1)} %reshape.19.bias1, f32[1,320]{1,0:T(1,128)S(1)} %reshape.20.bias2, bf16[48,80,128]{2,1,0:T(8,128)(2,1)} %get-tuple-element.30.refs_0_, ...), custom_call_target="tpu_custom_call" | custom-call | flops 21233664000 | bytes 1048576 | tf_op jit(solution)/shard_map/encoder/pallas_call | solution.py:462
  65.2 1.2 %laid.13.refs_5_ = bf16[54,80,128]{2,1,0:T(8,128)(2,1)} custom-call(bf16[27,80,128]{2,1,0:T(8,128)(2,1)S(1)} %laid.12.refs_0_, bf16[27,80,128]{2,1,0:T(8,128)(2,1)S(1)} %collective-permute-done.20.refs_1_), custom_call_target="tpu_custom_call" | custom-call | bytes 2097152 | tf_op jit(solution)/shard_map/laid/pallas_call | solution.py:127
  67.8 5.0 %collective-permute-start.13 = (bf16[2,48,384]{2,1,0:T(8,128)(2,1)S(1)}, bf16[2,48,384]{2,1,0:T(8,128)(2,1)S(1)}, u32[]{:S(2)}, u32[]{:S(2)}) collective-permute-start(bf16[2,48,384]{2,1,0:T(8,128)(2,1)S(1)} %get-tuple-element.36.own), channel_id=1, source_target_pairs={{0,2},{2,4},{4,6},{6,0},{1,3},{3,5},{5,7},{7,1},{8,10},{10,12},{12... | collective-permute-start | bytes 221192 | tf_op jit(solution)/shard_map/ppermute | solution.py:483
  72.8 1.2 %collective-permute-start.14 = (bf16[2,48,384]{2,1,0:T(8,128)(2,1)S(1)}, bf16[2,48,384]{2,1,0:T(8,128)(2,1)S(1)}, u32[]{:S(2)}, u32[]{:S(2)}) collective-permute-start(bf16[2,48,384]{2,1,0:T(8,128)(2,1)S(1)} %get-tuple-element.36.own), channel_id=1, source_target_pairs={{0,4},{2,6},{4,0},{6,2},{1,5},{3,7},{5,1},{7,3},{8,12},{10,14},{12... | collective-permute-start | bytes 221192 | tf_op jit(solution)/shard_map/ppermute | solution.py:483
  74.0 1.1 collective-permute-start.15
  76.4 2.7 %collective-permute-done.14.refs_1_ = bf16[2,48,384]{2,1,0:T(8,128)(2,1)S(1)} collective-permute-done((bf16[2,48,384]{2,1,0:T(8,128)(2,1)S(1)}, bf16[2,48,384]{2,1,0:T(8,128)(2,1)S(1)}, u32[]{:S(2)}, u32[]{:S(2)}) %collective-permute-start.14) | collective-permute-done | bytes 73760 | tf_op jit(solution)/shard_map/ppermute | solution.py:483
  79.6 2.0 %middle.1 = (bf16[4,48,256]{2,1,0:T(8,128)(2,1)S(1)}, bf16[4,48,256]{2,1,0:T(8,128)(2,1)S(1)}, bf16[4,48,256]{2,1,0:T(8,128)(2,1)S(1)}, bf16[4,48,256]{2,1,0:T(8,128)(2,1)S(1)}) custom-call(s32[4]{0:T(128)S(1)} %pad_add_fusion.place, bf16[2,48,384]{2,1,0:T(8,128)(2,1)S(1)} %get-tuple-element.36.own, bf16[2,48,384]{2,1,0:T(8,128)(2,1)S(1)} %collective-permute-done.13.refs_0_, ...), custom_call_target="tpu_custom_call" | custom-call | flops 4718592000 | bytes 1048576 | tf_op jit(solution)/shard_map/middle/pallas_call | solution.py:493
  81.6 2.2 %collective-permute-done.21.refs_6_ = bf16[54,80,128]{2,1,0:T(8,128)(2,1)} collective-permute-done((bf16[54,80,128]{2,1,0:T(8,128)(2,1)}, bf16[54,80,128]{2,1,0:T(8,128)(2,1)}, u32[]{:S(2)}, u32[]{:S(2)}) %collective-permute-start.21) | collective-permute-done | bytes 1105952 | tf_op jit(solution)/shard_map/ppermute | solution.py:441
  84.3 5.0 %collective-permute-start.17 = (bf16[4,48,256]{2,1,0:T(8,128)(2,1)S(1)}, bf16[4,48,256]{2,1,0:T(8,128)(2,1)S(1)}, u32[]{:S(2)}, u32[]{:S(2)}) collective-permute-start(bf16[4,48,256]{2,1,0:T(8,128)(2,1)S(1)} %get-tuple-element.42), channel_id=1, source_target_pairs={{0,2},{2,4},{4,6},{6,0},{1,3},{3,5},{5,7},{7,1},{8,10},{10,12},{12... | collective-permute-start | bytes 294920 | tf_op jit(solution)/shard_map/ppermute | solution.py:509
  89.3 1.2 %collective-permute-start.18 = (bf16[4,48,256]{2,1,0:T(8,128)(2,1)S(1)}, bf16[4,48,256]{2,1,0:T(8,128)(2,1)S(1)}, u32[]{:S(2)}, u32[]{:S(2)}) collective-permute-start(bf16[4,48,256]{2,1,0:T(8,128)(2,1)S(1)} %get-tuple-element.43), channel_id=1, source_target_pairs={{0,4},{2,6},{4,0},{6,2},{1,5},{3,7},{5,1},{7,3},{8,12},{10,14},{12... | collective-permute-start | bytes 294920 | tf_op jit(solution)/shard_map/ppermute | solution.py:509
  90.5 2.8 %collective-permute-done.17.refs_1_ = bf16[4,48,256]{2,1,0:T(8,128)(2,1)S(1)} collective-permute-done((bf16[4,48,256]{2,1,0:T(8,128)(2,1)S(1)}, bf16[4,48,256]{2,1,0:T(8,128)(2,1)S(1)}, u32[]{:S(2)}, u32[]{:S(2)}) %collective-permute-start.17) | collective-permute-done | bytes 98336 | tf_op jit(solution)/shard_map/ppermute | solution.py:509
  93.3 3.7 %collective-permute-start.19 = (bf16[4,48,256]{2,1,0:T(8,128)(2,1)S(1)}, bf16[4,48,256]{2,1,0:T(8,128)(2,1)S(1)}, u32[]{:S(2)}, u32[]{:S(2)}) collective-permute-start(bf16[4,48,256]{2,1,0:T(8,128)(2,1)S(1)} %get-tuple-element.44), channel_id=1, source_target_pairs={{0,6},{2,0},{4,2},{6,4},{1,7},{3,1},{5,3},{7,5},{8,14},{10,8},{12,... | collective-permute-start | bytes 294920 | tf_op jit(solution)/shard_map/ppermute | solution.py:509
  98.0 2.0 %collective-permute-done.19.refs_3_ = bf16[4,48,256]{2,1,0:T(8,128)(2,1)S(1)} collective-permute-done((bf16[4,48,256]{2,1,0:T(8,128)(2,1)S(1)}, bf16[4,48,256]{2,1,0:T(8,128)(2,1)S(1)}, u32[]{:S(2)}, u32[]{:S(2)}) %collective-permute-start.19) | collective-permute-done | bytes 98336 | tf_op jit(solution)/shard_map/ppermute | solution.py:509
  101.4 8.6 %joined.1.refined = bf16[480,384]{1,0:T(8,128)(2,1)S(1)} custom-call(s32[4]{0:T(128)S(1)} %pad_add_fusion.place, bf16[640,384]{1,0:T(8,128)(2,1)S(1)} %get-tuple-element.35.skip, f32[1,320]{1,0:T(1,128)S(1)} %reshape.21.bias, bf16[4,48,256]{2,1,0:T(8,128)(2,1)S(1)} %get-tuple-element.41.refs_0_, bf16[4,48,256]{2,1,0:T(8,128)(2,1)S(1)} %collective-permute-done.17.refs_1_, ...), custom_call_target="tpu_custom_call" | custom-call | flops 10616832000 | bytes 1048576 | tf_op jit(solution)/shard_map/joined/pallas_call | solution.py:538
  110.1 3.5 %last.1 = bf16[1,4,64,320]{3,2,1,0:T(8,128)(2,1)} custom-call(s32[4]{0:T(128)S(1)} %pad_add_fusion.place, bf16[480,384]{1,0:T(8,128)(2,1)S(1)} %joined.1.refined, f32[1,320]{1,0:T(1,128)S(1)} %reshape.23.bias, bf16[24,80,128]{2,1,0:T(8,128)(2,1)} %copy-done.7, bf16[18,80,128]{2,1,0:T(8,128)(2,1)S(1)} %laid.11.refs_1_, ...), custom_call_target="tpu_custom_call" | custom-call | flops 2359296000 | bytes 1048576 | tf_op jit(solution)/shard_map/last/pallas_call | solution.py:555
  (81 shorter events, 16.3 us)
Async XLA Ops:
  0.0 27.4 %copy-start = (bf16[2,4,64,320]{3,2,1,0:T(8,128)(2,1)S(1)}, bf16[2,4,64,320]{3,2,1,0:T(8,128)(2,1)}, u32[]{:S(2)}) copy-start(bf16[2,4,64,320]{3,2,1,0:T(8,128)(2,1)} %param.11) | copy-start | bytes 983044
  2.2 20.6 %copy-start.2 = (bf16[9,320,80]{1,2,0:T(8,128)(2,1)S(1)}, bf16[9,320,80]{1,2,0:T(8,128)(2,1)}, u32[]{:S(2)}) copy-start(bf16[9,320,80]{1,2,0:T(8,128)(2,1)} %param.20) | copy-start | bytes 1382404
  3.9 9.3 %collective-permute-start.3 = (bf16[6,80,128]{2,1,0:T(8,128)(2,1)S(1)}, bf16[6,80,128]{2,1,0:T(8,128)(2,1)S(1)}, u32[]{:S(2)}, u32[]{:S(2)}) collective-permute-start(bf16[6,80,128]{2,1,0:T(8,128)(2,1)S(1)} %get-tuple-element.28), channel_id=1, source_target_pairs={{0,2},{2,4},{4,6},{6,0},{1,3},{3,5},{5,7},{7,1},{8,10},{10,12},{12... | collective-permute-start | bytes 368648 | tf_op jit(solution)/shard_map/ppermute | solution.py:140
  6.9 10.7 %collective-permute-start.4 = (bf16[6,80,128]{2,1,0:T(8,128)(2,1)S(1)}, bf16[6,80,128]{2,1,0:T(8,128)(2,1)S(1)}, u32[]{:S(2)}, u32[]{:S(2)}) collective-permute-start(bf16[6,80,128]{2,1,0:T(8,128)(2,1)S(1)} %get-tuple-element.28), channel_id=1, source_target_pairs={{0,4},{2,6},{4,0},{6,2},{1,5},{3,7},{5,1},{7,3},{8,12},{10,14},{12... | collective-permute-start | bytes 368648 | tf_op jit(solution)/shard_map/ppermute | solution.py:140
  9.5 8.1 %collective-permute-start.5 = (bf16[6,80,128]{2,1,0:T(8,128)(2,1)S(1)}, bf16[6,80,128]{2,1,0:T(8,128)(2,1)S(1)}, u32[]{:S(2)}, u32[]{:S(2)}) collective-permute-start(bf16[6,80,128]{2,1,0:T(8,128)(2,1)S(1)} %get-tuple-element.28), channel_id=1, source_target_pairs={{0,6},{2,0},{4,2},{6,4},{1,7},{3,1},{5,3},{7,5},{8,14},{10,8},{12,... | collective-permute-start | bytes 368648 | tf_op jit(solution)/shard_map/ppermute | solution.py:140
  18.1 12.5 %collective-permute-start.6 = (bf16[18,80,128]{2,1,0:T(8,128)(2,1)S(1)}, bf16[18,80,128]{2,1,0:T(8,128)(2,1)S(1)}, u32[]{:S(2)}, u32[]{:S(2)}) collective-permute-start(bf16[18,80,128]{2,1,0:T(8,128)(2,1)S(1)} %laid.7.refs_0_), channel_id=1, source_target_pairs={{0,1},{1,0},{2,3},{3,2},{4,5},{5,4},{6,7},{7,6},{8,24},{9,25},{10,... | collective-permute-start | bytes 1105928 | tf_op jit(solution)/shard_map/ppermute | solution.py:441
  24.3 13.5 %collective-permute-start.7 = (bf16[12,80,128]{2,1,0:T(8,128)(2,1)S(1)}, bf16[12,80,128]{2,1,0:T(8,128)(2,1)S(1)}, u32[]{:S(2)}, u32[]{:S(2)}) collective-permute-start(bf16[12,80,128]{2,1,0:T(8,128)(2,1)S(1)} %laid.9), channel_id=1, source_target_pairs={{0,2},{2,4},{4,6},{6,0},{1,3},{3,5},{5,7},{7,1},{8,10},{10,12},{12... | collective-permute-start | bytes 737288 | tf_op jit(solution)/shard_map/ppermute | solution.py:140
  27.4 26.2 %copy-start.8 = (f32[320]{0:T(512)S(1)}, f32[320]{0:T(512)}, u32[]{:S(2)}) copy-start(f32[320]{0:T(512)} %param.13) | copy-start | bytes 3844
  27.4 26.2 %copy-start.9 = (f32[320]{0:T(512)S(1)}, f32[320]{0:T(512)}, u32[]{:S(2)}) copy-start(f32[320]{0:T(512)} %param.15) | copy-start | bytes 3844
  27.4 9.3 %collective-permute-start = (bf16[4,64,320]{2,1,0:T(8,128)(2,1)S(1)}, bf16[4,64,320]{2,1,0:T(8,128)(2,1)S(1)}, u32[]{:S(2)}, u32[]{:S(2)}) collective-permute-start(bf16[4,64,320]{2,1,0:T(8,128)(2,1)S(1)} %dynamic-slice_bitcast_fusion), channel_id=1, source_target_pairs={{0,2},{2,4},{4,6},{1,3},{3,5},{5,7},{8,10},{10,12},{12,14},{9,11},... | collective-permute-start | bytes 491528 | tf_op jit(solution)/shard_map/ppermute | solution.py:421
  29.3 8.5 %collective-permute-start.1 = (bf16[4,64,320]{2,1,0:T(8,128)(2,1)S(1)}, bf16[4,64,320]{2,1,0:T(8,128)(2,1)S(1)}, u32[]{:S(2)}, u32[]{:S(2)}) collective-permute-start(bf16[4,64,320]{2,1,0:T(8,128)(2,1)S(1)} %dynamic-slice_bitcast_fusion), channel_id=1, source_target_pairs={{2,0},{4,2},{6,4},{3,1},{5,3},{7,5},{10,8},{12,10},{14,12},{11,9},... | collective-permute-start | bytes 491528 | tf_op jit(solution)/shard_map/ppermute | solution.py:422
  31.0 22.9 %copy-start.1 = (bf16[36,80,128]{2,1,0:T(8,128)(2,1)}, bf16[36,80,128]{2,1,0:T(8,128)(2,1)S(1)}, u32[]{:S(2)}) copy-start(bf16[36,80,128]{2,1,0:T(8,128)(2,1)S(1)} %laid.8.refs_1_) | copy-start | bytes 2211844
  37.8 15.8 %collective-permute-start.8 = (bf16[36,80,128]{2,1,0:T(8,128)(2,1)S(1)}, bf16[36,80,128]{2,1,0:T(8,128)(2,1)}, u32[]{:S(2)}, u32[]{:S(2)}) collective-permute-start(bf16[36,80,128]{2,1,0:T(8,128)(2,1)S(1)} %laid.8.refs_1_), channel_id=1, source_target_pairs={{0,16},{1,17},{2,18},{3,19},{4,20},{5,21},{6,22},{7,23},{8,9},{9,8... | collective-permute-start | bytes 2211848 | tf_op jit(solution)/shard_map/ppermute | solution.py:441
  38.6 15.0 %collective-permute-start.9 = (bf16[12,80,128]{2,1,0:T(8,128)(2,1)S(1)}, bf16[12,80,128]{2,1,0:T(8,128)(2,1)S(1)}, u32[]{:S(2)}, u32[]{:S(2)}) collective-permute-start(bf16[12,80,128]{2,1,0:T(8,128)(2,1)S(1)} %laid.9), channel_id=1, source_target_pairs={{0,4},{2,6},{4,0},{6,2},{1,5},{3,7},{5,1},{7,3},{8,12},{10,14},{12... | collective-permute-start | bytes 737288 | tf_op jit(solution)/shard_map/ppermute | solution.py:140
  40.1 13.5 %collective-permute-start.10 = (bf16[12,80,128]{2,1,0:T(8,128)(2,1)S(1)}, bf16[12,80,128]{2,1,0:T(8,128)(2,1)S(1)}, u32[]{:S(2)}, u32[]{:S(2)}) collective-permute-start(bf16[12,80,128]{2,1,0:T(8,128)(2,1)S(1)} %laid.9), channel_id=1, source_target_pairs={{0,6},{2,0},{4,2},{6,4},{1,7},{3,1},{5,3},{7,5},{8,14},{10,8},{12,... | collective-permute-start | bytes 737288 | tf_op jit(solution)/shard_map/ppermute | solution.py:140
  43.1 5.3 %collective-permute-start.2 = (bf16[12,8,320]{2,1,0:T(8,128)(2,1)S(1)}, bf16[12,8,320]{2,1,0:T(8,128)(2,1)S(1)}, u32[]{:S(2)}, u32[]{:S(2)}) collective-permute-start(bf16[12,8,320]{2,1,0:T(8,128)(2,1)S(1)} %slice_select_fusion), channel_id=1, source_target_pairs={{0,1},{1,0},{2,3},{3,2},{4,5},{5,4},{6,7},{7,6},{8,9},{9,8},{10,11... | collective-permute-start | bytes 184328 | tf_op jit(solution)/shard_map/ppermute | solution.py:426
  43.8 11.6 %collective-permute-start.11 = (bf16[36,80,128]{2,1,0:T(8,128)(2,1)S(1)}, bf16[36,80,128]{2,1,0:T(8,128)(2,1)S(1)}, u32[]{:S(2)}, u32[]{:S(2)}) collective-permute-start(bf16[36,80,128]{2,1,0:T(8,128)(2,1)S(1)} %laid.8.refs_1_), channel_id=1, source_target_pairs={{0,8},{8,0},{1,9},{9,1},{2,10},{10,2},{3,11},{11,3},{4,12},{12,4},... | collective-permute-start | bytes 2211848 | tf_op jit(solution)/shard_map/ppermute | solution.py:154
  53.6 2.4 %collective-permute-start.12 = (bf16[36,80,128]{2,1,0:T(8,128)(2,1)}, bf16[36,80,128]{2,1,0:T(8,128)(2,1)S(1)}, u32[]{:S(2)}, u32[]{:S(2)}) collective-permute-start(bf16[36,80,128]{2,1,0:T(8,128)(2,1)} %collective-permute-done.8.refs_2_), channel_id=1, source_target_pairs={{0,8},{8,0},{1,9},{9,1},{2,10},{10,2},{3,11},{11,3},{4,12},{12,4},... | collective-permute-start | bytes 2211848 | tf_op jit(solution)/shard_map/ppermute | solution.py:154
  54.6 10.6 %collective-permute-start.20 = (bf16[27,80,128]{2,1,0:T(8,128)(2,1)S(1)}, bf16[27,80,128]{2,1,0:T(8,128)(2,1)S(1)}, u32[]{:S(2)}, u32[]{:S(2)}) collective-permute-start(bf16[27,80,128]{2,1,0:T(8,128)(2,1)S(1)} %laid.12.refs_0_), channel_id=1, source_target_pairs={{0,1},{1,0},{2,3},{3,2},{4,5},{5,4},{6,7},{7,6},{8,24},{9,25},{10,... | collective-permute-start | bytes 1658888 | tf_op jit(solution)/shard_map/ppermute | solution.py:441
  66.4 17.4 %collective-permute-start.21 = (bf16[54,80,128]{2,1,0:T(8,128)(2,1)}, bf16[54,80,128]{2,1,0:T(8,128)(2,1)}, u32[]{:S(2)}, u32[]{:S(2)}) collective-permute-start(bf16[54,80,128]{2,1,0:T(8,128)(2,1)} %laid.13.refs_5_), channel_id=1, source_target_pairs={{0,16},{1,17},{2,18},{3,19},{4,20},{5,21},{6,22},{7,23},{8,9},{9,8... | collective-permute-start | bytes 3317768 | tf_op jit(solution)/shard_map/ppermute | solution.py:441
  66.7 9.2 %collective-permute-start.16 = (bf16[9,80,128]{2,1,0:T(8,128)(2,1)S(1)}, bf16[9,80,128]{2,1,0:T(8,128)(2,1)S(1)}, u32[]{:S(2)}, u32[]{:S(2)}) collective-permute-start(bf16[9,80,128]{2,1,0:T(8,128)(2,1)S(1)} %laid.10.refs_0_), channel_id=1, source_target_pairs={{0,1},{1,0},{2,3},{3,2},{4,5},{5,4},{6,7},{7,6},{8,24},{9,25},{10,... | collective-permute-start | bytes 552968 | tf_op jit(solution)/shard_map/ppermute | solution.py:441
  67.8 8.7 %collective-permute-start.13 = (bf16[2,48,384]{2,1,0:T(8,128)(2,1)S(1)}, bf16[2,48,384]{2,1,0:T(8,128)(2,1)S(1)}, u32[]{:S(2)}, u32[]{:S(2)}) collective-permute-start(bf16[2,48,384]{2,1,0:T(8,128)(2,1)S(1)} %get-tuple-element.36.own), channel_id=1, source_target_pairs={{0,2},{2,4},{4,6},{6,0},{1,3},{3,5},{5,7},{7,1},{8,10},{10,12},{12... | collective-permute-start | bytes 221192 | tf_op jit(solution)/shard_map/ppermute | solution.py:483
  72.8 6.4 %collective-permute-start.14 = (bf16[2,48,384]{2,1,0:T(8,128)(2,1)S(1)}, bf16[2,48,384]{2,1,0:T(8,128)(2,1)S(1)}, u32[]{:S(2)}, u32[]{:S(2)}) collective-permute-start(bf16[2,48,384]{2,1,0:T(8,128)(2,1)S(1)} %get-tuple-element.36.own), channel_id=1, source_target_pairs={{0,4},{2,6},{4,0},{6,2},{1,5},{3,7},{5,1},{7,3},{8,12},{10,14},{12... | collective-permute-start | bytes 221192 | tf_op jit(solution)/shard_map/ppermute | solution.py:483
  74.0 5.6 %collective-permute-start.15 = (bf16[2,48,384]{2,1,0:T(8,128)(2,1)S(1)}, bf16[2,48,384]{2,1,0:T(8,128)(2,1)S(1)}, u32[]{:S(2)}, u32[]{:S(2)}) collective-permute-start(bf16[2,48,384]{2,1,0:T(8,128)(2,1)S(1)} %get-tuple-element.36.own), channel_id=1, source_target_pairs={{0,6},{2,0},{4,2},{6,4},{1,7},{3,1},{5,3},{7,5},{8,14},{10,8},{12,... | collective-permute-start | bytes 221192 | tf_op jit(solution)/shard_map/ppermute | solution.py:483
  75.9 24.1 %collective-permute-start.22 = (bf16[54,80,128]{2,1,0:T(8,128)(2,1)}, bf16[54,80,128]{2,1,0:T(8,128)(2,1)S(1)}, u32[]{:S(2)}, u32[]{:S(2)}) collective-permute-start(bf16[54,80,128]{2,1,0:T(8,128)(2,1)} %laid.13.refs_5_), channel_id=1, source_target_pairs={{0,8},{8,0},{1,9},{9,1},{2,10},{10,2},{3,11},{11,3},{4,12},{12,4},... | collective-permute-start | bytes 3317768 | tf_op jit(solution)/shard_map/ppermute | solution.py:154
  83.8 16.2 %collective-permute-start.23 = (bf16[54,80,128]{2,1,0:T(8,128)(2,1)}, bf16[54,80,128]{2,1,0:T(8,128)(2,1)S(1)}, u32[]{:S(2)}, u32[]{:S(2)}) collective-permute-start(bf16[54,80,128]{2,1,0:T(8,128)(2,1)} %collective-permute-done.21.refs_6_), channel_id=1, source_target_pairs={{0,8},{8,0},{1,9},{9,1},{2,10},{10,2},{3,11},{11,3},{4,12},{12,4},... | collective-permute-start | bytes 3317768 | tf_op jit(solution)/shard_map/ppermute | solution.py:154
  83.8 16.1 %collective-permute-start.24 = (bf16[18,80,128]{2,1,0:T(8,128)(2,1)S(1)}, bf16[18,80,128]{2,1,0:T(8,128)(2,1)S(1)}, u32[]{:S(2)}, u32[]{:S(2)}) collective-permute-start(bf16[18,80,128]{2,1,0:T(8,128)(2,1)S(1)} %laid.11.refs_1_), channel_id=1, source_target_pairs={{0,16},{1,17},{2,18},{3,19},{4,20},{5,21},{6,22},{7,23},{8,9},{9,8... | collective-permute-start | bytes 1105928 | tf_op jit(solution)/shard_map/ppermute | solution.py:441
  84.3 9.1 %collective-permute-start.17 = (bf16[4,48,256]{2,1,0:T(8,128)(2,1)S(1)}, bf16[4,48,256]{2,1,0:T(8,128)(2,1)S(1)}, u32[]{:S(2)}, u32[]{:S(2)}) collective-permute-start(bf16[4,48,256]{2,1,0:T(8,128)(2,1)S(1)} %get-tuple-element.42), channel_id=1, source_target_pairs={{0,2},{2,4},{4,6},{6,0},{1,3},{3,5},{5,7},{7,1},{8,10},{10,12},{12... | collective-permute-start | bytes 294920 | tf_op jit(solution)/shard_map/ppermute | solution.py:509
  89.3 8.6 %collective-permute-start.18 = (bf16[4,48,256]{2,1,0:T(8,128)(2,1)S(1)}, bf16[4,48,256]{2,1,0:T(8,128)(2,1)S(1)}, u32[]{:S(2)}, u32[]{:S(2)}) collective-permute-start(bf16[4,48,256]{2,1,0:T(8,128)(2,1)S(1)} %get-tuple-element.43), channel_id=1, source_target_pairs={{0,4},{2,6},{4,0},{6,2},{1,5},{3,7},{5,1},{7,3},{8,12},{10,14},{12... | collective-permute-start | bytes 294920 | tf_op jit(solution)/shard_map/ppermute | solution.py:509
  93.3 6.6 %collective-permute-start.19 = (bf16[4,48,256]{2,1,0:T(8,128)(2,1)S(1)}, bf16[4,48,256]{2,1,0:T(8,128)(2,1)S(1)}, u32[]{:S(2)}, u32[]{:S(2)}) collective-permute-start(bf16[4,48,256]{2,1,0:T(8,128)(2,1)S(1)} %get-tuple-element.44), channel_id=1, source_target_pairs={{0,6},{2,0},{4,2},{6,4},{1,7},{3,1},{5,3},{7,5},{8,14},{10,8},{12,... | collective-permute-start | bytes 294920 | tf_op jit(solution)/shard_map/ppermute | solution.py:509
  97.9 12.1 %collective-permute-start.25 = (bf16[18,80,128]{2,1,0:T(8,128)(2,1)S(1)}, bf16[18,80,128]{2,1,0:T(8,128)(2,1)S(1)}, u32[]{:S(2)}, u32[]{:S(2)}) collective-permute-start(bf16[18,80,128]{2,1,0:T(8,128)(2,1)S(1)} %laid.11.refs_1_), channel_id=1, source_target_pairs={{0,8},{8,0},{1,9},{9,1},{2,10},{10,2},{3,11},{11,3},{4,12},{12,4},... | collective-permute-start | bytes 1105928 | tf_op jit(solution)/shard_map/ppermute | solution.py:154
  100.0 10.1 %collective-permute-start.26 = (bf16[18,80,128]{2,1,0:T(8,128)(2,1)S(1)}, bf16[18,80,128]{2,1,0:T(8,128)(2,1)S(1)}, u32[]{:S(2)}, u32[]{:S(2)}) collective-permute-start(bf16[18,80,128]{2,1,0:T(8,128)(2,1)S(1)} %collective-permute-done.24.refs_2_), channel_id=1, source_target_pairs={{0,8},{8,0},{1,9},{9,1},{2,10},{10,2},{3,11},{11,3},{4,12},{12,4},... | collective-permute-start | bytes 1105928 | tf_op jit(solution)/shard_map/ppermute | solution.py:154
  (11 other events, 57.6 us)

commit v3 on v2

--- a/solution.py
+++ b/solution.py
@@ -323,18 +323,8 @@
         outs[by][...] = result[pl.ds(tall * at, tall + 2)]
 
 
-def joined_body(size, sets, parts, place, skip, bias, *refs):
-    tile_rows, tile_cols = size[:2]
-    wide = tile_cols + 2 * SIDE
-    mids, refs = refs[:SHARDS], refs[SHARDS:]
-    sources, refs = refs[:sets], refs[sets:]
-    out, weights, shifted, raised, field, acc, sem = refs
-    copies = load_weights(place, parts, sources, weights, sem)
-    for copy in copies:
-        copy.start()
-    spread(skip[...].astype(F32), shifted)
-    half = mids[0].shape[1]
-    tall = tile_rows // 2 + 2
+def field_body(sets, place, *refs):
+    mids, field = refs[:SHARDS], refs[SHARDS]
     tail = mids[0][:, :, LANES:]
     for mid in mids[1:]:
         tail = tail + mid[:, :, LANES:]
@@ -342,6 +332,20 @@
     for by in range(SHARDS):
         shard = lax.rem(place[2] - by + SHARDS, SHARDS) if sets > 1 else by
         field[shard] = mids[by][:, :, :LANES]
+
+
+def joined_body(size, sets, parts, place, skip, bias, *refs):
+    tile_rows, tile_cols = size[:2]
+    wide = tile_cols + 2 * SIDE
+    field, refs = refs[0], refs[1:]
+    sources, refs = refs[:sets], refs[sets:]
+    out, weights, shifted, raised, acc, sem = refs
+    copies = load_weights(place, parts, sources, weights, sem)
+    for copy in copies:
+        copy.start()
+    spread(skip[...].astype(F32), shifted)
+    half = field.shape[2]
+    tall = tile_rows // 2 + 2
     cell = lax.broadcasted_iota(jnp.int32, (3 * wide, half), 0)
     move = jnp.where(cell >= 2 * wide, 1 - 2 * wide, jnp.where(cell >= wide, -wide, -1))
     source = lax.broadcasted_iota(jnp.int32, (3 * wide, half), 1)
@@ -440,8 +444,9 @@
         first, second = plane_moves(mesh_shape)
         across = lambda block, pairs: lax.ppermute(block, AXES, pairs)
         here0 = from_planes(mine0, row_count)
-        here1 = from_planes(laid(mine1, mine2), row_count)
-        block0 = laid(*here0)
+        late = laid(mine1, mine2)
+        here1 = from_planes(late, row_count)
+        block0 = laid(*after(here0, late))
         block0 = laid(block0, across(block0, first))
         block0 = after(block0, here1[0], above, below)
         far0 = swap_cores(block0)
@@ -510,7 +515,7 @@
         ]
         next1 = after(next1, sent[0])
         held1 = (block1, next1, far1, swap_cores(next1))
-        next2 = after(across(after(block2, sent[0]), second), *mids)
+        next2 = after(across(block2, second), *mids)
         held2 = (block2, next2, swap_cores(block2), swap_cores(next2))
         weights += [(own1,) + held1, (own2,) + held2]
     else:
@@ -535,23 +540,31 @@
             tail = jnp.pad(block[:, :, LANES:], ((0, 0), (0, 0), (32 * shard, 96 - 32 * shard)))
             mids.append(jnp.concatenate([block[:, :, :LANES], tail], axis=2))
 
+    field = pl.pallas_call(
+        functools.partial(field_body, sets),
+        out_shape=jax.ShapeDtypeStruct((5, tall + 2, half, LANES), BF),
+        in_specs=[SMEM] + [VMEM] * SHARDS,
+        out_specs=VMEM,
+        compiler_params=params(),
+        cost_estimate=cost(40 * tile_rows * wide),
+        name="field",
+    )(place, *mids)
     refined = pl.pallas_call(
         functools.partial(joined_body, size, sets, groups[1][1]),
         out_shape=jax.ShapeDtypeStruct(((tile_rows + 2) * wide, 3 * LANES), BF),
-        in_specs=[SMEM, VMEM, VMEM] + [VMEM] * SHARDS + [HBM] * sets,
+        in_specs=[SMEM, VMEM, VMEM, VMEM] + [HBM] * sets,
         out_specs=VMEM,
         scratch_shapes=[
             packed(weights[1]),
             scratch(3, (tile_rows + 4) * wide, 3 * LANES),
             scratch(3, (tile_rows + 4) * wide, 5 * LANES),
-            scratch(5, tall + 2, half, LANES),
             pltpu.VMEM(((tile_rows + 2) * wide, channels), F32),
             pltpu.SemaphoreType.DMA,
         ],
         compiler_params=params(),
         cost_estimate=cost(6 * (tile_rows + 2) * wide),
         name="joined",
-    )(place, skip, lines(dec_first_bias), *mids, *weights[1])
+    )(place, skip, lines(dec_first_bias), field, *weights[1])
     return pl.pallas_call(
         functools.partial(last_body, size, sets, groups[2][1]),
         out_shape=jax.ShapeDtypeStruct((1, tile_rows, tile_cols, channels), BF),

time: 114 us -> 104 us (0.912)
  waiting for transfers between devices: 35.1 us -> 30 us
  starting transfers between devices: 40.4 us -> 35.6 us
    ppermute x3, starting transfers between devices: 10 us -> 3.98 us  [shards(): lax.ppermute(sent[by], 'row', cyclic(row_count, by))]
    ppermute x6, waiting for transfers between devices: 12 us -> 7.81 us  [from_planes(): lax.ppermute(mine, 'row', cyclic(count, by))]
    ppermute x6, waiting for transfers between devices: 2.23 us -> 0.85 us  [shards(): across = lambda block, pairs: lax.ppermute(block, AXES, pairs)]
    ppermute x6, waiting for transfers between devices: 0.66 us -> 1.92 us  [swap_cores(): return lax.ppermute(block, 'segment', [(0, 1), (1, 0)])]
    ppermute x6, starting transfers between devices: 4.64 us -> 5.87 us  [shards(): across = lambda block, pairs: lax.ppermute(block, AXES, pairs)]
    unnamed x34 -> x38, local copies, waits for them, and re-layouts: 6.1 us -> 5.38 us
  transfers between devices with their start and end apart: 27 -> 27, of which waited for: 13 -> 12; matrix products, arithmetic and copies ran while one was open for 1% -> 1% of each run, Pallas kernels for 21% -> 23%
where the time goes in v3:
time: 104 us
  starting transfers between devices  35.6 us (34%)
  Pallas kernels  31.1 us (30%)
  waiting for transfers between devices  30 us (29%)
  local copies, waits for them, and re-layouts  6.2 us (6%)
    ppermute x6, starting transfers between devices, from_planes(): lax.ppermute(mine, 'row', cyclic(count, by))  14.4 us
    pallas_call x1, Pallas kernels, shards(): pl.pallas_call(functools.partial(joined_body, size, sets, groups[1][1]),...  8.64 us
    pallas_call x1, Pallas kernels, shards(): pl.pallas_call(functools.partial(encoder_body, size, sets, groups[0][1]),...  8.26 us
    ppermute x6, waiting for transfers between devices, from_planes(): lax.ppermute(mine, 'row', cyclic(count, by))  7.81 us
    ppermute x3, starting transfers between devices, shards(): lax.ppermute(pooled, 'row', cyclic(row_count, by))  7.32 us
    ppermute x6, starting transfers between devices, shards(): across = lambda block, pairs: lax.ppermute(block, AXES, pairs)  5.87 us
    ppermute x1, waiting for transfers between devices, shards(): above = lax.ppermute(tile, 'row', down)  5.71 us
    unnamed x38, local copies, waits for them, and re-layouts  5.38 us
  transfers between devices with their start and end apart: 27, of which 12 were waited for; matrix products, arithmetic and copies ran while one was open for 1% of the time, Pallas kernels for 23%

profile of v3, /device:TPU:0, one launch (start us, length us, event | category | flops | bytes accessed | tf_op | source)
XLA Modules:
  0.0 103.7 jit_solution(11341583567331135484)
XLA Ops:
  0.1 1.1 %copy-done.3 = bf16[9,320,80]{1,2,0:T(8,128)(2,1)S(1)} copy-done((bf16[9,320,80]{1,2,0:T(8,128)(2,1)S(1)}, bf16[9,320,80]{1,2,0:T(8,128)(2,1)}, u32[]{:S(2)}) %copy-start.3) | copy-done | bytes 460824
  2.3 1.7 %pack_weights.3 = (bf16[48,80,128]{2,1,0:T(8,128)(2,1)}, bf16[6,80,128]{2,1,0:T(8,128)(2,1)S(1)}) custom-call(s32[4]{0:T(128)S(1)} %pad_add_fusion.place, bf16[9,80,320]{2,1,0:T(8,128)(2,1)S(1)} %bitcast.15, bf16[9,80,320]{2,1,0:T(8,128)(2,1)S(1)} %bitcast.16), custom_call_target="tpu_custom_call" | custom-call | tf_op jit(solution)/shard_map/pack_weights/pallas_call | solution.py:75
  4.0 3.0 %collective-permute-start.3 = (bf16[6,80,128]{2,1,0:T(8,128)(2,1)S(1)}, bf16[6,80,128]{2,1,0:T(8,128)(2,1)S(1)}, u32[]{:S(2)}, u32[]{:S(2)}) collective-permute-start(bf16[6,80,128]{2,1,0:T(8,128)(2,1)S(1)} %get-tuple-element.30), channel_id=1, source_target_pairs={{0,2},{2,4},{4,6},{6,0},{1,3},{3,5},{5,7},{7,1},{8,10},{10,12},{12... | collective-permute-start | bytes 368648 | tf_op jit(solution)/shard_map/ppermute | solution.py:140
  7.0 2.6 %collective-permute-start.4 = (bf16[6,80,128]{2,1,0:T(8,128)(2,1)S(1)}, bf16[6,80,128]{2,1,0:T(8,128)(2,1)S(1)}, u32[]{:S(2)}, u32[]{:S(2)}) collective-permute-start(bf16[6,80,128]{2,1,0:T(8,128)(2,1)S(1)} %get-tuple-element.30), channel_id=1, source_target_pairs={{0,4},{2,6},{4,0},{6,2},{1,5},{3,7},{5,1},{7,3},{8,12},{10,14},{12... | collective-permute-start | bytes 368648 | tf_op jit(solution)/shard_map/ppermute | solution.py:140
  9.6 1.3 %collective-permute-start.5 = (bf16[6,80,128]{2,1,0:T(8,128)(2,1)S(1)}, bf16[6,80,128]{2,1,0:T(8,128)(2,1)S(1)}, u32[]{:S(2)}, u32[]{:S(2)}) collective-permute-start(bf16[6,80,128]{2,1,0:T(8,128)(2,1)S(1)} %get-tuple-element.30), channel_id=1, source_target_pairs={{0,6},{2,0},{4,2},{6,4},{1,7},{3,1},{5,3},{7,5},{8,14},{10,8},{12,... | collective-permute-start | bytes 368648 | tf_op jit(solution)/shard_map/ppermute | solution.py:140
  10.9 2.0 %pack_weights.4 = (bf16[72,80,128]{2,1,0:T(8,128)(2,1)S(1)}, bf16[9,80,128]{2,1,0:T(8,128)(2,1)S(1)}) custom-call(s32[4]{0:T(128)S(1)} %pad_add_fusion.place, bf16[9,80,960]{2,1,0:T(8,128)(2,1)} %bitcast.19), custom_call_target="tpu_custom_call" | custom-call | tf_op jit(solution)/shard_map/pack_weights/pallas_call | solution.py:75
  12.9 1.1 %copy-done.5 = bf16[72,80,128]{2,1,0:T(8,128)(2,1)} copy-done((bf16[72,80,128]{2,1,0:T(8,128)(2,1)}, bf16[72,80,128]{2,1,0:T(8,128)(2,1)S(1)}, u32[]{:S(2)}) %copy-start.5) | copy-done | bytes 1474584
  15.1 2.6 %collective-permute-done.4.refs_1_ = bf16[6,80,128]{2,1,0:T(8,128)(2,1)S(1)} collective-permute-done((bf16[6,80,128]{2,1,0:T(8,128)(2,1)S(1)}, bf16[6,80,128]{2,1,0:T(8,128)(2,1)S(1)}, u32[]{:S(2)}, u32[]{:S(2)}) %collective-permute-start.4) | collective-permute-done | bytes 122912 | tf_op jit(solution)/shard_map/ppermute | solution.py:140
  18.2 1.6 %collective-permute-start.6 = (bf16[18,80,128]{2,1,0:T(8,128)(2,1)S(1)}, bf16[18,80,128]{2,1,0:T(8,128)(2,1)S(1)}, u32[]{:S(2)}, u32[]{:S(2)}) collective-permute-start(bf16[18,80,128]{2,1,0:T(8,128)(2,1)S(1)} %laid.8.refs_0_), channel_id=1, source_target_pairs={{0,1},{1,0},{2,3},{3,2},{4,5},{5,4},{6,7},{7,6},{8,24},{9,25},{10,... | collective-permute-start | bytes 1105928 | tf_op jit(solution)/shard_map/ppermute | solution.py:445
  19.7 3.1 %collective-permute-start.7 = (bf16[12,80,128]{2,1,0:T(8,128)(2,1)S(1)}, bf16[12,80,128]{2,1,0:T(8,128)(2,1)S(1)}, u32[]{:S(2)}, u32[]{:S(2)}) collective-permute-start(bf16[12,80,128]{2,1,0:T(8,128)(2,1)S(1)} %laid.7), channel_id=1, source_target_pairs={{0,2},{2,4},{4,6},{6,0},{1,3},{3,5},{5,7},{7,1},{8,10},{10,12},{12... | collective-permute-start | bytes 737288 | tf_op jit(solution)/shard_map/ppermute | solution.py:140
  22.9 1.9 %collective-permute-start = (bf16[4,64,320]{2,1,0:T(8,128)(2,1)S(1)}, bf16[4,64,320]{2,1,0:T(8,128)(2,1)S(1)}, u32[]{:S(2)}, u32[]{:S(2)}) collective-permute-start(bf16[4,64,320]{2,1,0:T(8,128)(2,1)S(1)} %dynamic-slice_bitcast_fusion), channel_id=1, source_target_pairs={{0,2},{2,4},{4,6},{1,3},{3,5},{5,7},{8,10},{10,12},{12,14},{9,11},... | collective-permute-start | bytes 491528 | tf_op jit(solution)/shard_map/ppermute | solution.py:425
  24.8 1.3 %collective-permute-start.1 = (bf16[4,64,320]{2,1,0:T(8,128)(2,1)S(1)}, bf16[4,64,320]{2,1,0:T(8,128)(2,1)S(1)}, u32[]{:S(2)}, u32[]{:S(2)}) collective-permute-start(bf16[4,64,320]{2,1,0:T(8,128)(2,1)S(1)} %dynamic-slice_bitcast_fusion), channel_id=1, source_target_pairs={{2,0},{4,2},{6,4},{3,1},{5,3},{7,5},{10,8},{12,10},{14,12},{11,9},... | collective-permute-start | bytes 491528 | tf_op jit(solution)/shard_map/ppermute | solution.py:426
  26.5 5.7 %collective-permute-done = bf16[4,64,320]{2,1,0:T(8,128)(2,1)S(1)} collective-permute-done((bf16[4,64,320]{2,1,0:T(8,128)(2,1)S(1)}, bf16[4,64,320]{2,1,0:T(8,128)(2,1)S(1)}, u32[]{:S(2)}, u32[]{:S(2)}) %collective-permute-start) | collective-permute-done | bytes 163872 | tf_op jit(solution)/shard_map/ppermute | solution.py:425
  34.1 1.5 %collective-permute-start.9 = (bf16[12,80,128]{2,1,0:T(8,128)(2,1)S(1)}, bf16[12,80,128]{2,1,0:T(8,128)(2,1)S(1)}, u32[]{:S(2)}, u32[]{:S(2)}) collective-permute-start(bf16[12,80,128]{2,1,0:T(8,128)(2,1)S(1)} %laid.7), channel_id=1, source_target_pairs={{0,4},{2,6},{4,0},{6,2},{1,5},{3,7},{5,1},{7,3},{8,12},{10,14},{12... | collective-permute-start | bytes 737288 | tf_op jit(solution)/shard_map/ppermute | solution.py:140
  35.5 2.9 %collective-permute-start.10 = (bf16[12,80,128]{2,1,0:T(8,128)(2,1)S(1)}, bf16[12,80,128]{2,1,0:T(8,128)(2,1)S(1)}, u32[]{:S(2)}, u32[]{:S(2)}) collective-permute-start(bf16[12,80,128]{2,1,0:T(8,128)(2,1)S(1)} %laid.7), channel_id=1, source_target_pairs={{0,6},{2,0},{4,2},{6,4},{1,7},{3,1},{5,3},{7,5},{8,14},{10,8},{12,... | collective-permute-start | bytes 737288 | tf_op jit(solution)/shard_map/ppermute | solution.py:140
  39.2 4.6 %collective-permute-done.2 = bf16[12,8,320]{2,1,0:T(8,128)(2,1)S(1)} collective-permute-done((bf16[12,8,320]{2,1,0:T(8,128)(2,1)S(1)}, bf16[12,8,320]{2,1,0:T(8,128)(2,1)S(1)}, u32[]{:S(2)}, u32[]{:S(2)}) %collective-permute-start.2) | collective-permute-done | bytes 61472 | tf_op jit(solution)/shard_map/ppermute | solution.py:430
  43.8 5.2 %collective-permute-done.9.refs_1_ = bf16[12,80,128]{2,1,0:T(8,128)(2,1)S(1)} collective-permute-done((bf16[12,80,128]{2,1,0:T(8,128)(2,1)S(1)}, bf16[12,80,128]{2,1,0:T(8,128)(2,1)S(1)}, u32[]{:S(2)}, u32[]{:S(2)}) %collective-permute-start.9) | collective-permute-done | bytes 245792 | tf_op jit(solution)/shard_map/ppermute | solution.py:140
  52.3 8.3 %encoder.1 = (bf16[640,384]{1,0:T(8,128)(2,1)S(1)}, bf16[2,48,384]{2,1,0:T(8,128)(2,1)S(1)}) custom-call(s32[4]{0:T(128)S(1)} %pad_add_fusion.place, bf16[960,384]{1,0:T(8,128)(2,1)S(1)} %bitcast.13, f32[1,320]{1,0:T(1,128)S(1)} %reshape.19.bias1, f32[1,320]{1,0:T(1,128)S(1)} %reshape.20.bias2, bf16[48,80,128]{2,1,0:T(8,128)(2,1)} %get-tuple-element.32.refs_0_, ...), custom_call_target="tpu_custom_call" | custom-call | flops 21233664000 | bytes 1048576 | tf_op jit(solution)/shard_map/encoder/pallas_call | solution.py:467
  60.5 1.2 %laid.13.refs_2_ = bf16[54,80,128]{2,1,0:T(8,128)(2,1)} custom-call(bf16[27,80,128]{2,1,0:T(8,128)(2,1)S(1)} %laid.12.refs_0_, bf16[27,80,128]{2,1,0:T(8,128)(2,1)S(1)} %collective-permute-done.20.refs_1_), custom_call_target="tpu_custom_call" | custom-call | bytes 2097152 | tf_op jit(solution)/shard_map/laid/pallas_call | solution.py:127
  62.1 1.2 %collective-permute-start.16 = (bf16[9,80,128]{2,1,0:T(8,128)(2,1)S(1)}, bf16[9,80,128]{2,1,0:T(8,128)(2,1)S(1)}, u32[]{:S(2)}, u32[]{:S(2)}) collective-permute-start(bf16[9,80,128]{2,1,0:T(8,128)(2,1)S(1)} %laid.10.refs_0_), channel_id=1, source_target_pairs={{0,1},{1,0},{2,3},{3,2},{4,5},{5,4},{6,7},{7,6},{8,24},{9,25},{10,... | collective-permute-start | bytes 552968 | tf_op jit(solution)/shard_map/ppermute | solution.py:445
  63.3 5.0 %collective-permute-start.13 = (bf16[2,48,384]{2,1,0:T(8,128)(2,1)S(1)}, bf16[2,48,384]{2,1,0:T(8,128)(2,1)S(1)}, u32[]{:S(2)}, u32[]{:S(2)}) collective-permute-start(bf16[2,48,384]{2,1,0:T(8,128)(2,1)S(1)} %get-tuple-element.41.own), channel_id=1, source_target_pairs={{0,2},{2,4},{4,6},{6,0},{1,3},{3,5},{5,7},{7,1},{8,10},{10,12},{12... | collective-permute-start | bytes 221192 | tf_op jit(solution)/shard_map/ppermute | solution.py:488
  68.2 1.3 %collective-permute-start.14 = (bf16[2,48,384]{2,1,0:T(8,128)(2,1)S(1)}, bf16[2,48,384]{2,1,0:T(8,128)(2,1)S(1)}, u32[]{:S(2)}, u32[]{:S(2)}) collective-permute-start(bf16[2,48,384]{2,1,0:T(8,128)(2,1)S(1)} %get-tuple-element.41.own), channel_id=1, source_target_pairs={{0,4},{2,6},{4,0},{6,2},{1,5},{3,7},{5,1},{7,3},{8,12},{10,14},{12... | collective-permute-start | bytes 221192 | tf_op jit(solution)/shard_map/ppermute | solution.py:488
  71.9 2.8 %collective-permute-done.14.refs_1_ = bf16[2,48,384]{2,1,0:T(8,128)(2,1)S(1)} collective-permute-done((bf16[2,48,384]{2,1,0:T(8,128)(2,1)S(1)}, bf16[2,48,384]{2,1,0:T(8,128)(2,1)S(1)}, u32[]{:S(2)}, u32[]{:S(2)}) %collective-permute-start.14) | collective-permute-done | bytes 73760 | tf_op jit(solution)/shard_map/ppermute | solution.py:488
  75.2 2.0 %middle.1 = (bf16[4,48,256]{2,1,0:T(8,128)(2,1)S(1)}, bf16[4,48,256]{2,1,0:T(8,128)(2,1)S(1)}, bf16[4,48,256]{2,1,0:T(8,128)(2,1)S(1)}, bf16[4,48,256]{2,1,0:T(8,128)(2,1)S(1)}) custom-call(s32[4]{0:T(128)S(1)} %pad_add_fusion.place, bf16[2,48,384]{2,1,0:T(8,128)(2,1)S(1)} %get-tuple-element.41.own, bf16[2,48,384]{2,1,0:T(8,128)(2,1)S(1)} %collective-permute-done.13.refs_0_, ...), custom_call_target="tpu_custom_call" | custom-call | flops 4718592000 | bytes 1048576 | tf_op jit(solution)/shard_map/middle/pallas_call | solution.py:498
  77.2 1.5 %collective-permute-start.17 = (bf16[4,48,256]{2,1,0:T(8,128)(2,1)S(1)}, bf16[4,48,256]{2,1,0:T(8,128)(2,1)S(1)}, u32[]{:S(2)}, u32[]{:S(2)}) collective-permute-start(bf16[4,48,256]{2,1,0:T(8,128)(2,1)S(1)} %get-tuple-element.47), channel_id=1, source_target_pairs={{0,2},{2,4},{4,6},{6,0},{1,3},{3,5},{5,7},{7,1},{8,10},{10,12},{12... | collective-permute-start | bytes 294920 | tf_op jit(solution)/shard_map/ppermute | solution.py:514
  78.7 1.6 %collective-permute-start.18 = (bf16[4,48,256]{2,1,0:T(8,128)(2,1)S(1)}, bf16[4,48,256]{2,1,0:T(8,128)(2,1)S(1)}, u32[]{:S(2)}, u32[]{:S(2)}) collective-permute-start(bf16[4,48,256]{2,1,0:T(8,128)(2,1)S(1)} %get-tuple-element.48), channel_id=1, source_target_pairs={{0,4},{2,6},{4,0},{6,2},{1,5},{3,7},{5,1},{7,3},{8,12},{10,14},{12... | collective-permute-start | bytes 294920 | tf_op jit(solution)/shard_map/ppermute | solution.py:514
  81.2 1.5 %collective-permute-start.24 = (bf16[18,80,128]{2,1,0:T(8,128)(2,1)S(1)}, bf16[18,80,128]{2,1,0:T(8,128)(2,1)S(1)}, u32[]{:S(2)}, u32[]{:S(2)}) collective-permute-start(bf16[18,80,128]{2,1,0:T(8,128)(2,1)S(1)} %laid.11.refs_1_), channel_id=1, source_target_pairs={{0,16},{1,17},{2,18},{3,19},{4,20},{5,21},{6,22},{7,23},{8,9},{9,8... | collective-permute-start | bytes 1105928 | tf_op jit(solution)/shard_map/ppermute | solution.py:445
  82.7 2.1 %collective-permute-done.17.refs_1_ = bf16[4,48,256]{2,1,0:T(8,128)(2,1)S(1)} collective-permute-done((bf16[4,48,256]{2,1,0:T(8,128)(2,1)S(1)}, bf16[4,48,256]{2,1,0:T(8,128)(2,1)S(1)}, u32[]{:S(2)}, u32[]{:S(2)}) %collective-permute-start.17) | collective-permute-done | bytes 98336 | tf_op jit(solution)/shard_map/ppermute | solution.py:514
  84.8 2.6 %collective-permute-done.18.refs_2_ = bf16[4,48,256]{2,1,0:T(8,128)(2,1)S(1)} collective-permute-done((bf16[4,48,256]{2,1,0:T(8,128)(2,1)S(1)}, bf16[4,48,256]{2,1,0:T(8,128)(2,1)S(1)}, u32[]{:S(2)}, u32[]{:S(2)}) %collective-permute-start.18) | collective-permute-done | bytes 98336 | tf_op jit(solution)/shard_map/ppermute | solution.py:514
  88.8 1.5 %collective-permute-done.23.refs_5_ = bf16[54,80,128]{2,1,0:T(8,128)(2,1)S(1)} collective-permute-done((bf16[54,80,128]{2,1,0:T(8,128)(2,1)}, bf16[54,80,128]{2,1,0:T(8,128)(2,1)S(1)}, u32[]{:S(2)}, u32[]{:S(2)}) %collective-permute-start.23) | collective-permute-done | bytes 1105952 | tf_op jit(solution)/shard_map/ppermute | solution.py:154
  91.3 8.6 %joined.1.refined = bf16[480,384]{1,0:T(8,128)(2,1)S(1)} custom-call(s32[4]{0:T(128)S(1)} %pad_add_fusion.place, bf16[640,384]{1,0:T(8,128)(2,1)S(1)} %get-tuple-element.40.skip, f32[1,320]{1,0:T(1,128)S(1)} %reshape.21.bias, bf16[5,4,48,128]{3,2,1,0:T(8,128)(2,1)S(1)} %field.1.refs_0_, bf16[72,80,128]{2,1,0:T(8,128)(2,1)} %copy-done.5, ...), custom_call_target="tpu_custom_call" | custom-call | flops 10616832000 | bytes 1048576 | tf_op jit(solution)/shard_map/joined/pallas_call | solution.py:552
  100.0 3.5 %last.1 = bf16[1,4,64,320]{3,2,1,0:T(8,128)(2,1)} custom-call(s32[4]{0:T(128)S(1)} %pad_add_fusion.place, bf16[480,384]{1,0:T(8,128)(2,1)S(1)} %joined.1.refined, f32[1,320]{1,0:T(1,128)S(1)} %reshape.23.bias, bf16[24,80,128]{2,1,0:T(8,128)(2,1)} %copy-done.7, bf16[18,80,128]{2,1,0:T(8,128)(2,1)S(1)} %laid.11.refs_1_, ...), custom_call_target="tpu_custom_call" | custom-call | flops 2359296000 | bytes 1048576 | tf_op jit(solution)/shard_map/last/pallas_call | solution.py:568
  (86 shorter events, 15.3 us)
Async XLA Ops:
  0.0 22.8 %copy-start = (bf16[2,4,64,320]{3,2,1,0:T(8,128)(2,1)S(1)}, bf16[2,4,64,320]{3,2,1,0:T(8,128)(2,1)}, u32[]{:S(2)}) copy-start(bf16[2,4,64,320]{3,2,1,0:T(8,128)(2,1)} %param.11) | copy-start | bytes 983044
  4.0 11.1 %collective-permute-start.3 = (bf16[6,80,128]{2,1,0:T(8,128)(2,1)S(1)}, bf16[6,80,128]{2,1,0:T(8,128)(2,1)S(1)}, u32[]{:S(2)}, u32[]{:S(2)}) collective-permute-start(bf16[6,80,128]{2,1,0:T(8,128)(2,1)S(1)} %get-tuple-element.30), channel_id=1, source_target_pairs={{0,2},{2,4},{4,6},{6,0},{1,3},{3,5},{5,7},{7,1},{8,10},{10,12},{12... | collective-permute-start | bytes 368648 | tf_op jit(solution)/shard_map/ppermute | solution.py:140
  7.0 10.7 %collective-permute-start.4 = (bf16[6,80,128]{2,1,0:T(8,128)(2,1)S(1)}, bf16[6,80,128]{2,1,0:T(8,128)(2,1)S(1)}, u32[]{:S(2)}, u32[]{:S(2)}) collective-permute-start(bf16[6,80,128]{2,1,0:T(8,128)(2,1)S(1)} %get-tuple-element.30), channel_id=1, source_target_pairs={{0,4},{2,6},{4,0},{6,2},{1,5},{3,7},{5,1},{7,3},{8,12},{10,14},{12... | collective-permute-start | bytes 368648 | tf_op jit(solution)/shard_map/ppermute | solution.py:140
  9.6 8.1 %collective-permute-start.5 = (bf16[6,80,128]{2,1,0:T(8,128)(2,1)S(1)}, bf16[6,80,128]{2,1,0:T(8,128)(2,1)S(1)}, u32[]{:S(2)}, u32[]{:S(2)}) collective-permute-start(bf16[6,80,128]{2,1,0:T(8,128)(2,1)S(1)} %get-tuple-element.30), channel_id=1, source_target_pairs={{0,6},{2,0},{4,2},{6,4},{1,7},{3,1},{5,3},{7,5},{8,14},{10,8},{12,... | collective-permute-start | bytes 368648 | tf_op jit(solution)/shard_map/ppermute | solution.py:140
  18.2 7.9 %collective-permute-start.6 = (bf16[18,80,128]{2,1,0:T(8,128)(2,1)S(1)}, bf16[18,80,128]{2,1,0:T(8,128)(2,1)S(1)}, u32[]{:S(2)}, u32[]{:S(2)}) collective-permute-start(bf16[18,80,128]{2,1,0:T(8,128)(2,1)S(1)} %laid.8.refs_0_), channel_id=1, source_target_pairs={{0,1},{1,0},{2,3},{3,2},{4,5},{5,4},{6,7},{7,6},{8,24},{9,25},{10,... | collective-permute-start | bytes 1105928 | tf_op jit(solution)/shard_map/ppermute | solution.py:445
  19.7 13.5 %collective-permute-start.7 = (bf16[12,80,128]{2,1,0:T(8,128)(2,1)S(1)}, bf16[12,80,128]{2,1,0:T(8,128)(2,1)S(1)}, u32[]{:S(2)}, u32[]{:S(2)}) collective-permute-start(bf16[12,80,128]{2,1,0:T(8,128)(2,1)S(1)} %laid.7), channel_id=1, source_target_pairs={{0,2},{2,4},{4,6},{6,0},{1,3},{3,5},{5,7},{7,1},{8,10},{10,12},{12... | collective-permute-start | bytes 737288 | tf_op jit(solution)/shard_map/ppermute | solution.py:140
  22.9 26.3 %copy-start.9 = (f32[320]{0:T(512)S(1)}, f32[320]{0:T(512)}, u32[]{:S(2)}) copy-start(f32[320]{0:T(512)} %param.13) | copy-start | bytes 3844
  22.9 26.3 %copy-start.10 = (f32[320]{0:T(512)S(1)}, f32[320]{0:T(512)}, u32[]{:S(2)}) copy-start(f32[320]{0:T(512)} %param.15) | copy-start | bytes 3844
  22.9 9.3 %collective-permute-start = (bf16[4,64,320]{2,1,0:T(8,128)(2,1)S(1)}, bf16[4,64,320]{2,1,0:T(8,128)(2,1)S(1)}, u32[]{:S(2)}, u32[]{:S(2)}) collective-permute-start(bf16[4,64,320]{2,1,0:T(8,128)(2,1)S(1)} %dynamic-slice_bitcast_fusion), channel_id=1, source_target_pairs={{0,2},{2,4},{4,6},{1,3},{3,5},{5,7},{8,10},{10,12},{12,14},{9,11},... | collective-permute-start | bytes 491528 | tf_op jit(solution)/shard_map/ppermute | solution.py:425
  24.8 8.5 %collective-permute-start.1 = (bf16[4,64,320]{2,1,0:T(8,128)(2,1)S(1)}, bf16[4,64,320]{2,1,0:T(8,128)(2,1)S(1)}, u32[]{:S(2)}, u32[]{:S(2)}) collective-permute-start(bf16[4,64,320]{2,1,0:T(8,128)(2,1)S(1)} %dynamic-slice_bitcast_fusion), channel_id=1, source_target_pairs={{2,0},{4,2},{6,4},{3,1},{5,3},{7,5},{10,8},{12,10},{14,12},{11,9},... | collective-permute-start | bytes 491528 | tf_op jit(solution)/shard_map/ppermute | solution.py:426
  26.5 22.9 %copy-start.1 = (bf16[36,80,128]{2,1,0:T(8,128)(2,1)}, bf16[36,80,128]{2,1,0:T(8,128)(2,1)S(1)}, u32[]{:S(2)}) copy-start(bf16[36,80,128]{2,1,0:T(8,128)(2,1)S(1)} %laid.9.refs_1_) | copy-start | bytes 2211844
  33.3 15.8 %collective-permute-start.8 = (bf16[36,80,128]{2,1,0:T(8,128)(2,1)S(1)}, bf16[36,80,128]{2,1,0:T(8,128)(2,1)S(1)}, u32[]{:S(2)}, u32[]{:S(2)}) collective-permute-start(bf16[36,80,128]{2,1,0:T(8,128)(2,1)S(1)} %laid.9.refs_1_), channel_id=1, source_target_pairs={{0,16},{1,17},{2,18},{3,19},{4,20},{5,21},{6,22},{7,23},{8,9},{9,8... | collective-permute-start | bytes 2211848 | tf_op jit(solution)/shard_map/ppermute | solution.py:445
  34.1 15.0 %collective-permute-start.9 = (bf16[12,80,128]{2,1,0:T(8,128)(2,1)S(1)}, bf16[12,80,128]{2,1,0:T(8,128)(2,1)S(1)}, u32[]{:S(2)}, u32[]{:S(2)}) collective-permute-start(bf16[12,80,128]{2,1,0:T(8,128)(2,1)S(1)} %laid.7), channel_id=1, source_target_pairs={{0,4},{2,6},{4,0},{6,2},{1,5},{3,7},{5,1},{7,3},{8,12},{10,14},{12... | collective-permute-start | bytes 737288 | tf_op jit(solution)/shard_map/ppermute | solution.py:140
  35.5 13.5 %collective-permute-start.10 = (bf16[12,80,128]{2,1,0:T(8,128)(2,1)S(1)}, bf16[12,80,128]{2,1,0:T(8,128)(2,1)S(1)}, u32[]{:S(2)}, u32[]{:S(2)}) collective-permute-start(bf16[12,80,128]{2,1,0:T(8,128)(2,1)S(1)} %laid.7), channel_id=1, source_target_pairs={{0,6},{2,0},{4,2},{6,4},{1,7},{3,1},{5,3},{7,5},{8,14},{10,8},{12,... | collective-permute-start | bytes 737288 | tf_op jit(solution)/shard_map/ppermute | solution.py:140
  38.6 5.3 %collective-permute-start.2 = (bf16[12,8,320]{2,1,0:T(8,128)(2,1)S(1)}, bf16[12,8,320]{2,1,0:T(8,128)(2,1)S(1)}, u32[]{:S(2)}, u32[]{:S(2)}) collective-permute-start(bf16[12,8,320]{2,1,0:T(8,128)(2,1)S(1)} %slice_select_fusion), channel_id=1, source_target_pairs={{0,1},{1,0},{2,3},{3,2},{4,5},{5,4},{6,7},{7,6},{8,9},{9,8},{10,11... | collective-permute-start | bytes 184328 | tf_op jit(solution)/shard_map/ppermute | solution.py:430
  39.2 11.7 %collective-permute-start.11 = (bf16[36,80,128]{2,1,0:T(8,128)(2,1)S(1)}, bf16[36,80,128]{2,1,0:T(8,128)(2,1)S(1)}, u32[]{:S(2)}, u32[]{:S(2)}) collective-permute-start(bf16[36,80,128]{2,1,0:T(8,128)(2,1)S(1)} %laid.9.refs_1_), channel_id=1, source_target_pairs={{0,8},{8,0},{1,9},{9,1},{2,10},{10,2},{3,11},{11,3},{4,12},{12,4},... | collective-permute-start | bytes 2211848 | tf_op jit(solution)/shard_map/ppermute | solution.py:154
  49.1 2.3 %collective-permute-start.12 = (bf16[36,80,128]{2,1,0:T(8,128)(2,1)S(1)}, bf16[36,80,128]{2,1,0:T(8,128)(2,1)S(1)}, u32[]{:S(2)}, u32[]{:S(2)}) collective-permute-start(bf16[36,80,128]{2,1,0:T(8,128)(2,1)S(1)} %collective-permute-done.8.refs_2_), channel_id=1, source_target_pairs={{0,8},{8,0},{1,9},{9,1},{2,10},{10,2},{3,11},{11,3},{4,12},{12,4},... | collective-permute-start | bytes 2211848 | tf_op jit(solution)/shard_map/ppermute | solution.py:154
  50.2 10.4 %collective-permute-start.20 = (bf16[27,80,128]{2,1,0:T(8,128)(2,1)S(1)}, bf16[27,80,128]{2,1,0:T(8,128)(2,1)S(1)}, u32[]{:S(2)}, u32[]{:S(2)}) collective-permute-start(bf16[27,80,128]{2,1,0:T(8,128)(2,1)S(1)} %laid.12.refs_0_), channel_id=1, source_target_pairs={{0,1},{1,0},{2,3},{3,2},{4,5},{5,4},{6,7},{7,6},{8,24},{9,25},{10,... | collective-permute-start | bytes 1658888 | tf_op jit(solution)/shard_map/ppermute | solution.py:445
  60.5 14.6 %copy-start.6 = (bf16[9,320,160]{1,2,0:T(8,128)(2,1)S(1)}, bf16[9,320,160]{1,2,0:T(8,128)(2,1)}, u32[]{:S(2)}) copy-start(bf16[9,320,160]{1,2,0:T(8,128)(2,1)} %param.16) | copy-start | bytes 2764804
  61.7 19.5 %collective-permute-start.21 = (bf16[54,80,128]{2,1,0:T(8,128)(2,1)}, bf16[54,80,128]{2,1,0:T(8,128)(2,1)}, u32[]{:S(2)}, u32[]{:S(2)}) collective-permute-start(bf16[54,80,128]{2,1,0:T(8,128)(2,1)} %laid.13.refs_2_), channel_id=1, source_target_pairs={{0,16},{1,17},{2,18},{3,19},{4,20},{5,21},{6,22},{7,23},{8,9},{9,8... | collective-permute-start | bytes 3317768 | tf_op jit(solution)/shard_map/ppermute | solution.py:445
  62.1 9.3 %collective-permute-start.16 = (bf16[9,80,128]{2,1,0:T(8,128)(2,1)S(1)}, bf16[9,80,128]{2,1,0:T(8,128)(2,1)S(1)}, u32[]{:S(2)}, u32[]{:S(2)}) collective-permute-start(bf16[9,80,128]{2,1,0:T(8,128)(2,1)S(1)} %laid.10.refs_0_), channel_id=1, source_target_pairs={{0,1},{1,0},{2,3},{3,2},{4,5},{5,4},{6,7},{7,6},{8,24},{9,25},{10,... | collective-permute-start | bytes 552968 | tf_op jit(solution)/shard_map/ppermute | solution.py:445
  63.3 8.6 %collective-permute-start.13 = (bf16[2,48,384]{2,1,0:T(8,128)(2,1)S(1)}, bf16[2,48,384]{2,1,0:T(8,128)(2,1)S(1)}, u32[]{:S(2)}, u32[]{:S(2)}) collective-permute-start(bf16[2,48,384]{2,1,0:T(8,128)(2,1)S(1)} %get-tuple-element.41.own), channel_id=1, source_target_pairs={{0,2},{2,4},{4,6},{6,0},{1,3},{3,5},{5,7},{7,1},{8,10},{10,12},{12... | collective-permute-start | bytes 221192 | tf_op jit(solution)/shard_map/ppermute | solution.py:488
  68.2 6.4 %collective-permute-start.14 = (bf16[2,48,384]{2,1,0:T(8,128)(2,1)S(1)}, bf16[2,48,384]{2,1,0:T(8,128)(2,1)S(1)}, u32[]{:S(2)}, u32[]{:S(2)}) collective-permute-start(bf16[2,48,384]{2,1,0:T(8,128)(2,1)S(1)} %get-tuple-element.41.own), channel_id=1, source_target_pairs={{0,4},{2,6},{4,0},{6,2},{1,5},{3,7},{5,1},{7,3},{8,12},{10,14},{12... | collective-permute-start | bytes 221192 | tf_op jit(solution)/shard_map/ppermute | solution.py:488
  69.6 5.6 %collective-permute-start.15 = (bf16[2,48,384]{2,1,0:T(8,128)(2,1)S(1)}, bf16[2,48,384]{2,1,0:T(8,128)(2,1)S(1)}, u32[]{:S(2)}, u32[]{:S(2)}) collective-permute-start(bf16[2,48,384]{2,1,0:T(8,128)(2,1)S(1)} %get-tuple-element.41.own), channel_id=1, source_target_pairs={{0,6},{2,0},{4,2},{6,4},{1,7},{3,1},{5,3},{7,5},{8,14},{10,8},{12,... | collective-permute-start | bytes 221192 | tf_op jit(solution)/shard_map/ppermute | solution.py:488
  77.2 7.6 %collective-permute-start.17 = (bf16[4,48,256]{2,1,0:T(8,128)(2,1)S(1)}, bf16[4,48,256]{2,1,0:T(8,128)(2,1)S(1)}, u32[]{:S(2)}, u32[]{:S(2)}) collective-permute-start(bf16[4,48,256]{2,1,0:T(8,128)(2,1)S(1)} %get-tuple-element.47), channel_id=1, source_target_pairs={{0,2},{2,4},{4,6},{6,0},{1,3},{3,5},{5,7},{7,1},{8,10},{10,12},{12... | collective-permute-start | bytes 294920 | tf_op jit(solution)/shard_map/ppermute | solution.py:514
  78.7 8.7 %collective-permute-start.18 = (bf16[4,48,256]{2,1,0:T(8,128)(2,1)S(1)}, bf16[4,48,256]{2,1,0:T(8,128)(2,1)S(1)}, u32[]{:S(2)}, u32[]{:S(2)}) collective-permute-start(bf16[4,48,256]{2,1,0:T(8,128)(2,1)S(1)} %get-tuple-element.48), channel_id=1, source_target_pairs={{0,4},{2,6},{4,0},{6,2},{1,5},{3,7},{5,1},{7,3},{8,12},{10,14},{12... | collective-permute-start | bytes 294920 | tf_op jit(solution)/shard_map/ppermute | solution.py:514
  80.3 7.0 %collective-permute-start.19 = (bf16[4,48,256]{2,1,0:T(8,128)(2,1)S(1)}, bf16[4,48,256]{2,1,0:T(8,128)(2,1)S(1)}, u32[]{:S(2)}, u32[]{:S(2)}) collective-permute-start(bf16[4,48,256]{2,1,0:T(8,128)(2,1)S(1)} %get-tuple-element.49), channel_id=1, source_target_pairs={{0,6},{2,0},{4,2},{6,4},{1,7},{3,1},{5,3},{7,5},{8,14},{10,8},{12,... | collective-permute-start | bytes 294920 | tf_op jit(solution)/shard_map/ppermute | solution.py:514
  81.2 7.7 %collective-permute-start.22 = (bf16[54,80,128]{2,1,0:T(8,128)(2,1)S(1)}, bf16[54,80,128]{2,1,0:T(8,128)(2,1)S(1)}, u32[]{:S(2)}, u32[]{:S(2)}) collective-permute-start(bf16[54,80,128]{2,1,0:T(8,128)(2,1)S(1)} %copy-done.8), channel_id=1, source_target_pairs={{0,8},{8,0},{1,9},{9,1},{2,10},{10,2},{3,11},{11,3},{4,12},{12,4},... | collective-permute-start | bytes 3317768 | tf_op jit(solution)/shard_map/ppermute | solution.py:154
  81.2 7.6 %collective-permute-start.24 = (bf16[18,80,128]{2,1,0:T(8,128)(2,1)S(1)}, bf16[18,80,128]{2,1,0:T(8,128)(2,1)S(1)}, u32[]{:S(2)}, u32[]{:S(2)}) collective-permute-start(bf16[18,80,128]{2,1,0:T(8,128)(2,1)S(1)} %laid.11.refs_1_), channel_id=1, source_target_pairs={{0,16},{1,17},{2,18},{3,19},{4,20},{5,21},{6,22},{7,23},{8,9},{9,8... | collective-permute-start | bytes 1105928 | tf_op jit(solution)/shard_map/ppermute | solution.py:445
  84.8 15.2 %collective-permute-start.25 = (bf16[18,80,128]{2,1,0:T(8,128)(2,1)S(1)}, bf16[18,80,128]{2,1,0:T(8,128)(2,1)S(1)}, u32[]{:S(2)}, u32[]{:S(2)}) collective-permute-start(bf16[18,80,128]{2,1,0:T(8,128)(2,1)S(1)} %laid.11.refs_1_), channel_id=1, source_target_pairs={{0,8},{8,0},{1,9},{9,1},{2,10},{10,2},{3,11},{11,3},{4,12},{12,4},... | collective-permute-start | bytes 1105928 | tf_op jit(solution)/shard_map/ppermute | solution.py:154
  87.4 3.0 %collective-permute-start.23 = (bf16[54,80,128]{2,1,0:T(8,128)(2,1)}, bf16[54,80,128]{2,1,0:T(8,128)(2,1)S(1)}, u32[]{:S(2)}, u32[]{:S(2)}) collective-permute-start(bf16[54,80,128]{2,1,0:T(8,128)(2,1)} %collective-permute-done.21.refs_3_), channel_id=1, source_target_pairs={{0,8},{8,0},{1,9},{9,1},{2,10},{10,2},{3,11},{11,3},{4,12},{12,4},... | collective-permute-start | bytes 3317768 | tf_op jit(solution)/shard_map/ppermute | solution.py:154
  88.8 11.2 %collective-permute-start.26 = (bf16[18,80,128]{2,1,0:T(8,128)(2,1)S(1)}, bf16[18,80,128]{2,1,0:T(8,128)(2,1)S(1)}, u32[]{:S(2)}, u32[]{:S(2)}) collective-permute-start(bf16[18,80,128]{2,1,0:T(8,128)(2,1)S(1)} %collective-permute-done.24.refs_2_), channel_id=1, source_target_pairs={{0,8},{8,0},{1,9},{9,1},{2,10},{10,2},{3,11},{11,3},{4,12},{12,4},... | collective-permute-start | bytes 1105928 | tf_op jit(solution)/shard_map/ppermute | solution.py:154
  (13 other events, 52.1 us)

commit v4 on v3

--- a/solution.py
+++ b/solution.py
@@ -82,6 +82,47 @@
         out_specs=[VMEM, VMEM],
         compiler_params=params(),
         name="pack_weights",
+    )(place, *weights)
+
+
+def piece_body(layouts, parts, place, *refs):
+    count = len(layouts)
+    sources, mine, held, sems = refs[:count], refs[count], refs[count + 1 : -1], refs[-1]
+    copies = [pltpu.make_async_copy(a, b, sems.at[i]) for i, (a, b) in enumerate(zip(sources, held))]
+    for copy in copies:
+        copy.start()
+    for copy in copies:
+        copy.wait()
+    chunks = [(source, chunk) for source, layer in zip(held, layouts) for chunk in layer]
+    size, channels = mine.shape[:2]
+    wanted = owner_piece(place, parts, place[1], 0)
+    for piece in range(parts):
+
+        @pl.when(wanted == piece)
+        def _(piece=piece):
+            for index in range(size):
+                block = [jnp.zeros((channels, LANES), BF)]
+                if piece * size + index < len(chunks):
+                    source, chunk = chunks[piece * size + index]
+                    block = [source[tap, :, pl.ds(first, width)] for tap, first, width in chunk]
+                    have = sum(part.shape[1] for part in block)
+                    if have < LANES:
+                        block.append(jnp.zeros((channels, LANES - have), BF))
+                mine[index] = block[0] if len(block) == 1 else jnp.concatenate(block, axis=1)
+
+
+def pack_piece(layouts, parts, place, weights):
+    total = padded_count([chunk for chunks in layouts for chunk in chunks])
+    weights = [jnp.swapaxes(weight, 1, 2) for weight in weights]
+    return pl.pallas_call(
+        functools.partial(piece_body, layouts, parts),
+        out_shape=jax.ShapeDtypeStruct((total // parts, weights[0].shape[1], LANES), BF),
+        in_specs=[SMEM] + [HBM] * len(weights),
+        out_specs=VMEM,
+        scratch_shapes=[pltpu.VMEM(weight.shape, BF) for weight in weights]
+        + [pltpu.SemaphoreType.DMA((len(weights),))],
+        compiler_params=pltpu.CompilerParams(vmem_limit_bytes=52 * 1024 * 1024),
+        name="pack_piece",
     )(place, *weights)
 
 
@@ -414,8 +455,10 @@
         ((plain,), 8, (dec_second,)),
     )
     if spread_out:
-        (own0, mine0), (own1, mine1), (own2, mine2) = (
-            pack(layouts, parts, place, group) for layouts, parts, group in groups
+        mine0 = pack_piece(groups[0][0], groups[0][1], place, groups[0][2])
+        later = after(place, mine0)
+        (own0, _), (own1, mine1), (own2, mine2) = (
+            pack(layouts, parts, later, group) for layouts, parts, group in groups
         )
 
     tile = lax.dynamic_index_in_dim(latent, seg, 0, keepdims=False)
@@ -446,7 +489,7 @@
         here0 = from_planes(mine0, row_count)
         late = laid(mine1, mine2)
         here1 = from_planes(late, row_count)
-        block0 = laid(*after(here0, late))
+        block0 = laid(*after(here0, late, own0))
         block0 = laid(block0, across(block0, first))
         block0 = after(block0, here1[0], above, below)
         far0 = swap_cores(block0)

time: 104 us -> 103 us (level)
  waiting for transfers between devices: 30 us -> 28.1 us
    ppermute x6, waiting for transfers between devices: 7.81 us -> 6.11 us  [from_planes(): lax.ppermute(mine, 'row', cyclic(count, by))]
  transfers between devices with their start and end apart: 27 -> 27, of which waited for: 12 -> 12; matrix products, arithmetic and copies ran while one was open for 1% -> 1% of each run, Pallas kernels for 23% -> 25%
where the time goes in v4:
time: 103 us
  starting transfers between devices  35.9 us (35%)
  Pallas kernels  31.8 us (31%)
  waiting for transfers between devices  28.1 us (27%)
  local copies, waits for them, and re-layouts  6.15 us (6%)
    ppermute x6, starting transfers between devices, from_planes(): lax.ppermute(mine, 'row', cyclic(count, by))  14.5 us
    pallas_call x1, Pallas kernels, shards(): pl.pallas_call(functools.partial(joined_body, size, sets, groups[1][1]),...  8.64 us
    pallas_call x1, Pallas kernels, shards(): pl.pallas_call(functools.partial(encoder_body, size, sets, groups[0][1]),...  8.26 us
    ppermute x3, starting transfers between devices, shards(): lax.ppermute(pooled, 'row', cyclic(row_count, by))  7.42 us
    ppermute x6, waiting for transfers between devices, from_planes(): lax.ppermute(mine, 'row', cyclic(count, by))  6.11 us
    ppermute x6, starting transfers between devices, shards(): across = lambda block, pairs: lax.ppermute(block, AXES, pairs)  6.03 us
    ppermute x1, waiting for transfers between devices, shards(): above = lax.ppermute(tile, 'row', down)  5.69 us
    unnamed x38, local copies, waits for them, and re-layouts  5.32 us
  transfers between devices with their start and end apart: 27, of which 12 were waited for; matrix products, arithmetic and copies ran while one was open for 1% of the time, Pallas kernels for 25%

profile of v4, /device:TPU:0, one launch (start us, length us, event | category | flops | bytes accessed | tf_op | source)
XLA Modules:
  0.0 102.9 jit_solution(1948318182636640694)
XLA Ops:
  0.1 1.1 %copy-done.1 = bf16[9,320,80]{1,2,0:T(8,128)(2,1)S(1)} copy-done((bf16[9,320,80]{1,2,0:T(8,128)(2,1)S(1)}, bf16[9,320,80]{1,2,0:T(8,128)(2,1)}, u32[]{:S(2)}) %copy-start.1) | copy-done | bytes 460824
  3.0 3.1 %collective-permute-start.3 = (bf16[6,80,128]{2,1,0:T(8,128)(2,1)S(1)}, bf16[6,80,128]{2,1,0:T(8,128)(2,1)S(1)}, u32[]{:S(2)}, u32[]{:S(2)}) collective-permute-start(bf16[6,80,128]{2,1,0:T(8,128)(2,1)S(1)} %pack_piece.1), channel_id=1, source_target_pairs={{0,2},{2,4},{4,6},{6,0},{1,3},{3,5},{5,7},{7,1},{8,10},{10,12},{12... | collective-permute-start | bytes 368648 | tf_op jit(solution)/shard_map/ppermute | solution.py:181
  6.1 2.6 %collective-permute-start.4 = (bf16[6,80,128]{2,1,0:T(8,128)(2,1)S(1)}, bf16[6,80,128]{2,1,0:T(8,128)(2,1)S(1)}, u32[]{:S(2)}, u32[]{:S(2)}) collective-permute-start(bf16[6,80,128]{2,1,0:T(8,128)(2,1)S(1)} %pack_piece.1), channel_id=1, source_target_pairs={{0,4},{2,6},{4,0},{6,2},{1,5},{3,7},{5,1},{7,3},{8,12},{10,14},{12... | collective-permute-start | bytes 368648 | tf_op jit(solution)/shard_map/ppermute | solution.py:181
  8.7 1.3 %collective-permute-start.5 = (bf16[6,80,128]{2,1,0:T(8,128)(2,1)S(1)}, bf16[6,80,128]{2,1,0:T(8,128)(2,1)S(1)}, u32[]{:S(2)}, u32[]{:S(2)}) collective-permute-start(bf16[6,80,128]{2,1,0:T(8,128)(2,1)S(1)} %pack_piece.1), channel_id=1, source_target_pairs={{0,6},{2,0},{4,2},{6,4},{1,7},{3,1},{5,3},{7,5},{8,14},{10,8},{12,... | collective-permute-start | bytes 368648 | tf_op jit(solution)/shard_map/ppermute | solution.py:181
  10.0 1.7 %pack_weights.3 = (bf16[48,80,128]{2,1,0:T(8,128)(2,1)}, bf16[6,80,128]{2,1,0:T(8,128)(2,1)}) custom-call(s32[4]{0:T(128)S(1)} %pad_add_fusion.place, bf16[9,80,320]{2,1,0:T(8,128)(2,1)S(1)} %bitcast.14, bf16[9,80,320]{2,1,0:T(8,128)(2,1)S(1)} %bitcast.16), custom_call_target="tpu_custom_call" | custom-call | tf_op jit(solution)/shard_map/pack_weights/pallas_call | solution.py:75
  11.7 2.0 %pack_weights.4 = (bf16[72,80,128]{2,1,0:T(8,128)(2,1)S(1)}, bf16[9,80,128]{2,1,0:T(8,128)(2,1)S(1)}) custom-call(s32[4]{0:T(128)S(1)} %pad_add_fusion.place, bf16[9,80,960]{2,1,0:T(8,128)(2,1)} %bitcast.21), custom_call_target="tpu_custom_call" | custom-call | tf_op jit(solution)/shard_map/pack_weights/pallas_call | solution.py:75
  13.7 1.1 %copy-done.5 = bf16[72,80,128]{2,1,0:T(8,128)(2,1)} copy-done((bf16[72,80,128]{2,1,0:T(8,128)(2,1)}, bf16[72,80,128]{2,1,0:T(8,128)(2,1)S(1)}, u32[]{:S(2)}) %copy-start.5) | copy-done | bytes 1474584
  17.3 1.6 %collective-permute-start.6 = (bf16[18,80,128]{2,1,0:T(8,128)(2,1)S(1)}, bf16[18,80,128]{2,1,0:T(8,128)(2,1)S(1)}, u32[]{:S(2)}, u32[]{:S(2)}) collective-permute-start(bf16[18,80,128]{2,1,0:T(8,128)(2,1)S(1)} %laid.8.refs_0_), channel_id=1, source_target_pairs={{0,1},{1,0},{2,3},{3,2},{4,5},{5,4},{6,7},{7,6},{8,24},{9,25},{10,... | collective-permute-start | bytes 1105928 | tf_op jit(solution)/shard_map/ppermute | solution.py:488
  18.9 3.1 %collective-permute-start.7 = (bf16[12,80,128]{2,1,0:T(8,128)(2,1)S(1)}, bf16[12,80,128]{2,1,0:T(8,128)(2,1)S(1)}, u32[]{:S(2)}, u32[]{:S(2)}) collective-permute-start(bf16[12,80,128]{2,1,0:T(8,128)(2,1)S(1)} %laid.7), channel_id=1, source_target_pairs={{0,2},{2,4},{4,6},{6,0},{1,3},{3,5},{5,7},{7,1},{8,10},{10,12},{12... | collective-permute-start | bytes 737288 | tf_op jit(solution)/shard_map/ppermute | solution.py:181
  22.1 1.9 %collective-permute-start = (bf16[4,64,320]{2,1,0:T(8,128)(2,1)S(1)}, bf16[4,64,320]{2,1,0:T(8,128)(2,1)S(1)}, u32[]{:S(2)}, u32[]{:S(2)}) collective-permute-start(bf16[4,64,320]{2,1,0:T(8,128)(2,1)S(1)} %dynamic-slice_bitcast_fusion), channel_id=1, source_target_pairs={{0,2},{2,4},{4,6},{1,3},{3,5},{5,7},{8,10},{10,12},{12,14},{9,11},... | collective-permute-start | bytes 491528 | tf_op jit(solution)/shard_map/ppermute | solution.py:468
  24.0 1.3 %collective-permute-start.1 = (bf16[4,64,320]{2,1,0:T(8,128)(2,1)S(1)}, bf16[4,64,320]{2,1,0:T(8,128)(2,1)S(1)}, u32[]{:S(2)}, u32[]{:S(2)}) collective-permute-start(bf16[4,64,320]{2,1,0:T(8,128)(2,1)S(1)} %dynamic-slice_bitcast_fusion), channel_id=1, source_target_pairs={{2,0},{4,2},{6,4},{3,1},{5,3},{7,5},{10,8},{12,10},{14,12},{11,9},... | collective-permute-start | bytes 491528 | tf_op jit(solution)/shard_map/ppermute | solution.py:469
  25.6 5.7 %collective-permute-done = bf16[4,64,320]{2,1,0:T(8,128)(2,1)S(1)} collective-permute-done((bf16[4,64,320]{2,1,0:T(8,128)(2,1)S(1)}, bf16[4,64,320]{2,1,0:T(8,128)(2,1)S(1)}, u32[]{:S(2)}, u32[]{:S(2)}) %collective-permute-start) | collective-permute-done | bytes 163872 | tf_op jit(solution)/shard_map/ppermute | solution.py:468
  31.3 1.1 %collective-permute-done.1 = bf16[4,64,320]{2,1,0:T(8,128)(2,1)S(1)} collective-permute-done((bf16[4,64,320]{2,1,0:T(8,128)(2,1)S(1)}, bf16[4,64,320]{2,1,0:T(8,128)(2,1)S(1)}, u32[]{:S(2)}, u32[]{:S(2)}) %collective-permute-start.1) | collective-permute-done | bytes 163872 | tf_op jit(solution)/shard_map/ppermute | solution.py:469
  33.2 1.5 %collective-permute-start.9 = (bf16[12,80,128]{2,1,0:T(8,128)(2,1)S(1)}, bf16[12,80,128]{2,1,0:T(8,128)(2,1)S(1)}, u32[]{:S(2)}, u32[]{:S(2)}) collective-permute-start(bf16[12,80,128]{2,1,0:T(8,128)(2,1)S(1)} %laid.7), channel_id=1, source_target_pairs={{0,4},{2,6},{4,0},{6,2},{1,5},{3,7},{5,1},{7,3},{8,12},{10,14},{12... | collective-permute-start | bytes 737288 | tf_op jit(solution)/shard_map/ppermute | solution.py:181
  34.7 2.9 %collective-permute-start.10 = (bf16[12,80,128]{2,1,0:T(8,128)(2,1)S(1)}, bf16[12,80,128]{2,1,0:T(8,128)(2,1)S(1)}, u32[]{:S(2)}, u32[]{:S(2)}) collective-permute-start(bf16[12,80,128]{2,1,0:T(8,128)(2,1)S(1)} %laid.7), channel_id=1, source_target_pairs={{0,6},{2,0},{4,2},{6,4},{1,7},{3,1},{5,3},{7,5},{8,14},{10,8},{12,... | collective-permute-start | bytes 737288 | tf_op jit(solution)/shard_map/ppermute | solution.py:181
  38.4 4.6 %collective-permute-done.2 = bf16[12,8,320]{2,1,0:T(8,128)(2,1)S(1)} collective-permute-done((bf16[12,8,320]{2,1,0:T(8,128)(2,1)S(1)}, bf16[12,8,320]{2,1,0:T(8,128)(2,1)S(1)}, u32[]{:S(2)}, u32[]{:S(2)}) %collective-permute-start.2) | collective-permute-done | bytes 61472 | tf_op jit(solution)/shard_map/ppermute | solution.py:473
  43.0 5.2 %collective-permute-done.9.refs_1_ = bf16[12,80,128]{2,1,0:T(8,128)(2,1)S(1)} collective-permute-done((bf16[12,80,128]{2,1,0:T(8,128)(2,1)S(1)}, bf16[12,80,128]{2,1,0:T(8,128)(2,1)S(1)}, u32[]{:S(2)}, u32[]{:S(2)}) %collective-permute-start.9) | collective-permute-done | bytes 245792 | tf_op jit(solution)/shard_map/ppermute | solution.py:181
  51.4 8.3 %encoder.1 = (bf16[640,384]{1,0:T(8,128)(2,1)S(1)}, bf16[2,48,384]{2,1,0:T(8,128)(2,1)S(1)}) custom-call(s32[4]{0:T(128)S(1)} %pad_add_fusion.place, bf16[960,384]{1,0:T(8,128)(2,1)S(1)} %bitcast.17, f32[1,320]{1,0:T(1,128)S(1)} %reshape.19.bias1, f32[1,320]{1,0:T(1,128)S(1)} %reshape.20.bias2, bf16[48,80,128]{2,1,0:T(8,128)(2,1)} %get-tuple-element.32.refs_0_, ...), custom_call_target="tpu_custom_call" | custom-call | flops 21233664000 | bytes 1048576 | tf_op jit(solution)/shard_map/encoder/pallas_call | solution.py:510
  59.7 1.2 %laid.13.refs_2_ = bf16[54,80,128]{2,1,0:T(8,128)(2,1)} custom-call(bf16[27,80,128]{2,1,0:T(8,128)(2,1)S(1)} %laid.12.refs_0_, bf16[27,80,128]{2,1,0:T(8,128)(2,1)S(1)} %collective-permute-done.20.refs_1_), custom_call_target="tpu_custom_call" | custom-call | bytes 2097152 | tf_op jit(solution)/shard_map/laid/pallas_call | solution.py:168
  61.2 1.2 %collective-permute-start.16 = (bf16[9,80,128]{2,1,0:T(8,128)(2,1)S(1)}, bf16[9,80,128]{2,1,0:T(8,128)(2,1)S(1)}, u32[]{:S(2)}, u32[]{:S(2)}) collective-permute-start(bf16[9,80,128]{2,1,0:T(8,128)(2,1)S(1)} %laid.10.refs_0_), channel_id=1, source_target_pairs={{0,1},{1,0},{2,3},{3,2},{4,5},{5,4},{6,7},{7,6},{8,24},{9,25},{10,... | collective-permute-start | bytes 552968 | tf_op jit(solution)/shard_map/ppermute | solution.py:488
  62.4 5.1 %collective-permute-start.13 = (bf16[2,48,384]{2,1,0:T(8,128)(2,1)S(1)}, bf16[2,48,384]{2,1,0:T(8,128)(2,1)S(1)}, u32[]{:S(2)}, u32[]{:S(2)}) collective-permute-start(bf16[2,48,384]{2,1,0:T(8,128)(2,1)S(1)} %get-tuple-element.41.own), channel_id=1, source_target_pairs={{0,2},{2,4},{4,6},{6,0},{1,3},{3,5},{5,7},{7,1},{8,10},{10,12},{12... | collective-permute-start | bytes 221192 | tf_op jit(solution)/shard_map/ppermute | solution.py:531
  67.5 1.3 %collective-permute-start.14 = (bf16[2,48,384]{2,1,0:T(8,128)(2,1)S(1)}, bf16[2,48,384]{2,1,0:T(8,128)(2,1)S(1)}, u32[]{:S(2)}, u32[]{:S(2)}) collective-permute-start(bf16[2,48,384]{2,1,0:T(8,128)(2,1)S(1)} %get-tuple-element.41.own), channel_id=1, source_target_pairs={{0,4},{2,6},{4,0},{6,2},{1,5},{3,7},{5,1},{7,3},{8,12},{10,14},{12... | collective-permute-start | bytes 221192 | tf_op jit(solution)/shard_map/ppermute | solution.py:531
  71.1 2.8 %collective-permute-done.14.refs_1_ = bf16[2,48,384]{2,1,0:T(8,128)(2,1)S(1)} collective-permute-done((bf16[2,48,384]{2,1,0:T(8,128)(2,1)S(1)}, bf16[2,48,384]{2,1,0:T(8,128)(2,1)S(1)}, u32[]{:S(2)}, u32[]{:S(2)}) %collective-permute-start.14) | collective-permute-done | bytes 73760 | tf_op jit(solution)/shard_map/ppermute | solution.py:531
  74.4 2.0 %middle.1 = (bf16[4,48,256]{2,1,0:T(8,128)(2,1)S(1)}, bf16[4,48,256]{2,1,0:T(8,128)(2,1)S(1)}, bf16[4,48,256]{2,1,0:T(8,128)(2,1)S(1)}, bf16[4,48,256]{2,1,0:T(8,128)(2,1)S(1)}) custom-call(s32[4]{0:T(128)S(1)} %pad_add_fusion.place, bf16[2,48,384]{2,1,0:T(8,128)(2,1)S(1)} %get-tuple-element.41.own, bf16[2,48,384]{2,1,0:T(8,128)(2,1)S(1)} %collective-permute-done.13.refs_0_, ...), custom_call_target="tpu_custom_call" | custom-call | flops 4718592000 | bytes 1048576 | tf_op jit(solution)/shard_map/middle/pallas_call | solution.py:541
  76.4 1.5 %collective-permute-start.17 = (bf16[4,48,256]{2,1,0:T(8,128)(2,1)S(1)}, bf16[4,48,256]{2,1,0:T(8,128)(2,1)S(1)}, u32[]{:S(2)}, u32[]{:S(2)}) collective-permute-start(bf16[4,48,256]{2,1,0:T(8,128)(2,1)S(1)} %get-tuple-element.47), channel_id=1, source_target_pairs={{0,2},{2,4},{4,6},{6,0},{1,3},{3,5},{5,7},{7,1},{8,10},{10,12},{12... | collective-permute-start | bytes 294920 | tf_op jit(solution)/shard_map/ppermute | solution.py:557
  77.9 1.6 %collective-permute-start.18 = (bf16[4,48,256]{2,1,0:T(8,128)(2,1)S(1)}, bf16[4,48,256]{2,1,0:T(8,128)(2,1)S(1)}, u32[]{:S(2)}, u32[]{:S(2)}) collective-permute-start(bf16[4,48,256]{2,1,0:T(8,128)(2,1)S(1)} %get-tuple-element.48), channel_id=1, source_target_pairs={{0,4},{2,6},{4,0},{6,2},{1,5},{3,7},{5,1},{7,3},{8,12},{10,14},{12... | collective-permute-start | bytes 294920 | tf_op jit(solution)/shard_map/ppermute | solution.py:557
  80.5 1.5 %collective-permute-start.24 = (bf16[18,80,128]{2,1,0:T(8,128)(2,1)S(1)}, bf16[18,80,128]{2,1,0:T(8,128)(2,1)S(1)}, u32[]{:S(2)}, u32[]{:S(2)}) collective-permute-start(bf16[18,80,128]{2,1,0:T(8,128)(2,1)S(1)} %laid.11.refs_1_), channel_id=1, source_target_pairs={{0,16},{1,17},{2,18},{3,19},{4,20},{5,21},{6,22},{7,23},{8,9},{9,8... | collective-permute-start | bytes 1105928 | tf_op jit(solution)/shard_map/ppermute | solution.py:488
  82.0 2.0 %collective-permute-done.17.refs_1_ = bf16[4,48,256]{2,1,0:T(8,128)(2,1)S(1)} collective-permute-done((bf16[4,48,256]{2,1,0:T(8,128)(2,1)S(1)}, bf16[4,48,256]{2,1,0:T(8,128)(2,1)S(1)}, u32[]{:S(2)}, u32[]{:S(2)}) %collective-permute-start.17) | collective-permute-done | bytes 98336 | tf_op jit(solution)/shard_map/ppermute | solution.py:557
  84.0 2.6 %collective-permute-done.18.refs_2_ = bf16[4,48,256]{2,1,0:T(8,128)(2,1)S(1)} collective-permute-done((bf16[4,48,256]{2,1,0:T(8,128)(2,1)S(1)}, bf16[4,48,256]{2,1,0:T(8,128)(2,1)S(1)}, u32[]{:S(2)}, u32[]{:S(2)}) %collective-permute-start.18) | collective-permute-done | bytes 98336 | tf_op jit(solution)/shard_map/ppermute | solution.py:557
  88.1 1.5 %collective-permute-done.23.refs_5_ = bf16[54,80,128]{2,1,0:T(8,128)(2,1)S(1)} collective-permute-done((bf16[54,80,128]{2,1,0:T(8,128)(2,1)}, bf16[54,80,128]{2,1,0:T(8,128)(2,1)S(1)}, u32[]{:S(2)}, u32[]{:S(2)}) %collective-permute-start.23) | collective-permute-done | bytes 1105952 | tf_op jit(solution)/shard_map/ppermute | solution.py:195
  90.6 8.6 %joined.1.refined = bf16[480,384]{1,0:T(8,128)(2,1)S(1)} custom-call(s32[4]{0:T(128)S(1)} %pad_add_fusion.place, bf16[640,384]{1,0:T(8,128)(2,1)S(1)} %get-tuple-element.40.skip, f32[1,320]{1,0:T(1,128)S(1)} %reshape.21.bias, bf16[5,4,48,128]{3,2,1,0:T(8,128)(2,1)S(1)} %field.1.refs_0_, bf16[72,80,128]{2,1,0:T(8,128)(2,1)} %copy-done.5, ...), custom_call_target="tpu_custom_call" | custom-call | flops 10616832000 | bytes 1048576 | tf_op jit(solution)/shard_map/joined/pallas_call | solution.py:595
  99.2 3.5 %last.1 = bf16[1,4,64,320]{3,2,1,0:T(8,128)(2,1)} custom-call(s32[4]{0:T(128)S(1)} %pad_add_fusion.place, bf16[480,384]{1,0:T(8,128)(2,1)S(1)} %joined.1.refined, f32[1,320]{1,0:T(1,128)S(1)} %reshape.23.bias, bf16[24,80,128]{2,1,0:T(8,128)(2,1)} %copy-done.7, bf16[18,80,128]{2,1,0:T(8,128)(2,1)S(1)} %laid.11.refs_1_, ...), custom_call_target="tpu_custom_call" | custom-call | flops 2359296000 | bytes 1048576 | tf_op jit(solution)/shard_map/last/pallas_call | solution.py:611
  (87 shorter events, 15.9 us)
Async XLA Ops:
  0.0 22.0 %copy-start = (bf16[2,4,64,320]{3,2,1,0:T(8,128)(2,1)S(1)}, bf16[2,4,64,320]{3,2,1,0:T(8,128)(2,1)}, u32[]{:S(2)}) copy-start(bf16[2,4,64,320]{3,2,1,0:T(8,128)(2,1)} %param.11) | copy-start | bytes 983044
  3.0 12.8 %collective-permute-start.3 = (bf16[6,80,128]{2,1,0:T(8,128)(2,1)S(1)}, bf16[6,80,128]{2,1,0:T(8,128)(2,1)S(1)}, u32[]{:S(2)}, u32[]{:S(2)}) collective-permute-start(bf16[6,80,128]{2,1,0:T(8,128)(2,1)S(1)} %pack_piece.1), channel_id=1, source_target_pairs={{0,2},{2,4},{4,6},{6,0},{1,3},{3,5},{5,7},{7,1},{8,10},{10,12},{12... | collective-permute-start | bytes 368648 | tf_op jit(solution)/shard_map/ppermute | solution.py:181
  6.1 10.7 %collective-permute-start.4 = (bf16[6,80,128]{2,1,0:T(8,128)(2,1)S(1)}, bf16[6,80,128]{2,1,0:T(8,128)(2,1)S(1)}, u32[]{:S(2)}, u32[]{:S(2)}) collective-permute-start(bf16[6,80,128]{2,1,0:T(8,128)(2,1)S(1)} %pack_piece.1), channel_id=1, source_target_pairs={{0,4},{2,6},{4,0},{6,2},{1,5},{3,7},{5,1},{7,3},{8,12},{10,14},{12... | collective-permute-start | bytes 368648 | tf_op jit(solution)/shard_map/ppermute | solution.py:181
  8.7 8.1 %collective-permute-start.5 = (bf16[6,80,128]{2,1,0:T(8,128)(2,1)S(1)}, bf16[6,80,128]{2,1,0:T(8,128)(2,1)S(1)}, u32[]{:S(2)}, u32[]{:S(2)}) collective-permute-start(bf16[6,80,128]{2,1,0:T(8,128)(2,1)S(1)} %pack_piece.1), channel_id=1, source_target_pairs={{0,6},{2,0},{4,2},{6,4},{1,7},{3,1},{5,3},{7,5},{8,14},{10,8},{12,... | collective-permute-start | bytes 368648 | tf_op jit(solution)/shard_map/ppermute | solution.py:181
  17.3 8.0 %collective-permute-start.6 = (bf16[18,80,128]{2,1,0:T(8,128)(2,1)S(1)}, bf16[18,80,128]{2,1,0:T(8,128)(2,1)S(1)}, u32[]{:S(2)}, u32[]{:S(2)}) collective-permute-start(bf16[18,80,128]{2,1,0:T(8,128)(2,1)S(1)} %laid.8.refs_0_), channel_id=1, source_target_pairs={{0,1},{1,0},{2,3},{3,2},{4,5},{5,4},{6,7},{7,6},{8,24},{9,25},{10,... | collective-permute-start | bytes 1105928 | tf_op jit(solution)/shard_map/ppermute | solution.py:488
  18.9 13.5 %collective-permute-start.7 = (bf16[12,80,128]{2,1,0:T(8,128)(2,1)S(1)}, bf16[12,80,128]{2,1,0:T(8,128)(2,1)S(1)}, u32[]{:S(2)}, u32[]{:S(2)}) collective-permute-start(bf16[12,80,128]{2,1,0:T(8,128)(2,1)S(1)} %laid.7), channel_id=1, source_target_pairs={{0,2},{2,4},{4,6},{6,0},{1,3},{3,5},{5,7},{7,1},{8,10},{10,12},{12... | collective-permute-start | bytes 737288 | tf_op jit(solution)/shard_map/ppermute | solution.py:181
  22.0 26.3 %copy-start.9 = (f32[320]{0:T(512)S(1)}, f32[320]{0:T(512)}, u32[]{:S(2)}) copy-start(f32[320]{0:T(512)} %param.13) | copy-start | bytes 3844
  22.0 26.3 %copy-start.10 = (f32[320]{0:T(512)S(1)}, f32[320]{0:T(512)}, u32[]{:S(2)}) copy-start(f32[320]{0:T(512)} %param.15) | copy-start | bytes 3844
  22.1 9.3 %collective-permute-start = (bf16[4,64,320]{2,1,0:T(8,128)(2,1)S(1)}, bf16[4,64,320]{2,1,0:T(8,128)(2,1)S(1)}, u32[]{:S(2)}, u32[]{:S(2)}) collective-permute-start(bf16[4,64,320]{2,1,0:T(8,128)(2,1)S(1)} %dynamic-slice_bitcast_fusion), channel_id=1, source_target_pairs={{0,2},{2,4},{4,6},{1,3},{3,5},{5,7},{8,10},{10,12},{12,14},{9,11},... | collective-permute-start | bytes 491528 | tf_op jit(solution)/shard_map/ppermute | solution.py:468
  24.0 8.5 %collective-permute-start.1 = (bf16[4,64,320]{2,1,0:T(8,128)(2,1)S(1)}, bf16[4,64,320]{2,1,0:T(8,128)(2,1)S(1)}, u32[]{:S(2)}, u32[]{:S(2)}) collective-permute-start(bf16[4,64,320]{2,1,0:T(8,128)(2,1)S(1)} %dynamic-slice_bitcast_fusion), channel_id=1, source_target_pairs={{2,0},{4,2},{6,4},{3,1},{5,3},{7,5},{10,8},{12,10},{14,12},{11,9},... | collective-permute-start | bytes 491528 | tf_op jit(solution)/shard_map/ppermute | solution.py:469
  25.6 22.9 %copy-start.3 = (bf16[36,80,128]{2,1,0:T(8,128)(2,1)}, bf16[36,80,128]{2,1,0:T(8,128)(2,1)S(1)}, u32[]{:S(2)}) copy-start(bf16[36,80,128]{2,1,0:T(8,128)(2,1)S(1)} %laid.9.refs_1_) | copy-start | bytes 2211844
  32.4 15.8 %collective-permute-start.8 = (bf16[36,80,128]{2,1,0:T(8,128)(2,1)S(1)}, bf16[36,80,128]{2,1,0:T(8,128)(2,1)S(1)}, u32[]{:S(2)}, u32[]{:S(2)}) collective-permute-start(bf16[36,80,128]{2,1,0:T(8,128)(2,1)S(1)} %laid.9.refs_1_), channel_id=1, source_target_pairs={{0,16},{1,17},{2,18},{3,19},{4,20},{5,21},{6,22},{7,23},{8,9},{9,8... | collective-permute-start | bytes 2211848 | tf_op jit(solution)/shard_map/ppermute | solution.py:488
  33.2 15.0 %collective-permute-start.9 = (bf16[12,80,128]{2,1,0:T(8,128)(2,1)S(1)}, bf16[12,80,128]{2,1,0:T(8,128)(2,1)S(1)}, u32[]{:S(2)}, u32[]{:S(2)}) collective-permute-start(bf16[12,80,128]{2,1,0:T(8,128)(2,1)S(1)} %laid.7), channel_id=1, source_target_pairs={{0,4},{2,6},{4,0},{6,2},{1,5},{3,7},{5,1},{7,3},{8,12},{10,14},{12... | collective-permute-start | bytes 737288 | tf_op jit(solution)/shard_map/ppermute | solution.py:181
  34.7 13.5 %collective-permute-start.10 = (bf16[12,80,128]{2,1,0:T(8,128)(2,1)S(1)}, bf16[12,80,128]{2,1,0:T(8,128)(2,1)S(1)}, u32[]{:S(2)}, u32[]{:S(2)}) collective-permute-start(bf16[12,80,128]{2,1,0:T(8,128)(2,1)S(1)} %laid.7), channel_id=1, source_target_pairs={{0,6},{2,0},{4,2},{6,4},{1,7},{3,1},{5,3},{7,5},{8,14},{10,8},{12,... | collective-permute-start | bytes 737288 | tf_op jit(solution)/shard_map/ppermute | solution.py:181
  37.8 5.3 %collective-permute-start.2 = (bf16[12,8,320]{2,1,0:T(8,128)(2,1)S(1)}, bf16[12,8,320]{2,1,0:T(8,128)(2,1)S(1)}, u32[]{:S(2)}, u32[]{:S(2)}) collective-permute-start(bf16[12,8,320]{2,1,0:T(8,128)(2,1)S(1)} %slice_select_fusion), channel_id=1, source_target_pairs={{0,1},{1,0},{2,3},{3,2},{4,5},{5,4},{6,7},{7,6},{8,9},{9,8},{10,11... | collective-permute-start | bytes 184328 | tf_op jit(solution)/shard_map/ppermute | solution.py:473
  38.4 11.8 %collective-permute-start.11 = (bf16[36,80,128]{2,1,0:T(8,128)(2,1)S(1)}, bf16[36,80,128]{2,1,0:T(8,128)(2,1)S(1)}, u32[]{:S(2)}, u32[]{:S(2)}) collective-permute-start(bf16[36,80,128]{2,1,0:T(8,128)(2,1)S(1)} %laid.9.refs_1_), channel_id=1, source_target_pairs={{0,8},{8,0},{1,9},{9,1},{2,10},{10,2},{3,11},{11,3},{4,12},{12,4},... | collective-permute-start | bytes 2211848 | tf_op jit(solution)/shard_map/ppermute | solution.py:195
  48.2 2.3 %collective-permute-start.12 = (bf16[36,80,128]{2,1,0:T(8,128)(2,1)S(1)}, bf16[36,80,128]{2,1,0:T(8,128)(2,1)S(1)}, u32[]{:S(2)}, u32[]{:S(2)}) collective-permute-start(bf16[36,80,128]{2,1,0:T(8,128)(2,1)S(1)} %collective-permute-done.8.refs_2_), channel_id=1, source_target_pairs={{0,8},{8,0},{1,9},{9,1},{2,10},{10,2},{3,11},{11,3},{4,12},{12,4},... | collective-permute-start | bytes 2211848 | tf_op jit(solution)/shard_map/ppermute | solution.py:195
  49.3 10.4 %collective-permute-start.20 = (bf16[27,80,128]{2,1,0:T(8,128)(2,1)S(1)}, bf16[27,80,128]{2,1,0:T(8,128)(2,1)S(1)}, u32[]{:S(2)}, u32[]{:S(2)}) collective-permute-start(bf16[27,80,128]{2,1,0:T(8,128)(2,1)S(1)} %laid.12.refs_0_), channel_id=1, source_target_pairs={{0,1},{1,0},{2,3},{3,2},{4,5},{5,4},{6,7},{7,6},{8,24},{9,25},{10,... | collective-permute-start | bytes 1658888 | tf_op jit(solution)/shard_map/ppermute | solution.py:488
  59.7 14.7 %copy-start.6 = (bf16[9,320,160]{1,2,0:T(8,128)(2,1)S(1)}, bf16[9,320,160]{1,2,0:T(8,128)(2,1)}, u32[]{:S(2)}) copy-start(bf16[9,320,160]{1,2,0:T(8,128)(2,1)} %param.16) | copy-start | bytes 2764804
  60.9 19.6 %collective-permute-start.21 = (bf16[54,80,128]{2,1,0:T(8,128)(2,1)}, bf16[54,80,128]{2,1,0:T(8,128)(2,1)}, u32[]{:S(2)}, u32[]{:S(2)}) collective-permute-start(bf16[54,80,128]{2,1,0:T(8,128)(2,1)} %laid.13.refs_2_), channel_id=1, source_target_pairs={{0,16},{1,17},{2,18},{3,19},{4,20},{5,21},{6,22},{7,23},{8,9},{9,8... | collective-permute-start | bytes 3317768 | tf_op jit(solution)/shard_map/ppermute | solution.py:488
  61.2 9.4 %collective-permute-start.16 = (bf16[9,80,128]{2,1,0:T(8,128)(2,1)S(1)}, bf16[9,80,128]{2,1,0:T(8,128)(2,1)S(1)}, u32[]{:S(2)}, u32[]{:S(2)}) collective-permute-start(bf16[9,80,128]{2,1,0:T(8,128)(2,1)S(1)} %laid.10.refs_0_), channel_id=1, source_target_pairs={{0,1},{1,0},{2,3},{3,2},{4,5},{5,4},{6,7},{7,6},{8,24},{9,25},{10,... | collective-permute-start | bytes 552968 | tf_op jit(solution)/shard_map/ppermute | solution.py:488
  62.4 8.7 %collective-permute-start.13 = (bf16[2,48,384]{2,1,0:T(8,128)(2,1)S(1)}, bf16[2,48,384]{2,1,0:T(8,128)(2,1)S(1)}, u32[]{:S(2)}, u32[]{:S(2)}) collective-permute-start(bf16[2,48,384]{2,1,0:T(8,128)(2,1)S(1)} %get-tuple-element.41.own), channel_id=1, source_target_pairs={{0,2},{2,4},{4,6},{6,0},{1,3},{3,5},{5,7},{7,1},{8,10},{10,12},{12... | collective-permute-start | bytes 221192 | tf_op jit(solution)/shard_map/ppermute | solution.py:531
  67.5 6.4 %collective-permute-start.14 = (bf16[2,48,384]{2,1,0:T(8,128)(2,1)S(1)}, bf16[2,48,384]{2,1,0:T(8,128)(2,1)S(1)}, u32[]{:S(2)}, u32[]{:S(2)}) collective-permute-start(bf16[2,48,384]{2,1,0:T(8,128)(2,1)S(1)} %get-tuple-element.41.own), channel_id=1, source_target_pairs={{0,4},{2,6},{4,0},{6,2},{1,5},{3,7},{5,1},{7,3},{8,12},{10,14},{12... | collective-permute-start | bytes 221192 | tf_op jit(solution)/shard_map/ppermute | solution.py:531
  68.8 5.6 %collective-permute-start.15 = (bf16[2,48,384]{2,1,0:T(8,128)(2,1)S(1)}, bf16[2,48,384]{2,1,0:T(8,128)(2,1)S(1)}, u32[]{:S(2)}, u32[]{:S(2)}) collective-permute-start(bf16[2,48,384]{2,1,0:T(8,128)(2,1)S(1)} %get-tuple-element.41.own), channel_id=1, source_target_pairs={{0,6},{2,0},{4,2},{6,4},{1,7},{3,1},{5,3},{7,5},{8,14},{10,8},{12,... | collective-permute-start | bytes 221192 | tf_op jit(solution)/shard_map/ppermute | solution.py:531
  76.4 7.6 %collective-permute-start.17 = (bf16[4,48,256]{2,1,0:T(8,128)(2,1)S(1)}, bf16[4,48,256]{2,1,0:T(8,128)(2,1)S(1)}, u32[]{:S(2)}, u32[]{:S(2)}) collective-permute-start(bf16[4,48,256]{2,1,0:T(8,128)(2,1)S(1)} %get-tuple-element.47), channel_id=1, source_target_pairs={{0,2},{2,4},{4,6},{6,0},{1,3},{3,5},{5,7},{7,1},{8,10},{10,12},{12... | collective-permute-start | bytes 294920 | tf_op jit(solution)/shard_map/ppermute | solution.py:557
  77.9 8.7 %collective-permute-start.18 = (bf16[4,48,256]{2,1,0:T(8,128)(2,1)S(1)}, bf16[4,48,256]{2,1,0:T(8,128)(2,1)S(1)}, u32[]{:S(2)}, u32[]{:S(2)}) collective-permute-start(bf16[4,48,256]{2,1,0:T(8,128)(2,1)S(1)} %get-tuple-element.48), channel_id=1, source_target_pairs={{0,4},{2,6},{4,0},{6,2},{1,5},{3,7},{5,1},{7,3},{8,12},{10,14},{12... | collective-permute-start | bytes 294920 | tf_op jit(solution)/shard_map/ppermute | solution.py:557
  79.6 7.0 %collective-permute-start.19 = (bf16[4,48,256]{2,1,0:T(8,128)(2,1)S(1)}, bf16[4,48,256]{2,1,0:T(8,128)(2,1)S(1)}, u32[]{:S(2)}, u32[]{:S(2)}) collective-permute-start(bf16[4,48,256]{2,1,0:T(8,128)(2,1)S(1)} %get-tuple-element.49), channel_id=1, source_target_pairs={{0,6},{2,0},{4,2},{6,4},{1,7},{3,1},{5,3},{7,5},{8,14},{10,8},{12,... | collective-permute-start | bytes 294920 | tf_op jit(solution)/shard_map/ppermute | solution.py:557
  80.4 7.7 %collective-permute-start.22 = (bf16[54,80,128]{2,1,0:T(8,128)(2,1)S(1)}, bf16[54,80,128]{2,1,0:T(8,128)(2,1)S(1)}, u32[]{:S(2)}, u32[]{:S(2)}) collective-permute-start(bf16[54,80,128]{2,1,0:T(8,128)(2,1)S(1)} %copy-done.8), channel_id=1, source_target_pairs={{0,8},{8,0},{1,9},{9,1},{2,10},{10,2},{3,11},{11,3},{4,12},{12,4},... | collective-permute-start | bytes 3317768 | tf_op jit(solution)/shard_map/ppermute | solution.py:195
  80.5 7.6 %collective-permute-start.24 = (bf16[18,80,128]{2,1,0:T(8,128)(2,1)S(1)}, bf16[18,80,128]{2,1,0:T(8,128)(2,1)S(1)}, u32[]{:S(2)}, u32[]{:S(2)}) collective-permute-start(bf16[18,80,128]{2,1,0:T(8,128)(2,1)S(1)} %laid.11.refs_1_), channel_id=1, source_target_pairs={{0,16},{1,17},{2,18},{3,19},{4,20},{5,21},{6,22},{7,23},{8,9},{9,8... | collective-permute-start | bytes 1105928 | tf_op jit(solution)/shard_map/ppermute | solution.py:488
  84.0 15.2 %collective-permute-start.25 = (bf16[18,80,128]{2,1,0:T(8,128)(2,1)S(1)}, bf16[18,80,128]{2,1,0:T(8,128)(2,1)S(1)}, u32[]{:S(2)}, u32[]{:S(2)}) collective-permute-start(bf16[18,80,128]{2,1,0:T(8,128)(2,1)S(1)} %laid.11.refs_1_), channel_id=1, source_target_pairs={{0,8},{8,0},{1,9},{9,1},{2,10},{10,2},{3,11},{11,3},{4,12},{12,4},... | collective-permute-start | bytes 1105928 | tf_op jit(solution)/shard_map/ppermute | solution.py:195
  86.6 3.0 %collective-permute-start.23 = (bf16[54,80,128]{2,1,0:T(8,128)(2,1)}, bf16[54,80,128]{2,1,0:T(8,128)(2,1)S(1)}, u32[]{:S(2)}, u32[]{:S(2)}) collective-permute-start(bf16[54,80,128]{2,1,0:T(8,128)(2,1)} %collective-permute-done.21.refs_3_), channel_id=1, source_target_pairs={{0,8},{8,0},{1,9},{9,1},{2,10},{10,2},{3,11},{11,3},{4,12},{12,4},... | collective-permute-start | bytes 3317768 | tf_op jit(solution)/shard_map/ppermute | solution.py:195
  88.1 11.2 %collective-permute-start.26 = (bf16[18,80,128]{2,1,0:T(8,128)(2,1)S(1)}, bf16[18,80,128]{2,1,0:T(8,128)(2,1)S(1)}, u32[]{:S(2)}, u32[]{:S(2)}) collective-permute-start(bf16[18,80,128]{2,1,0:T(8,128)(2,1)S(1)} %collective-permute-done.24.refs_2_), channel_id=1, source_target_pairs={{0,8},{8,0},{1,9},{9,1},{2,10},{10,2},{3,11},{11,3},{4,12},{12,4},... | collective-permute-start | bytes 1105928 | tf_op jit(solution)/shard_map/ppermute | solution.py:195
  (13 other events, 48.2 us)

commit v5 on v4

--- a/solution.py
+++ b/solution.py
@@ -20,7 +20,7 @@
 
 
 def params():
-    return pltpu.CompilerParams(vmem_limit_bytes=52 * 1024 * 1024)
+    return pltpu.CompilerParams(vmem_limit_bytes=36 * 1024 * 1024)
 
 
 def cost(cells):

time: 103 us -> 99.4 us (0.965)
  Pallas kernels: 31.8 us -> 27.5 us
  local copies, waits for them, and re-layouts: 6.15 us -> 8.24 us
    pallas_call x1, Pallas kernels: 8.64 us -> 7.05 us  [shards(): pl.pallas_call(functools.partial(joined_body, size, sets, groups[1][1]),...]
    unnamed x38 -> x40, local copies, waits for them, and re-layouts: 5.32 us -> 6.49 us
    pallas_call x3, Pallas kernels: 4.31 us -> 3.15 us  [pack(): pl.pallas_call(functools.partial(pack_body, layouts, parts), out_shape=[j...]
  transfers between devices with their start and end apart: 27 -> 27, of which waited for: 12 -> 14; matrix products, arithmetic and copies ran while one was open for 1% -> 4% of each run, Pallas kernels for 25% -> 23%
where the time goes in v5:
time: 99.4 us; the launch traced here: 99 us
  starting transfers between devices  35.2 us (35%)
  Pallas kernels  27.5 us (28%)
  waiting for transfers between devices  27.2 us (27%)
  local copies, waits for them, and re-layouts  8.24 us (8%)
    ppermute x6, starting transfers between devices, from_planes(): lax.ppermute(mine, 'row', cyclic(count, by))  14.5 us
    pallas_call x1, Pallas kernels, shards(): pl.pallas_call(functools.partial(encoder_body, size, sets, groups[0][1]),...  7.67 us
    pallas_call x1, Pallas kernels, shards(): pl.pallas_call(functools.partial(joined_body, size, sets, groups[1][1]),...  7.05 us
    ppermute x3, starting transfers between devices, shards(): lax.ppermute(pooled, 'row', cyclic(row_count, by))  6.88 us
    unnamed x40, local copies, waits for them, and re-layouts  6.49 us
    ppermute x6, starting transfers between devices, shards(): across = lambda block, pairs: lax.ppermute(block, AXES, pairs)  5.86 us
    ppermute x1, waiting for transfers between devices, shards(): above = lax.ppermute(tile, 'row', down)  5.57 us
    ppermute x6, waiting for transfers between devices, from_planes(): lax.ppermute(mine, 'row', cyclic(count, by))  5.39 us
  transfers between devices with their start and end apart: 27, of which 14 were waited for; matrix products, arithmetic and copies ran while one was open for 4% of the time, Pallas kernels for 23%

profile of v5, /device:TPU:0, one launch (start us, length us, event | category | flops | bytes accessed | tf_op | source)
XLA Modules:
  0.0 99.0 jit_solution(7720197691103387463)
XLA Ops:
  0.1 1.1 %copy-done.1 = bf16[9,320,80]{1,2,0:T(8,128)(2,1)S(1)} copy-done((bf16[9,320,80]{1,2,0:T(8,128)(2,1)S(1)}, bf16[9,320,80]{1,2,0:T(8,128)(2,1)}, u32[]{:S(2)}) %copy-start.1) | copy-done | bytes 460824
  3.0 3.1 %collective-permute-start.3 = (bf16[6,80,128]{2,1,0:T(8,128)(2,1)S(1)}, bf16[6,80,128]{2,1,0:T(8,128)(2,1)S(1)}, u32[]{:S(2)}, u32[]{:S(2)}) collective-permute-start(bf16[6,80,128]{2,1,0:T(8,128)(2,1)S(1)} %pack_piece.1), channel_id=1, source_target_pairs={{0,2},{2,4},{4,6},{6,0},{1,3},{3,5},{5,7},{7,1},{8,10},{10,12},{12... | collective-permute-start | bytes 368648 | tf_op jit(solution)/shard_map/ppermute | solution.py:181
  6.1 2.6 %collective-permute-start.4 = (bf16[6,80,128]{2,1,0:T(8,128)(2,1)S(1)}, bf16[6,80,128]{2,1,0:T(8,128)(2,1)S(1)}, u32[]{:S(2)}, u32[]{:S(2)}) collective-permute-start(bf16[6,80,128]{2,1,0:T(8,128)(2,1)S(1)} %pack_piece.1), channel_id=1, source_target_pairs={{0,4},{2,6},{4,0},{6,2},{1,5},{3,7},{5,1},{7,3},{8,12},{10,14},{12... | collective-permute-start | bytes 368648 | tf_op jit(solution)/shard_map/ppermute | solution.py:181
  8.7 1.3 %collective-permute-start.5 = (bf16[6,80,128]{2,1,0:T(8,128)(2,1)S(1)}, bf16[6,80,128]{2,1,0:T(8,128)(2,1)S(1)}, u32[]{:S(2)}, u32[]{:S(2)}) collective-permute-start(bf16[6,80,128]{2,1,0:T(8,128)(2,1)S(1)} %pack_piece.1), channel_id=1, source_target_pairs={{0,6},{2,0},{4,2},{6,4},{1,7},{3,1},{5,3},{7,5},{8,14},{10,8},{12,... | collective-permute-start | bytes 368648 | tf_op jit(solution)/shard_map/ppermute | solution.py:181
  10.0 1.4 %pack_weights.3 = (bf16[48,80,128]{2,1,0:T(8,128)(2,1)S(1)}, bf16[6,80,128]{2,1,0:T(8,128)(2,1)}) custom-call(s32[4]{0:T(128)S(1)} %pad_add_fusion.place, bf16[9,80,320]{2,1,0:T(8,128)(2,1)S(1)} %bitcast.14, bf16[9,80,320]{2,1,0:T(8,128)(2,1)S(1)} %bitcast.16), custom_call_target="tpu_custom_call" | custom-call | tf_op jit(solution)/shard_map/pack_weights/pallas_call | solution.py:75
  11.4 1.2 %pack_weights.4 = (bf16[72,80,128]{2,1,0:T(8,128)(2,1)S(1)}, bf16[9,80,128]{2,1,0:T(8,128)(2,1)S(1)}) custom-call(s32[4]{0:T(128)S(1)} %pad_add_fusion.place, bf16[9,80,960]{2,1,0:T(8,128)(2,1)S(1)} %bitcast.17), custom_call_target="tpu_custom_call" | custom-call | tf_op jit(solution)/shard_map/pack_weights/pallas_call | solution.py:75
  12.6 1.1 %copy-done.5 = bf16[72,80,128]{2,1,0:T(8,128)(2,1)} copy-done((bf16[72,80,128]{2,1,0:T(8,128)(2,1)}, bf16[72,80,128]{2,1,0:T(8,128)(2,1)S(1)}, u32[]{:S(2)}) %copy-start.5) | copy-done | bytes 1474584
  14.7 2.1 %collective-permute-done.4.refs_1_ = bf16[6,80,128]{2,1,0:T(8,128)(2,1)S(1)} collective-permute-done((bf16[6,80,128]{2,1,0:T(8,128)(2,1)S(1)}, bf16[6,80,128]{2,1,0:T(8,128)(2,1)S(1)}, u32[]{:S(2)}, u32[]{:S(2)}) %collective-permute-start.4) | collective-permute-done | bytes 122912 | tf_op jit(solution)/shard_map/ppermute | solution.py:181
  17.3 1.6 %collective-permute-start.6 = (bf16[18,80,128]{2,1,0:T(8,128)(2,1)S(1)}, bf16[18,80,128]{2,1,0:T(8,128)(2,1)S(1)}, u32[]{:S(2)}, u32[]{:S(2)}) collective-permute-start(bf16[18,80,128]{2,1,0:T(8,128)(2,1)S(1)} %laid.8.refs_0_), channel_id=1, source_target_pairs={{0,1},{1,0},{2,3},{3,2},{4,5},{5,4},{6,7},{7,6},{8,24},{9,25},{10,... | collective-permute-start | bytes 1105928 | tf_op jit(solution)/shard_map/ppermute | solution.py:488
  18.9 3.1 %collective-permute-start.7 = (bf16[12,80,128]{2,1,0:T(8,128)(2,1)S(1)}, bf16[12,80,128]{2,1,0:T(8,128)(2,1)S(1)}, u32[]{:S(2)}, u32[]{:S(2)}) collective-permute-start(bf16[12,80,128]{2,1,0:T(8,128)(2,1)S(1)} %laid.7), channel_id=1, source_target_pairs={{0,2},{2,4},{4,6},{6,0},{1,3},{3,5},{5,7},{7,1},{8,10},{10,12},{12... | collective-permute-start | bytes 737288 | tf_op jit(solution)/shard_map/ppermute | solution.py:181
  22.1 2.1 %collective-permute-start = (bf16[4,64,320]{2,1,0:T(8,128)(2,1)S(1)}, bf16[4,64,320]{2,1,0:T(8,128)(2,1)S(1)}, u32[]{:S(2)}, u32[]{:S(2)}) collective-permute-start(bf16[4,64,320]{2,1,0:T(8,128)(2,1)S(1)} %dynamic-slice_bitcast_fusion), channel_id=1, source_target_pairs={{0,2},{2,4},{4,6},{1,3},{3,5},{5,7},{8,10},{10,12},{12,14},{9,11},... | collective-permute-start | bytes 491528 | tf_op jit(solution)/shard_map/ppermute | solution.py:468
  24.1 1.3 %collective-permute-start.1 = (bf16[4,64,320]{2,1,0:T(8,128)(2,1)S(1)}, bf16[4,64,320]{2,1,0:T(8,128)(2,1)S(1)}, u32[]{:S(2)}, u32[]{:S(2)}) collective-permute-start(bf16[4,64,320]{2,1,0:T(8,128)(2,1)S(1)} %dynamic-slice_bitcast_fusion), channel_id=1, source_target_pairs={{2,0},{4,2},{6,4},{3,1},{5,3},{7,5},{10,8},{12,10},{14,12},{11,9},... | collective-permute-start | bytes 491528 | tf_op jit(solution)/shard_map/ppermute | solution.py:469
  25.8 5.6 %collective-permute-done = bf16[4,64,320]{2,1,0:T(8,128)(2,1)S(1)} collective-permute-done((bf16[4,64,320]{2,1,0:T(8,128)(2,1)S(1)}, bf16[4,64,320]{2,1,0:T(8,128)(2,1)S(1)}, u32[]{:S(2)}, u32[]{:S(2)}) %collective-permute-start) | collective-permute-done | bytes 163872 | tf_op jit(solution)/shard_map/ppermute | solution.py:468
  31.4 1.1 %collective-permute-done.1 = bf16[4,64,320]{2,1,0:T(8,128)(2,1)S(1)} collective-permute-done((bf16[4,64,320]{2,1,0:T(8,128)(2,1)S(1)}, bf16[4,64,320]{2,1,0:T(8,128)(2,1)S(1)}, u32[]{:S(2)}, u32[]{:S(2)}) %collective-permute-start.1) | collective-permute-done | bytes 163872 | tf_op jit(solution)/shard_map/ppermute | solution.py:469
  33.4 1.5 %collective-permute-start.9 = (bf16[12,80,128]{2,1,0:T(8,128)(2,1)S(1)}, bf16[12,80,128]{2,1,0:T(8,128)(2,1)S(1)}, u32[]{:S(2)}, u32[]{:S(2)}) collective-permute-start(bf16[12,80,128]{2,1,0:T(8,128)(2,1)S(1)} %laid.7), channel_id=1, source_target_pairs={{0,4},{2,6},{4,0},{6,2},{1,5},{3,7},{5,1},{7,3},{8,12},{10,14},{12... | collective-permute-start | bytes 737288 | tf_op jit(solution)/shard_map/ppermute | solution.py:181
  34.9 2.9 %collective-permute-start.10 = (bf16[12,80,128]{2,1,0:T(8,128)(2,1)S(1)}, bf16[12,80,128]{2,1,0:T(8,128)(2,1)S(1)}, u32[]{:S(2)}, u32[]{:S(2)}) collective-permute-start(bf16[12,80,128]{2,1,0:T(8,128)(2,1)S(1)} %laid.7), channel_id=1, source_target_pairs={{0,6},{2,0},{4,2},{6,4},{1,7},{3,1},{5,3},{7,5},{8,14},{10,8},{12,... | collective-permute-start | bytes 737288 | tf_op jit(solution)/shard_map/ppermute | solution.py:181
  41.3 3.8 %collective-permute-done.2 = bf16[12,8,320]{2,1,0:T(8,128)(2,1)S(1)} collective-permute-done((bf16[12,8,320]{2,1,0:T(8,128)(2,1)S(1)}, bf16[12,8,320]{2,1,0:T(8,128)(2,1)S(1)}, u32[]{:S(2)}, u32[]{:S(2)}) %collective-permute-start.2) | collective-permute-done | bytes 61472 | tf_op jit(solution)/shard_map/ppermute | solution.py:473
  45.1 3.3 %collective-permute-done.9.refs_1_ = bf16[12,80,128]{2,1,0:T(8,128)(2,1)S(1)} collective-permute-done((bf16[12,80,128]{2,1,0:T(8,128)(2,1)S(1)}, bf16[12,80,128]{2,1,0:T(8,128)(2,1)S(1)}, u32[]{:S(2)}, u32[]{:S(2)}) %collective-permute-start.9) | collective-permute-done | bytes 245792 | tf_op jit(solution)/shard_map/ppermute | solution.py:181
  50.8 7.7 %encoder.1 = (bf16[640,384]{1,0:T(8,128)(2,1)S(1)}, bf16[2,48,384]{2,1,0:T(8,128)(2,1)S(1)}) custom-call(s32[4]{0:T(128)S(1)} %pad_add_fusion.place, bf16[960,384]{1,0:T(8,128)(2,1)S(1)} %bitcast.18, f32[1,320]{1,0:T(1,128)S(1)} %reshape.19.bias1, f32[1,320]{1,0:T(1,128)S(1)} %reshape.20.bias2, bf16[48,80,128]{2,1,0:T(8,128)(2,1)S(1)} %get-tuple-element.32.refs_0_, ...), custom_call_target="tpu_custom_call" | custom-call | flops 21233664000 | bytes 1048576 | tf_op jit(solution)/shard_map/encoder/pallas_call | solution.py:510
  60.3 4.5 %collective-permute-start.13 = (bf16[2,48,384]{2,1,0:T(8,128)(2,1)S(1)}, bf16[2,48,384]{2,1,0:T(8,128)(2,1)S(1)}, u32[]{:S(2)}, u32[]{:S(2)}) collective-permute-start(bf16[2,48,384]{2,1,0:T(8,128)(2,1)S(1)} %get-tuple-element.41.own), channel_id=1, source_target_pairs={{0,2},{2,4},{4,6},{6,0},{1,3},{3,5},{5,7},{7,1},{8,10},{10,12},{12... | collective-permute-start | bytes 221192 | tf_op jit(solution)/shard_map/ppermute | solution.py:531
  64.8 1.5 %collective-permute-start.14 = (bf16[2,48,384]{2,1,0:T(8,128)(2,1)S(1)}, bf16[2,48,384]{2,1,0:T(8,128)(2,1)S(1)}, u32[]{:S(2)}, u32[]{:S(2)}) collective-permute-start(bf16[2,48,384]{2,1,0:T(8,128)(2,1)S(1)} %get-tuple-element.41.own), channel_id=1, source_target_pairs={{0,4},{2,6},{4,0},{6,2},{1,5},{3,7},{5,1},{7,3},{8,12},{10,14},{12... | collective-permute-start | bytes 221192 | tf_op jit(solution)/shard_map/ppermute | solution.py:531
  68.5 2.7 %collective-permute-done.14.refs_1_ = bf16[2,48,384]{2,1,0:T(8,128)(2,1)S(1)} collective-permute-done((bf16[2,48,384]{2,1,0:T(8,128)(2,1)S(1)}, bf16[2,48,384]{2,1,0:T(8,128)(2,1)S(1)}, u32[]{:S(2)}, u32[]{:S(2)}) %collective-permute-start.14) | collective-permute-done | bytes 73760 | tf_op jit(solution)/shard_map/ppermute | solution.py:531
  71.8 1.2 %copy-done.7 = bf16[9,320,160]{1,2,0:T(8,128)(2,1)S(1)} copy-done((bf16[9,320,160]{1,2,0:T(8,128)(2,1)S(1)}, bf16[9,320,160]{1,2,0:T(8,128)(2,1)}, u32[]{:S(2)}) %copy-start.7) | copy-done | bytes 921624
  73.1 2.0 %middle.1 = (bf16[4,48,256]{2,1,0:T(8,128)(2,1)S(1)}, bf16[4,48,256]{2,1,0:T(8,128)(2,1)S(1)}, bf16[4,48,256]{2,1,0:T(8,128)(2,1)S(1)}, bf16[4,48,256]{2,1,0:T(8,128)(2,1)S(1)}) custom-call(s32[4]{0:T(128)S(1)} %pad_add_fusion.place, bf16[2,48,384]{2,1,0:T(8,128)(2,1)S(1)} %get-tuple-element.41.own, bf16[2,48,384]{2,1,0:T(8,128)(2,1)S(1)} %collective-permute-done.13.refs_0_, ...), custom_call_target="tpu_custom_call" | custom-call | flops 4718592000 | bytes 1048576 | tf_op jit(solution)/shard_map/middle/pallas_call | solution.py:541
  75.0 1.5 %collective-permute-start.17 = (bf16[4,48,256]{2,1,0:T(8,128)(2,1)S(1)}, bf16[4,48,256]{2,1,0:T(8,128)(2,1)S(1)}, u32[]{:S(2)}, u32[]{:S(2)}) collective-permute-start(bf16[4,48,256]{2,1,0:T(8,128)(2,1)S(1)} %get-tuple-element.47), channel_id=1, source_target_pairs={{0,2},{2,4},{4,6},{6,0},{1,3},{3,5},{5,7},{7,1},{8,10},{10,12},{12... | collective-permute-start | bytes 294920 | tf_op jit(solution)/shard_map/ppermute | solution.py:557
  76.6 1.5 %collective-permute-start.18 = (bf16[4,48,256]{2,1,0:T(8,128)(2,1)S(1)}, bf16[4,48,256]{2,1,0:T(8,128)(2,1)S(1)}, u32[]{:S(2)}, u32[]{:S(2)}) collective-permute-start(bf16[4,48,256]{2,1,0:T(8,128)(2,1)S(1)} %get-tuple-element.48), channel_id=1, source_target_pairs={{0,4},{2,6},{4,0},{6,2},{1,5},{3,7},{5,1},{7,3},{8,12},{10,14},{12... | collective-permute-start | bytes 294920 | tf_op jit(solution)/shard_map/ppermute | solution.py:557
  79.1 1.8 %collective-permute-start.24 = (bf16[18,80,128]{2,1,0:T(8,128)(2,1)S(1)}, bf16[18,80,128]{2,1,0:T(8,128)(2,1)S(1)}, u32[]{:S(2)}, u32[]{:S(2)}) collective-permute-start(bf16[18,80,128]{2,1,0:T(8,128)(2,1)S(1)} %laid.11.refs_1_), channel_id=1, source_target_pairs={{0,16},{1,17},{2,18},{3,19},{4,20},{5,21},{6,22},{7,23},{8,9},{9,8... | collective-permute-start | bytes 1105928 | tf_op jit(solution)/shard_map/ppermute | solution.py:488
  80.9 1.8 %collective-permute-done.17.refs_1_ = bf16[4,48,256]{2,1,0:T(8,128)(2,1)S(1)} collective-permute-done((bf16[4,48,256]{2,1,0:T(8,128)(2,1)S(1)}, bf16[4,48,256]{2,1,0:T(8,128)(2,1)S(1)}, u32[]{:S(2)}, u32[]{:S(2)}) %collective-permute-start.17) | collective-permute-done | bytes 98336 | tf_op jit(solution)/shard_map/ppermute | solution.py:557
  82.7 2.6 %collective-permute-done.18.refs_2_ = bf16[4,48,256]{2,1,0:T(8,128)(2,1)S(1)} collective-permute-done((bf16[4,48,256]{2,1,0:T(8,128)(2,1)S(1)}, bf16[4,48,256]{2,1,0:T(8,128)(2,1)S(1)}, u32[]{:S(2)}, u32[]{:S(2)}) %collective-permute-start.18) | collective-permute-done | bytes 98336 | tf_op jit(solution)/shard_map/ppermute | solution.py:557
  86.7 1.5 %collective-permute-done.23.refs_5_ = bf16[54,80,128]{2,1,0:T(8,128)(2,1)S(1)} collective-permute-done((bf16[54,80,128]{2,1,0:T(8,128)(2,1)}, bf16[54,80,128]{2,1,0:T(8,128)(2,1)S(1)}, u32[]{:S(2)}, u32[]{:S(2)}) %collective-permute-start.23) | collective-permute-done | bytes 1105952 | tf_op jit(solution)/shard_map/ppermute | solution.py:195
  88.2 7.1 %joined.1.refined = bf16[480,384]{1,0:T(8,128)(2,1)S(1)} custom-call(s32[4]{0:T(128)S(1)} %pad_add_fusion.place, bf16[640,384]{1,0:T(8,128)(2,1)S(1)} %copy-done.11, f32[1,320]{1,0:T(1,128)S(1)} %reshape.21.bias, bf16[5,4,48,128]{3,2,1,0:T(8,128)(2,1)S(1)} %field.1.refs_0_, bf16[72,80,128]{2,1,0:T(8,128)(2,1)S(1)} %copy-done.6, ...), custom_call_target="tpu_custom_call" | custom-call | flops 10616832000 | bytes 1048576 | tf_op jit(solution)/shard_map/joined/pallas_call | solution.py:595
  95.3 3.5 %last.1 = bf16[1,4,64,320]{3,2,1,0:T(8,128)(2,1)} custom-call(s32[4]{0:T(128)S(1)} %pad_add_fusion.place, bf16[480,384]{1,0:T(8,128)(2,1)S(1)} %joined.1.refined, f32[1,320]{1,0:T(1,128)S(1)} %reshape.23.bias, bf16[24,80,128]{2,1,0:T(8,128)(2,1)S(1)} %copy-done.9, bf16[18,80,128]{2,1,0:T(8,128)(2,1)S(1)} %laid.11.refs_1_, ...), custom_call_target="tpu_custom_call" | custom-call | flops 2359296000 | bytes 1048576 | tf_op jit(solution)/shard_map/last/pallas_call | solution.py:611
  (89 shorter events, 17.6 us)
Async XLA Ops:
  0.0 22.0 %copy-start = (bf16[2,4,64,320]{3,2,1,0:T(8,128)(2,1)S(1)}, bf16[2,4,64,320]{3,2,1,0:T(8,128)(2,1)}, u32[]{:S(2)}) copy-start(bf16[2,4,64,320]{3,2,1,0:T(8,128)(2,1)} %param.11) | copy-start | bytes 983044
  3.0 10.7 %copy-start.4 = (bf16[9,320,80]{1,2,0:T(8,128)(2,1)S(1)}, bf16[9,320,80]{1,2,0:T(8,128)(2,1)}, u32[]{:S(2)}) copy-start(bf16[9,320,80]{1,2,0:T(8,128)(2,1)} %param.20) | copy-start | bytes 1382404
  3.0 11.7 %collective-permute-start.3 = (bf16[6,80,128]{2,1,0:T(8,128)(2,1)S(1)}, bf16[6,80,128]{2,1,0:T(8,128)(2,1)S(1)}, u32[]{:S(2)}, u32[]{:S(2)}) collective-permute-start(bf16[6,80,128]{2,1,0:T(8,128)(2,1)S(1)} %pack_piece.1), channel_id=1, source_target_pairs={{0,2},{2,4},{4,6},{6,0},{1,3},{3,5},{5,7},{7,1},{8,10},{10,12},{12... | collective-permute-start | bytes 368648 | tf_op jit(solution)/shard_map/ppermute | solution.py:181
  6.1 10.7 %collective-permute-start.4 = (bf16[6,80,128]{2,1,0:T(8,128)(2,1)S(1)}, bf16[6,80,128]{2,1,0:T(8,128)(2,1)S(1)}, u32[]{:S(2)}, u32[]{:S(2)}) collective-permute-start(bf16[6,80,128]{2,1,0:T(8,128)(2,1)S(1)} %pack_piece.1), channel_id=1, source_target_pairs={{0,4},{2,6},{4,0},{6,2},{1,5},{3,7},{5,1},{7,3},{8,12},{10,14},{12... | collective-permute-start | bytes 368648 | tf_op jit(solution)/shard_map/ppermute | solution.py:181
  8.7 8.1 %collective-permute-start.5 = (bf16[6,80,128]{2,1,0:T(8,128)(2,1)S(1)}, bf16[6,80,128]{2,1,0:T(8,128)(2,1)S(1)}, u32[]{:S(2)}, u32[]{:S(2)}) collective-permute-start(bf16[6,80,128]{2,1,0:T(8,128)(2,1)S(1)} %pack_piece.1), channel_id=1, source_target_pairs={{0,6},{2,0},{4,2},{6,4},{1,7},{3,1},{5,3},{7,5},{8,14},{10,8},{12,... | collective-permute-start | bytes 368648 | tf_op jit(solution)/shard_map/ppermute | solution.py:181
  17.3 8.1 %collective-permute-start.6 = (bf16[18,80,128]{2,1,0:T(8,128)(2,1)S(1)}, bf16[18,80,128]{2,1,0:T(8,128)(2,1)S(1)}, u32[]{:S(2)}, u32[]{:S(2)}) collective-permute-start(bf16[18,80,128]{2,1,0:T(8,128)(2,1)S(1)} %laid.8.refs_0_), channel_id=1, source_target_pairs={{0,1},{1,0},{2,3},{3,2},{4,5},{5,4},{6,7},{7,6},{8,24},{9,25},{10,... | collective-permute-start | bytes 1105928 | tf_op jit(solution)/shard_map/ppermute | solution.py:488
  18.9 13.5 %collective-permute-start.7 = (bf16[12,80,128]{2,1,0:T(8,128)(2,1)S(1)}, bf16[12,80,128]{2,1,0:T(8,128)(2,1)S(1)}, u32[]{:S(2)}, u32[]{:S(2)}) collective-permute-start(bf16[12,80,128]{2,1,0:T(8,128)(2,1)S(1)} %laid.7), channel_id=1, source_target_pairs={{0,2},{2,4},{4,6},{6,0},{1,3},{3,5},{5,7},{7,1},{8,10},{10,12},{12... | collective-permute-start | bytes 737288 | tf_op jit(solution)/shard_map/ppermute | solution.py:181
  22.0 11.4 %copy-start.12 = (bf16[4,64,320]{2,1,0:T(8,128)(2,1)}, bf16[4,64,320]{2,1,0:T(8,128)(2,1)S(1)}, u32[]{:S(2)}) copy-start(bf16[4,64,320]{2,1,0:T(8,128)(2,1)S(1)} %dynamic-slice_bitcast_fusion) | copy-start | bytes 491524
  22.0 26.4 %copy-start.15 = (f32[320]{0:T(512)S(1)}, f32[320]{0:T(512)}, u32[]{:S(2)}) copy-start(f32[320]{0:T(512)} %param.13) | copy-start | bytes 3844
  22.1 26.4 %copy-start.16 = (f32[320]{0:T(512)S(1)}, f32[320]{0:T(512)}, u32[]{:S(2)}) copy-start(f32[320]{0:T(512)} %param.15) | copy-start | bytes 3844
  22.1 9.3 %collective-permute-start = (bf16[4,64,320]{2,1,0:T(8,128)(2,1)S(1)}, bf16[4,64,320]{2,1,0:T(8,128)(2,1)S(1)}, u32[]{:S(2)}, u32[]{:S(2)}) collective-permute-start(bf16[4,64,320]{2,1,0:T(8,128)(2,1)S(1)} %dynamic-slice_bitcast_fusion), channel_id=1, source_target_pairs={{0,2},{2,4},{4,6},{1,3},{3,5},{5,7},{8,10},{10,12},{12,14},{9,11},... | collective-permute-start | bytes 491528 | tf_op jit(solution)/shard_map/ppermute | solution.py:468
  24.1 8.3 %collective-permute-start.1 = (bf16[4,64,320]{2,1,0:T(8,128)(2,1)S(1)}, bf16[4,64,320]{2,1,0:T(8,128)(2,1)S(1)}, u32[]{:S(2)}, u32[]{:S(2)}) collective-permute-start(bf16[4,64,320]{2,1,0:T(8,128)(2,1)S(1)} %dynamic-slice_bitcast_fusion), channel_id=1, source_target_pairs={{2,0},{4,2},{6,4},{3,1},{5,3},{7,5},{10,8},{12,10},{14,12},{11,9},... | collective-permute-start | bytes 491528 | tf_op jit(solution)/shard_map/ppermute | solution.py:469
  32.5 15.9 %collective-permute-start.8 = (bf16[36,80,128]{2,1,0:T(8,128)(2,1)S(1)}, bf16[36,80,128]{2,1,0:T(8,128)(2,1)}, u32[]{:S(2)}, u32[]{:S(2)}) collective-permute-start(bf16[36,80,128]{2,1,0:T(8,128)(2,1)S(1)} %laid.9.refs_1_), channel_id=1, source_target_pairs={{0,16},{1,17},{2,18},{3,19},{4,20},{5,21},{6,22},{7,23},{8,9},{9,8... | collective-permute-start | bytes 2211848 | tf_op jit(solution)/shard_map/ppermute | solution.py:488
  33.4 15.0 %collective-permute-start.9 = (bf16[12,80,128]{2,1,0:T(8,128)(2,1)S(1)}, bf16[12,80,128]{2,1,0:T(8,128)(2,1)S(1)}, u32[]{:S(2)}, u32[]{:S(2)}) collective-permute-start(bf16[12,80,128]{2,1,0:T(8,128)(2,1)S(1)} %laid.7), channel_id=1, source_target_pairs={{0,4},{2,6},{4,0},{6,2},{1,5},{3,7},{5,1},{7,3},{8,12},{10,14},{12... | collective-permute-start | bytes 737288 | tf_op jit(solution)/shard_map/ppermute | solution.py:181
  34.9 13.5 %collective-permute-start.10 = (bf16[12,80,128]{2,1,0:T(8,128)(2,1)S(1)}, bf16[12,80,128]{2,1,0:T(8,128)(2,1)S(1)}, u32[]{:S(2)}, u32[]{:S(2)}) collective-permute-start(bf16[12,80,128]{2,1,0:T(8,128)(2,1)S(1)} %laid.7), channel_id=1, source_target_pairs={{0,6},{2,0},{4,2},{6,4},{1,7},{3,1},{5,3},{7,5},{8,14},{10,8},{12,... | collective-permute-start | bytes 737288 | tf_op jit(solution)/shard_map/ppermute | solution.py:181
  40.7 4.4 %collective-permute-start.2 = (bf16[12,8,320]{2,1,0:T(8,128)(2,1)S(1)}, bf16[12,8,320]{2,1,0:T(8,128)(2,1)S(1)}, u32[]{:S(2)}, u32[]{:S(2)}) collective-permute-start(bf16[12,8,320]{2,1,0:T(8,128)(2,1)S(1)} %slice_select_fusion), channel_id=1, source_target_pairs={{0,1},{1,0},{2,3},{3,2},{4,5},{5,4},{6,7},{7,6},{8,9},{9,8},{10,11... | collective-permute-start | bytes 184328 | tf_op jit(solution)/shard_map/ppermute | solution.py:473
  41.3 8.9 %collective-permute-start.11 = (bf16[36,80,128]{2,1,0:T(8,128)(2,1)S(1)}, bf16[36,80,128]{2,1,0:T(8,128)(2,1)S(1)}, u32[]{:S(2)}, u32[]{:S(2)}) collective-permute-start(bf16[36,80,128]{2,1,0:T(8,128)(2,1)S(1)} %laid.9.refs_1_), channel_id=1, source_target_pairs={{0,8},{8,0},{1,9},{9,1},{2,10},{10,2},{3,11},{11,3},{4,12},{12,4},... | collective-permute-start | bytes 2211848 | tf_op jit(solution)/shard_map/ppermute | solution.py:195
  48.4 2.4 %collective-permute-start.12 = (bf16[36,80,128]{2,1,0:T(8,128)(2,1)}, bf16[36,80,128]{2,1,0:T(8,128)(2,1)S(1)}, u32[]{:S(2)}, u32[]{:S(2)}) collective-permute-start(bf16[36,80,128]{2,1,0:T(8,128)(2,1)} %collective-permute-done.8.refs_2_), channel_id=1, source_target_pairs={{0,8},{8,0},{1,9},{9,1},{2,10},{10,2},{3,11},{11,3},{4,12},{12,4},... | collective-permute-start | bytes 2211848 | tf_op jit(solution)/shard_map/ppermute | solution.py:195
  49.4 9.6 %collective-permute-start.20 = (bf16[27,80,128]{2,1,0:T(8,128)(2,1)S(1)}, bf16[27,80,128]{2,1,0:T(8,128)(2,1)S(1)}, u32[]{:S(2)}, u32[]{:S(2)}) collective-permute-start(bf16[27,80,128]{2,1,0:T(8,128)(2,1)S(1)} %laid.12.refs_0_), channel_id=1, source_target_pairs={{0,1},{1,0},{2,3},{3,2},{4,5},{5,4},{6,7},{7,6},{8,24},{9,25},{10,... | collective-permute-start | bytes 1658888 | tf_op jit(solution)/shard_map/ppermute | solution.py:488
  59.2 20.0 %collective-permute-start.21 = (bf16[54,80,128]{2,1,0:T(8,128)(2,1)S(1)}, bf16[54,80,128]{2,1,0:T(8,128)(2,1)}, u32[]{:S(2)}, u32[]{:S(2)}) collective-permute-start(bf16[54,80,128]{2,1,0:T(8,128)(2,1)S(1)} %laid.13.refs_2_), channel_id=1, source_target_pairs={{0,16},{1,17},{2,18},{3,19},{4,20},{5,21},{6,22},{7,23},{8,9},{9,8... | collective-permute-start | bytes 3317768 | tf_op jit(solution)/shard_map/ppermute | solution.py:488
  59.5 8.4 %collective-permute-start.16 = (bf16[9,80,128]{2,1,0:T(8,128)(2,1)S(1)}, bf16[9,80,128]{2,1,0:T(8,128)(2,1)S(1)}, u32[]{:S(2)}, u32[]{:S(2)}) collective-permute-start(bf16[9,80,128]{2,1,0:T(8,128)(2,1)S(1)} %laid.10.refs_0_), channel_id=1, source_target_pairs={{0,1},{1,0},{2,3},{3,2},{4,5},{5,4},{6,7},{7,6},{8,24},{9,25},{10,... | collective-permute-start | bytes 552968 | tf_op jit(solution)/shard_map/ppermute | solution.py:488
  60.3 8.3 %collective-permute-start.13 = (bf16[2,48,384]{2,1,0:T(8,128)(2,1)S(1)}, bf16[2,48,384]{2,1,0:T(8,128)(2,1)S(1)}, u32[]{:S(2)}, u32[]{:S(2)}) collective-permute-start(bf16[2,48,384]{2,1,0:T(8,128)(2,1)S(1)} %get-tuple-element.41.own), channel_id=1, source_target_pairs={{0,2},{2,4},{4,6},{6,0},{1,3},{3,5},{5,7},{7,1},{8,10},{10,12},{12... | collective-permute-start | bytes 221192 | tf_op jit(solution)/shard_map/ppermute | solution.py:531
  64.8 6.5 %collective-permute-start.14 = (bf16[2,48,384]{2,1,0:T(8,128)(2,1)S(1)}, bf16[2,48,384]{2,1,0:T(8,128)(2,1)S(1)}, u32[]{:S(2)}, u32[]{:S(2)}) collective-permute-start(bf16[2,48,384]{2,1,0:T(8,128)(2,1)S(1)} %get-tuple-element.41.own), channel_id=1, source_target_pairs={{0,4},{2,6},{4,0},{6,2},{1,5},{3,7},{5,1},{7,3},{8,12},{10,14},{12... | collective-permute-start | bytes 221192 | tf_op jit(solution)/shard_map/ppermute | solution.py:531
  66.2 5.6 %collective-permute-start.15 = (bf16[2,48,384]{2,1,0:T(8,128)(2,1)S(1)}, bf16[2,48,384]{2,1,0:T(8,128)(2,1)S(1)}, u32[]{:S(2)}, u32[]{:S(2)}) collective-permute-start(bf16[2,48,384]{2,1,0:T(8,128)(2,1)S(1)} %get-tuple-element.41.own), channel_id=1, source_target_pairs={{0,6},{2,0},{4,2},{6,4},{1,7},{3,1},{5,3},{7,5},{8,14},{10,8},{12,... | collective-permute-start | bytes 221192 | tf_op jit(solution)/shard_map/ppermute | solution.py:531
  75.0 7.6 %collective-permute-start.17 = (bf16[4,48,256]{2,1,0:T(8,128)(2,1)S(1)}, bf16[4,48,256]{2,1,0:T(8,128)(2,1)S(1)}, u32[]{:S(2)}, u32[]{:S(2)}) collective-permute-start(bf16[4,48,256]{2,1,0:T(8,128)(2,1)S(1)} %get-tuple-element.47), channel_id=1, source_target_pairs={{0,2},{2,4},{4,6},{6,0},{1,3},{3,5},{5,7},{7,1},{8,10},{10,12},{12... | collective-permute-start | bytes 294920 | tf_op jit(solution)/shard_map/ppermute | solution.py:557
  76.6 8.7 %collective-permute-start.18 = (bf16[4,48,256]{2,1,0:T(8,128)(2,1)S(1)}, bf16[4,48,256]{2,1,0:T(8,128)(2,1)S(1)}, u32[]{:S(2)}, u32[]{:S(2)}) collective-permute-start(bf16[4,48,256]{2,1,0:T(8,128)(2,1)S(1)} %get-tuple-element.48), channel_id=1, source_target_pairs={{0,4},{2,6},{4,0},{6,2},{1,5},{3,7},{5,1},{7,3},{8,12},{10,14},{12... | collective-permute-start | bytes 294920 | tf_op jit(solution)/shard_map/ppermute | solution.py:557
  78.1 7.2 %collective-permute-start.19 = (bf16[4,48,256]{2,1,0:T(8,128)(2,1)S(1)}, bf16[4,48,256]{2,1,0:T(8,128)(2,1)S(1)}, u32[]{:S(2)}, u32[]{:S(2)}) collective-permute-start(bf16[4,48,256]{2,1,0:T(8,128)(2,1)S(1)} %get-tuple-element.49), channel_id=1, source_target_pairs={{0,6},{2,0},{4,2},{6,4},{1,7},{3,1},{5,3},{7,5},{8,14},{10,8},{12,... | collective-permute-start | bytes 294920 | tf_op jit(solution)/shard_map/ppermute | solution.py:557
  79.0 7.7 %collective-permute-start.22 = (bf16[54,80,128]{2,1,0:T(8,128)(2,1)S(1)}, bf16[54,80,128]{2,1,0:T(8,128)(2,1)S(1)}, u32[]{:S(2)}, u32[]{:S(2)}) collective-permute-start(bf16[54,80,128]{2,1,0:T(8,128)(2,1)S(1)} %laid.13.refs_2_), channel_id=1, source_target_pairs={{0,8},{8,0},{1,9},{9,1},{2,10},{10,2},{3,11},{11,3},{4,12},{12,4},... | collective-permute-start | bytes 3317768 | tf_op jit(solution)/shard_map/ppermute | solution.py:195
  79.1 7.6 %collective-permute-start.24 = (bf16[18,80,128]{2,1,0:T(8,128)(2,1)S(1)}, bf16[18,80,128]{2,1,0:T(8,128)(2,1)S(1)}, u32[]{:S(2)}, u32[]{:S(2)}) collective-permute-start(bf16[18,80,128]{2,1,0:T(8,128)(2,1)S(1)} %laid.11.refs_1_), channel_id=1, source_target_pairs={{0,16},{1,17},{2,18},{3,19},{4,20},{5,21},{6,22},{7,23},{8,9},{9,8... | collective-permute-start | bytes 1105928 | tf_op jit(solution)/shard_map/ppermute | solution.py:488
  82.7 12.6 %collective-permute-start.25 = (bf16[18,80,128]{2,1,0:T(8,128)(2,1)S(1)}, bf16[18,80,128]{2,1,0:T(8,128)(2,1)S(1)}, u32[]{:S(2)}, u32[]{:S(2)}) collective-permute-start(bf16[18,80,128]{2,1,0:T(8,128)(2,1)S(1)} %laid.11.refs_1_), channel_id=1, source_target_pairs={{0,8},{8,0},{1,9},{9,1},{2,10},{10,2},{3,11},{11,3},{4,12},{12,4},... | collective-permute-start | bytes 1105928 | tf_op jit(solution)/shard_map/ppermute | solution.py:195
  85.3 3.0 %collective-permute-start.23 = (bf16[54,80,128]{2,1,0:T(8,128)(2,1)}, bf16[54,80,128]{2,1,0:T(8,128)(2,1)S(1)}, u32[]{:S(2)}, u32[]{:S(2)}) collective-permute-start(bf16[54,80,128]{2,1,0:T(8,128)(2,1)} %collective-permute-done.21.refs_3_), channel_id=1, source_target_pairs={{0,8},{8,0},{1,9},{9,1},{2,10},{10,2},{3,11},{11,3},{4,12},{12,4},... | collective-permute-start | bytes 3317768 | tf_op jit(solution)/shard_map/ppermute | solution.py:195
  86.7 8.6 %collective-permute-start.26 = (bf16[18,80,128]{2,1,0:T(8,128)(2,1)S(1)}, bf16[18,80,128]{2,1,0:T(8,128)(2,1)S(1)}, u32[]{:S(2)}, u32[]{:S(2)}) collective-permute-start(bf16[18,80,128]{2,1,0:T(8,128)(2,1)S(1)} %collective-permute-done.24.refs_2_), channel_id=1, source_target_pairs={{0,8},{8,0},{1,9},{9,1},{2,10},{10,2},{3,11},{11,3},{4,12},{12,4},... | collective-permute-start | bytes 1105928 | tf_op jit(solution)/shard_map/ppermute | solution.py:195
  (14 other events, 57.3 us)

commit v6 on v5

--- a/solution.py
+++ b/solution.py
@@ -121,7 +121,7 @@
         out_specs=VMEM,
         scratch_shapes=[pltpu.VMEM(weight.shape, BF) for weight in weights]
         + [pltpu.SemaphoreType.DMA((len(weights),))],
-        compiler_params=pltpu.CompilerParams(vmem_limit_bytes=52 * 1024 * 1024),
+        compiler_params=pltpu.CompilerParams(vmem_limit_bytes=36 * 1024 * 1024),
         name="pack_piece",
     )(place, *weights)
 
@@ -534,7 +534,6 @@
         next1 = across(block1, second)
         block2 = laid(*here1, cut=(part1, part2))
         block2 = laid(block2, after(across(block2, first), pooled))
-        others = after(others, block2)
         part = mid_weight.shape[2]
         bias = lax.dynamic_slice_in_dim(mid_bias, row * part, part, 0)
         rows = tall * row_count
@@ -556,7 +555,7 @@
         mids = [sent[0]] + [
             lax.ppermute(sent[by], "row", cyclic(row_count, by)) for by in range(1, row_count)
         ]
-        next1 = after(next1, sent[0])
+        next1 = after(next1, sent[0], block2)
         held1 = (block1, next1, far1, swap_cores(next1))
         next2 = after(across(block2, second), *mids)
         held2 = (block2, next2, swap_cores(block2), swap_cores(next2))

time: 99.4 us -> 98.5 us (level)
    unnamed x40 -> x34, local copies, waits for them, and re-layouts: 6.49 us -> 5.56 us
  transfers between devices with their start and end apart: 27 -> 27, of which waited for: 14 -> 12; matrix products, arithmetic and copies ran while one was open for 4% -> 3% of each run, Pallas kernels for 23% -> 23%
where the time goes in v6:
time: 98.5 us; the launch traced here: 98.1 us
  starting transfers between devices  35.7 us (36%)
  Pallas kernels  27.5 us (28%)
  waiting for transfers between devices  26.8 us (27%)
  local copies, waits for them, and re-layouts  7.31 us (7%)
    ppermute x6, starting transfers between devices, from_planes(): lax.ppermute(mine, 'row', cyclic(count, by))  14 us
    pallas_call x1, Pallas kernels, shards(): pl.pallas_call(functools.partial(encoder_body, size, sets, groups[0][1]),...  7.67 us
    ppermute x3, starting transfers between devices, shards(): lax.ppermute(pooled, 'row', cyclic(row_count, by))  7.58 us
    pallas_call x1, Pallas kernels, shards(): pl.pallas_call(functools.partial(joined_body, size, sets, groups[1][1]),...  7.05 us
    ppermute x6, waiting for transfers between devices, from_planes(): lax.ppermute(mine, 'row', cyclic(count, by))  6.24 us
    unnamed x34, local copies, waits for them, and re-layouts  5.56 us
    ppermute x6, starting transfers between devices, shards(): across = lambda block, pairs: lax.ppermute(block, AXES, pairs)  5.42 us
    ppermute x1, waiting for transfers between devices, shards(): above = lax.ppermute(tile, 'row', down)  5.05 us
  transfers between devices with their start and end apart: 27, of which 12 were waited for; matrix products, arithmetic and copies ran while one was open for 3% of the time, Pallas kernels for 23%

profile of v6, /device:TPU:0, one launch (start us, length us, event | category | flops | bytes accessed | tf_op | source)
XLA Modules:
  0.0 98.1 jit_solution(18427711538817144698)
XLA Ops:
  0.1 1.1 %copy-done.1 = bf16[9,320,80]{1,2,0:T(8,128)(2,1)S(1)} copy-done((bf16[9,320,80]{1,2,0:T(8,128)(2,1)S(1)}, bf16[9,320,80]{1,2,0:T(8,128)(2,1)}, u32[]{:S(2)}) %copy-start.1) | copy-done | bytes 460824
  1.2 1.0 %copy-done.2 = bf16[9,320,80]{1,2,0:T(8,128)(2,1)S(1)} copy-done((bf16[9,320,80]{1,2,0:T(8,128)(2,1)S(1)}, bf16[9,320,80]{1,2,0:T(8,128)(2,1)}, u32[]{:S(2)}) %copy-start.2) | copy-done | bytes 460824
  3.0 3.1 %collective-permute-start.3 = (bf16[6,80,128]{2,1,0:T(8,128)(2,1)S(1)}, bf16[6,80,128]{2,1,0:T(8,128)(2,1)S(1)}, u32[]{:S(2)}, u32[]{:S(2)}) collective-permute-start(bf16[6,80,128]{2,1,0:T(8,128)(2,1)S(1)} %pack_piece.1), channel_id=1, source_target_pairs={{0,2},{2,4},{4,6},{6,0},{1,3},{3,5},{5,7},{7,1},{8,10},{10,12},{12... | collective-permute-start | bytes 368648 | tf_op jit(solution)/shard_map/ppermute | solution.py:181
  6.1 2.6 %collective-permute-start.4 = (bf16[6,80,128]{2,1,0:T(8,128)(2,1)S(1)}, bf16[6,80,128]{2,1,0:T(8,128)(2,1)S(1)}, u32[]{:S(2)}, u32[]{:S(2)}) collective-permute-start(bf16[6,80,128]{2,1,0:T(8,128)(2,1)S(1)} %pack_piece.1), channel_id=1, source_target_pairs={{0,4},{2,6},{4,0},{6,2},{1,5},{3,7},{5,1},{7,3},{8,12},{10,14},{12... | collective-permute-start | bytes 368648 | tf_op jit(solution)/shard_map/ppermute | solution.py:181
  8.7 1.3 %collective-permute-start.5 = (bf16[6,80,128]{2,1,0:T(8,128)(2,1)S(1)}, bf16[6,80,128]{2,1,0:T(8,128)(2,1)S(1)}, u32[]{:S(2)}, u32[]{:S(2)}) collective-permute-start(bf16[6,80,128]{2,1,0:T(8,128)(2,1)S(1)} %pack_piece.1), channel_id=1, source_target_pairs={{0,6},{2,0},{4,2},{6,4},{1,7},{3,1},{5,3},{7,5},{8,14},{10,8},{12,... | collective-permute-start | bytes 368648 | tf_op jit(solution)/shard_map/ppermute | solution.py:181
  10.0 1.4 %pack_weights.3 = (bf16[48,80,128]{2,1,0:T(8,128)(2,1)S(1)}, bf16[6,80,128]{2,1,0:T(8,128)(2,1)}) custom-call(s32[4]{0:T(128)S(1)} %pad_add_fusion.place, bf16[9,80,320]{2,1,0:T(8,128)(2,1)S(1)} %bitcast.14, bf16[9,80,320]{2,1,0:T(8,128)(2,1)S(1)} %bitcast.16), custom_call_target="tpu_custom_call" | custom-call | tf_op jit(solution)/shard_map/pack_weights/pallas_call | solution.py:75
  11.4 1.2 %pack_weights.4 = (bf16[72,80,128]{2,1,0:T(8,128)(2,1)S(1)}, bf16[9,80,128]{2,1,0:T(8,128)(2,1)S(1)}) custom-call(s32[4]{0:T(128)S(1)} %pad_add_fusion.place, bf16[9,80,960]{2,1,0:T(8,128)(2,1)S(1)} %bitcast.17), custom_call_target="tpu_custom_call" | custom-call | tf_op jit(solution)/shard_map/pack_weights/pallas_call | solution.py:75
  12.6 1.1 %copy-done.5 = bf16[72,80,128]{2,1,0:T(8,128)(2,1)} copy-done((bf16[72,80,128]{2,1,0:T(8,128)(2,1)}, bf16[72,80,128]{2,1,0:T(8,128)(2,1)S(1)}, u32[]{:S(2)}) %copy-start.5) | copy-done | bytes 1474584
  14.7 2.1 %collective-permute-done.4.refs_1_ = bf16[6,80,128]{2,1,0:T(8,128)(2,1)S(1)} collective-permute-done((bf16[6,80,128]{2,1,0:T(8,128)(2,1)S(1)}, bf16[6,80,128]{2,1,0:T(8,128)(2,1)S(1)}, u32[]{:S(2)}, u32[]{:S(2)}) %collective-permute-start.4) | collective-permute-done | bytes 122912 | tf_op jit(solution)/shard_map/ppermute | solution.py:181
  17.3 1.6 %collective-permute-start.6 = (bf16[18,80,128]{2,1,0:T(8,128)(2,1)S(1)}, bf16[18,80,128]{2,1,0:T(8,128)(2,1)S(1)}, u32[]{:S(2)}, u32[]{:S(2)}) collective-permute-start(bf16[18,80,128]{2,1,0:T(8,128)(2,1)S(1)} %laid.8.refs_0_), channel_id=1, source_target_pairs={{0,1},{1,0},{2,3},{3,2},{4,5},{5,4},{6,7},{7,6},{8,24},{9,25},{10,... | collective-permute-start | bytes 1105928 | tf_op jit(solution)/shard_map/ppermute | solution.py:488
  18.9 3.1 %collective-permute-start.7 = (bf16[12,80,128]{2,1,0:T(8,128)(2,1)S(1)}, bf16[12,80,128]{2,1,0:T(8,128)(2,1)S(1)}, u32[]{:S(2)}, u32[]{:S(2)}) collective-permute-start(bf16[12,80,128]{2,1,0:T(8,128)(2,1)S(1)} %laid.7), channel_id=1, source_target_pairs={{0,2},{2,4},{4,6},{6,0},{1,3},{3,5},{5,7},{7,1},{8,10},{10,12},{12... | collective-permute-start | bytes 737288 | tf_op jit(solution)/shard_map/ppermute | solution.py:181
  22.1 2.6 %collective-permute-start = (bf16[4,64,320]{2,1,0:T(8,128)(2,1)S(1)}, bf16[4,64,320]{2,1,0:T(8,128)(2,1)}, u32[]{:S(2)}, u32[]{:S(2)}) collective-permute-start(bf16[4,64,320]{2,1,0:T(8,128)(2,1)S(1)} %dynamic-slice_bitcast_fusion), channel_id=1, source_target_pairs={{0,2},{2,4},{4,6},{1,3},{3,5},{5,7},{8,10},{10,12},{12,14},{9,11},... | collective-permute-start | bytes 491528 | tf_op jit(solution)/shard_map/ppermute | solution.py:468
  24.7 1.3 %collective-permute-start.1 = (bf16[4,64,320]{2,1,0:T(8,128)(2,1)S(1)}, bf16[4,64,320]{2,1,0:T(8,128)(2,1)}, u32[]{:S(2)}, u32[]{:S(2)}) collective-permute-start(bf16[4,64,320]{2,1,0:T(8,128)(2,1)S(1)} %dynamic-slice_bitcast_fusion), channel_id=1, source_target_pairs={{2,0},{4,2},{6,4},{3,1},{5,3},{7,5},{10,8},{12,10},{14,12},{11,9},... | collective-permute-start | bytes 491528 | tf_op jit(solution)/shard_map/ppermute | solution.py:469
  26.3 5.0 %collective-permute-done = bf16[4,64,320]{2,1,0:T(8,128)(2,1)} collective-permute-done((bf16[4,64,320]{2,1,0:T(8,128)(2,1)S(1)}, bf16[4,64,320]{2,1,0:T(8,128)(2,1)}, u32[]{:S(2)}, u32[]{:S(2)}) %collective-permute-start) | collective-permute-done | bytes 163872 | tf_op jit(solution)/shard_map/ppermute | solution.py:468
  31.4 1.6 %collective-permute-done.1 = bf16[4,64,320]{2,1,0:T(8,128)(2,1)} collective-permute-done((bf16[4,64,320]{2,1,0:T(8,128)(2,1)S(1)}, bf16[4,64,320]{2,1,0:T(8,128)(2,1)}, u32[]{:S(2)}, u32[]{:S(2)}) %collective-permute-start.1) | collective-permute-done | bytes 163872 | tf_op jit(solution)/shard_map/ppermute | solution.py:469
  34.8 2.9 %collective-permute-start.10 = (bf16[12,80,128]{2,1,0:T(8,128)(2,1)S(1)}, bf16[12,80,128]{2,1,0:T(8,128)(2,1)S(1)}, u32[]{:S(2)}, u32[]{:S(2)}) collective-permute-start(bf16[12,80,128]{2,1,0:T(8,128)(2,1)S(1)} %laid.7), channel_id=1, source_target_pairs={{0,6},{2,0},{4,2},{6,4},{1,7},{3,1},{5,3},{7,5},{8,14},{10,8},{12,... | collective-permute-start | bytes 737288 | tf_op jit(solution)/shard_map/ppermute | solution.py:181
  40.4 4.1 %collective-permute-done.2 = bf16[12,8,320]{2,1,0:T(8,128)(2,1)S(1)} collective-permute-done((bf16[12,8,320]{2,1,0:T(8,128)(2,1)S(1)}, bf16[12,8,320]{2,1,0:T(8,128)(2,1)S(1)}, u32[]{:S(2)}, u32[]{:S(2)}) %collective-permute-start.2) | collective-permute-done | bytes 61472 | tf_op jit(solution)/shard_map/ppermute | solution.py:473
  44.5 4.2 %collective-permute-done.9.refs_1_ = bf16[12,80,128]{2,1,0:T(8,128)(2,1)S(1)} collective-permute-done((bf16[12,80,128]{2,1,0:T(8,128)(2,1)S(1)}, bf16[12,80,128]{2,1,0:T(8,128)(2,1)S(1)}, u32[]{:S(2)}, u32[]{:S(2)}) %collective-permute-start.9) | collective-permute-done | bytes 245792 | tf_op jit(solution)/shard_map/ppermute | solution.py:181
  51.1 7.7 %encoder.1 = (bf16[640,384]{1,0:T(8,128)(2,1)S(1)}, bf16[2,48,384]{2,1,0:T(8,128)(2,1)S(1)}) custom-call(s32[4]{0:T(128)S(1)} %pad_add_fusion.place, bf16[960,384]{1,0:T(8,128)(2,1)S(1)} %bitcast.18, f32[1,320]{1,0:T(1,128)S(1)} %reshape.19.bias1, f32[1,320]{1,0:T(1,128)S(1)} %reshape.20.bias2, bf16[48,80,128]{2,1,0:T(8,128)(2,1)S(1)} %get-tuple-element.29.refs_0_, ...), custom_call_target="tpu_custom_call" | custom-call | flops 21233664000 | bytes 1048576 | tf_op jit(solution)/shard_map/encoder/pallas_call | solution.py:510
  59.5 5.1 %collective-permute-start.13 = (bf16[2,48,384]{2,1,0:T(8,128)(2,1)S(1)}, bf16[2,48,384]{2,1,0:T(8,128)(2,1)S(1)}, u32[]{:S(2)}, u32[]{:S(2)}) collective-permute-start(bf16[2,48,384]{2,1,0:T(8,128)(2,1)S(1)} %get-tuple-element.38.own), channel_id=1, source_target_pairs={{0,2},{2,4},{4,6},{6,0},{1,3},{3,5},{5,7},{7,1},{8,10},{10,12},{12... | collective-permute-start | bytes 221192 | tf_op jit(solution)/shard_map/ppermute | solution.py:531
  65.6 1.5 %collective-permute-start.15 = (bf16[2,48,384]{2,1,0:T(8,128)(2,1)S(1)}, bf16[2,48,384]{2,1,0:T(8,128)(2,1)S(1)}, u32[]{:S(2)}, u32[]{:S(2)}) collective-permute-start(bf16[2,48,384]{2,1,0:T(8,128)(2,1)S(1)} %get-tuple-element.38.own), channel_id=1, source_target_pairs={{0,6},{2,0},{4,2},{6,4},{1,7},{3,1},{5,3},{7,5},{8,14},{10,8},{12,... | collective-permute-start | bytes 221192 | tf_op jit(solution)/shard_map/ppermute | solution.py:531
  68.7 2.5 %collective-permute-done.14.refs_1_ = bf16[2,48,384]{2,1,0:T(8,128)(2,1)S(1)} collective-permute-done((bf16[2,48,384]{2,1,0:T(8,128)(2,1)S(1)}, bf16[2,48,384]{2,1,0:T(8,128)(2,1)S(1)}, u32[]{:S(2)}, u32[]{:S(2)}) %collective-permute-start.14) | collective-permute-done | bytes 73760 | tf_op jit(solution)/shard_map/ppermute | solution.py:531
  71.2 1.2 %copy-done.7 = bf16[9,320,160]{1,2,0:T(8,128)(2,1)S(1)} copy-done((bf16[9,320,160]{1,2,0:T(8,128)(2,1)S(1)}, bf16[9,320,160]{1,2,0:T(8,128)(2,1)}, u32[]{:S(2)}) %copy-start.7) | copy-done | bytes 921624
  72.5 2.0 %middle.1 = (bf16[4,48,256]{2,1,0:T(8,128)(2,1)S(1)}, bf16[4,48,256]{2,1,0:T(8,128)(2,1)S(1)}, bf16[4,48,256]{2,1,0:T(8,128)(2,1)S(1)}, bf16[4,48,256]{2,1,0:T(8,128)(2,1)S(1)}) custom-call(s32[4]{0:T(128)S(1)} %pad_add_fusion.place, bf16[2,48,384]{2,1,0:T(8,128)(2,1)S(1)} %get-tuple-element.38.own, bf16[2,48,384]{2,1,0:T(8,128)(2,1)S(1)} %collective-permute-done.13.refs_0_, ...), custom_call_target="tpu_custom_call" | custom-call | flops 4718592000 | bytes 1048576 | tf_op jit(solution)/shard_map/middle/pallas_call | solution.py:540
  74.4 1.7 %collective-permute-start.16 = (bf16[4,48,256]{2,1,0:T(8,128)(2,1)S(1)}, bf16[4,48,256]{2,1,0:T(8,128)(2,1)S(1)}, u32[]{:S(2)}, u32[]{:S(2)}) collective-permute-start(bf16[4,48,256]{2,1,0:T(8,128)(2,1)S(1)} %get-tuple-element.40), channel_id=1, source_target_pairs={{0,2},{2,4},{4,6},{6,0},{1,3},{3,5},{5,7},{7,1},{8,10},{10,12},{12... | collective-permute-start | bytes 294920 | tf_op jit(solution)/shard_map/ppermute | solution.py:556
  76.1 1.8 %collective-permute-start.17 = (bf16[4,48,256]{2,1,0:T(8,128)(2,1)S(1)}, bf16[4,48,256]{2,1,0:T(8,128)(2,1)S(1)}, u32[]{:S(2)}, u32[]{:S(2)}) collective-permute-start(bf16[4,48,256]{2,1,0:T(8,128)(2,1)S(1)} %get-tuple-element.41), channel_id=1, source_target_pairs={{0,4},{2,6},{4,0},{6,2},{1,5},{3,7},{5,1},{7,3},{8,12},{10,14},{12... | collective-permute-start | bytes 294920 | tf_op jit(solution)/shard_map/ppermute | solution.py:556
  79.2 1.6 %collective-permute-start.24 = (bf16[18,80,128]{2,1,0:T(8,128)(2,1)S(1)}, bf16[18,80,128]{2,1,0:T(8,128)(2,1)S(1)}, u32[]{:S(2)}, u32[]{:S(2)}) collective-permute-start(bf16[18,80,128]{2,1,0:T(8,128)(2,1)S(1)} %laid.13.refs_1_), channel_id=1, source_target_pairs={{0,16},{1,17},{2,18},{3,19},{4,20},{5,21},{6,22},{7,23},{8,9},{9,8... | collective-permute-start | bytes 1105928 | tf_op jit(solution)/shard_map/ppermute | solution.py:488
  80.8 1.2 %collective-permute-done.16.refs_1_ = bf16[4,48,256]{2,1,0:T(8,128)(2,1)S(1)} collective-permute-done((bf16[4,48,256]{2,1,0:T(8,128)(2,1)S(1)}, bf16[4,48,256]{2,1,0:T(8,128)(2,1)S(1)}, u32[]{:S(2)}, u32[]{:S(2)}) %collective-permute-start.16) | collective-permute-done | bytes 98336 | tf_op jit(solution)/shard_map/ppermute | solution.py:556
  82.0 2.4 %collective-permute-done.17.refs_2_ = bf16[4,48,256]{2,1,0:T(8,128)(2,1)S(1)} collective-permute-done((bf16[4,48,256]{2,1,0:T(8,128)(2,1)S(1)}, bf16[4,48,256]{2,1,0:T(8,128)(2,1)S(1)}, u32[]{:S(2)}, u32[]{:S(2)}) %collective-permute-start.17) | collective-permute-done | bytes 98336 | tf_op jit(solution)/shard_map/ppermute | solution.py:556
  85.0 1.7 %collective-permute-done.24.refs_2_ = bf16[18,80,128]{2,1,0:T(8,128)(2,1)S(1)} collective-permute-done((bf16[18,80,128]{2,1,0:T(8,128)(2,1)S(1)}, bf16[18,80,128]{2,1,0:T(8,128)(2,1)S(1)}, u32[]{:S(2)}, u32[]{:S(2)}) %collective-permute-start.24) | collective-permute-done | bytes 368672 | tf_op jit(solution)/shard_map/ppermute | solution.py:488
  87.4 7.1 %joined.1.refined = bf16[480,384]{1,0:T(8,128)(2,1)S(1)} custom-call(s32[4]{0:T(128)S(1)} %pad_add_fusion.place, bf16[640,384]{1,0:T(8,128)(2,1)S(1)} %copy-done.11, f32[1,320]{1,0:T(1,128)S(1)} %reshape.21.bias, bf16[5,4,48,128]{3,2,1,0:T(8,128)(2,1)S(1)} %field.1.refs_0_, bf16[72,80,128]{2,1,0:T(8,128)(2,1)S(1)} %copy-done.6, ...), custom_call_target="tpu_custom_call" | custom-call | flops 10616832000 | bytes 1048576 | tf_op jit(solution)/shard_map/joined/pallas_call | solution.py:594
  94.5 3.5 %last.1 = bf16[1,4,64,320]{3,2,1,0:T(8,128)(2,1)} custom-call(s32[4]{0:T(128)S(1)} %pad_add_fusion.place, bf16[480,384]{1,0:T(8,128)(2,1)S(1)} %joined.1.refined, f32[1,320]{1,0:T(1,128)S(1)} %reshape.23.bias, bf16[24,80,128]{2,1,0:T(8,128)(2,1)S(1)} %copy-done.9, bf16[18,80,128]{2,1,0:T(8,128)(2,1)S(1)} %laid.13.refs_1_, ...), custom_call_target="tpu_custom_call" | custom-call | flops 2359296000 | bytes 1048576 | tf_op jit(solution)/shard_map/last/pallas_call | solution.py:610
  (83 shorter events, 15.4 us)
Async XLA Ops:
  0.0 22.0 %copy-start = (bf16[2,4,64,320]{3,2,1,0:T(8,128)(2,1)S(1)}, bf16[2,4,64,320]{3,2,1,0:T(8,128)(2,1)}, u32[]{:S(2)}) copy-start(bf16[2,4,64,320]{3,2,1,0:T(8,128)(2,1)} %param.11) | copy-start | bytes 983044
  2.2 9.2 %copy-start.3 = (bf16[9,960,80]{1,2,0:T(8,128)(2,1)S(1)}, bf16[9,960,80]{1,2,0:T(8,128)(2,1)}, u32[]{:S(2)}) copy-start(bf16[9,960,80]{1,2,0:T(8,128)(2,1)} %param.18) | copy-start | bytes 4147204
  3.0 10.7 %copy-start.4 = (bf16[9,320,80]{1,2,0:T(8,128)(2,1)S(1)}, bf16[9,320,80]{1,2,0:T(8,128)(2,1)}, u32[]{:S(2)}) copy-start(bf16[9,320,80]{1,2,0:T(8,128)(2,1)} %param.20) | copy-start | bytes 1382404
  3.0 11.7 %collective-permute-start.3 = (bf16[6,80,128]{2,1,0:T(8,128)(2,1)S(1)}, bf16[6,80,128]{2,1,0:T(8,128)(2,1)S(1)}, u32[]{:S(2)}, u32[]{:S(2)}) collective-permute-start(bf16[6,80,128]{2,1,0:T(8,128)(2,1)S(1)} %pack_piece.1), channel_id=1, source_target_pairs={{0,2},{2,4},{4,6},{6,0},{1,3},{3,5},{5,7},{7,1},{8,10},{10,12},{12... | collective-permute-start | bytes 368648 | tf_op jit(solution)/shard_map/ppermute | solution.py:181
  6.1 10.7 %collective-permute-start.4 = (bf16[6,80,128]{2,1,0:T(8,128)(2,1)S(1)}, bf16[6,80,128]{2,1,0:T(8,128)(2,1)S(1)}, u32[]{:S(2)}, u32[]{:S(2)}) collective-permute-start(bf16[6,80,128]{2,1,0:T(8,128)(2,1)S(1)} %pack_piece.1), channel_id=1, source_target_pairs={{0,4},{2,6},{4,0},{6,2},{1,5},{3,7},{5,1},{7,3},{8,12},{10,14},{12... | collective-permute-start | bytes 368648 | tf_op jit(solution)/shard_map/ppermute | solution.py:181
  8.7 8.1 %collective-permute-start.5 = (bf16[6,80,128]{2,1,0:T(8,128)(2,1)S(1)}, bf16[6,80,128]{2,1,0:T(8,128)(2,1)S(1)}, u32[]{:S(2)}, u32[]{:S(2)}) collective-permute-start(bf16[6,80,128]{2,1,0:T(8,128)(2,1)S(1)} %pack_piece.1), channel_id=1, source_target_pairs={{0,6},{2,0},{4,2},{6,4},{1,7},{3,1},{5,3},{7,5},{8,14},{10,8},{12,... | collective-permute-start | bytes 368648 | tf_op jit(solution)/shard_map/ppermute | solution.py:181
  17.3 8.7 %collective-permute-start.6 = (bf16[18,80,128]{2,1,0:T(8,128)(2,1)S(1)}, bf16[18,80,128]{2,1,0:T(8,128)(2,1)S(1)}, u32[]{:S(2)}, u32[]{:S(2)}) collective-permute-start(bf16[18,80,128]{2,1,0:T(8,128)(2,1)S(1)} %laid.8.refs_0_), channel_id=1, source_target_pairs={{0,1},{1,0},{2,3},{3,2},{4,5},{5,4},{6,7},{7,6},{8,24},{9,25},{10,... | collective-permute-start | bytes 1105928 | tf_op jit(solution)/shard_map/ppermute | solution.py:488
  18.9 14.0 %collective-permute-start.7 = (bf16[12,80,128]{2,1,0:T(8,128)(2,1)S(1)}, bf16[12,80,128]{2,1,0:T(8,128)(2,1)S(1)}, u32[]{:S(2)}, u32[]{:S(2)}) collective-permute-start(bf16[12,80,128]{2,1,0:T(8,128)(2,1)S(1)} %laid.7), channel_id=1, source_target_pairs={{0,2},{2,4},{4,6},{6,0},{1,3},{3,5},{5,7},{7,1},{8,10},{10,12},{12... | collective-permute-start | bytes 737288 | tf_op jit(solution)/shard_map/ppermute | solution.py:181
  22.0 26.6 %copy-start.12 = (f32[320]{0:T(512)S(1)}, f32[320]{0:T(512)}, u32[]{:S(2)}) copy-start(f32[320]{0:T(512)} %param.13) | copy-start | bytes 3844
  22.1 26.6 %copy-start.13 = (f32[320]{0:T(512)S(1)}, f32[320]{0:T(512)}, u32[]{:S(2)}) copy-start(f32[320]{0:T(512)} %param.15) | copy-start | bytes 3844
  22.1 9.3 %collective-permute-start = (bf16[4,64,320]{2,1,0:T(8,128)(2,1)S(1)}, bf16[4,64,320]{2,1,0:T(8,128)(2,1)}, u32[]{:S(2)}, u32[]{:S(2)}) collective-permute-start(bf16[4,64,320]{2,1,0:T(8,128)(2,1)S(1)} %dynamic-slice_bitcast_fusion), channel_id=1, source_target_pairs={{0,2},{2,4},{4,6},{1,3},{3,5},{5,7},{8,10},{10,12},{12,14},{9,11},... | collective-permute-start | bytes 491528 | tf_op jit(solution)/shard_map/ppermute | solution.py:468
  24.7 8.3 %collective-permute-start.1 = (bf16[4,64,320]{2,1,0:T(8,128)(2,1)S(1)}, bf16[4,64,320]{2,1,0:T(8,128)(2,1)}, u32[]{:S(2)}, u32[]{:S(2)}) collective-permute-start(bf16[4,64,320]{2,1,0:T(8,128)(2,1)S(1)} %dynamic-slice_bitcast_fusion), channel_id=1, source_target_pairs={{2,0},{4,2},{6,4},{3,1},{5,3},{7,5},{10,8},{12,10},{14,12},{11,9},... | collective-permute-start | bytes 491528 | tf_op jit(solution)/shard_map/ppermute | solution.py:469
  32.9 15.7 %collective-permute-start.8 = (bf16[36,80,128]{2,1,0:T(8,128)(2,1)S(1)}, bf16[36,80,128]{2,1,0:T(8,128)(2,1)}, u32[]{:S(2)}, u32[]{:S(2)}) collective-permute-start(bf16[36,80,128]{2,1,0:T(8,128)(2,1)S(1)} %laid.9.refs_1_), channel_id=1, source_target_pairs={{0,16},{1,17},{2,18},{3,19},{4,20},{5,21},{6,22},{7,23},{8,9},{9,8... | collective-permute-start | bytes 2211848 | tf_op jit(solution)/shard_map/ppermute | solution.py:488
  33.9 14.8 %collective-permute-start.9 = (bf16[12,80,128]{2,1,0:T(8,128)(2,1)S(1)}, bf16[12,80,128]{2,1,0:T(8,128)(2,1)S(1)}, u32[]{:S(2)}, u32[]{:S(2)}) collective-permute-start(bf16[12,80,128]{2,1,0:T(8,128)(2,1)S(1)} %laid.7), channel_id=1, source_target_pairs={{0,4},{2,6},{4,0},{6,2},{1,5},{3,7},{5,1},{7,3},{8,12},{10,14},{12... | collective-permute-start | bytes 737288 | tf_op jit(solution)/shard_map/ppermute | solution.py:181
  34.8 13.8 %collective-permute-start.10 = (bf16[12,80,128]{2,1,0:T(8,128)(2,1)S(1)}, bf16[12,80,128]{2,1,0:T(8,128)(2,1)S(1)}, u32[]{:S(2)}, u32[]{:S(2)}) collective-permute-start(bf16[12,80,128]{2,1,0:T(8,128)(2,1)S(1)} %laid.7), channel_id=1, source_target_pairs={{0,6},{2,0},{4,2},{6,4},{1,7},{3,1},{5,3},{7,5},{8,14},{10,8},{12,... | collective-permute-start | bytes 737288 | tf_op jit(solution)/shard_map/ppermute | solution.py:181
  39.7 4.8 %collective-permute-start.2 = (bf16[12,8,320]{2,1,0:T(8,128)(2,1)S(1)}, bf16[12,8,320]{2,1,0:T(8,128)(2,1)S(1)}, u32[]{:S(2)}, u32[]{:S(2)}) collective-permute-start(bf16[12,8,320]{2,1,0:T(8,128)(2,1)S(1)} %slice_select_fusion), channel_id=1, source_target_pairs={{0,1},{1,0},{2,3},{3,2},{4,5},{5,4},{6,7},{7,6},{8,9},{9,8},{10,11... | collective-permute-start | bytes 184328 | tf_op jit(solution)/shard_map/ppermute | solution.py:473
  40.4 9.8 %collective-permute-start.11 = (bf16[36,80,128]{2,1,0:T(8,128)(2,1)S(1)}, bf16[36,80,128]{2,1,0:T(8,128)(2,1)S(1)}, u32[]{:S(2)}, u32[]{:S(2)}) collective-permute-start(bf16[36,80,128]{2,1,0:T(8,128)(2,1)S(1)} %laid.9.refs_1_), channel_id=1, source_target_pairs={{0,8},{8,0},{1,9},{9,1},{2,10},{10,2},{3,11},{11,3},{4,12},{12,4},... | collective-permute-start | bytes 2211848 | tf_op jit(solution)/shard_map/ppermute | solution.py:195
  48.7 2.4 %collective-permute-start.12 = (bf16[36,80,128]{2,1,0:T(8,128)(2,1)}, bf16[36,80,128]{2,1,0:T(8,128)(2,1)S(1)}, u32[]{:S(2)}, u32[]{:S(2)}) collective-permute-start(bf16[36,80,128]{2,1,0:T(8,128)(2,1)} %collective-permute-done.8.refs_2_), channel_id=1, source_target_pairs={{0,8},{8,0},{1,9},{9,1},{2,10},{10,2},{3,11},{11,3},{4,12},{12,4},... | collective-permute-start | bytes 2211848 | tf_op jit(solution)/shard_map/ppermute | solution.py:195
  49.7 9.6 %collective-permute-start.19 = (bf16[27,80,128]{2,1,0:T(8,128)(2,1)S(1)}, bf16[27,80,128]{2,1,0:T(8,128)(2,1)S(1)}, u32[]{:S(2)}, u32[]{:S(2)}) collective-permute-start(bf16[27,80,128]{2,1,0:T(8,128)(2,1)S(1)} %laid.10.refs_0_), channel_id=1, source_target_pairs={{0,1},{1,0},{2,3},{3,2},{4,5},{5,4},{6,7},{7,6},{8,24},{9,25},{10,... | collective-permute-start | bytes 1658888 | tf_op jit(solution)/shard_map/ppermute | solution.py:488
  59.4 19.7 %collective-permute-start.20 = (bf16[54,80,128]{2,1,0:T(8,128)(2,1)S(1)}, bf16[54,80,128]{2,1,0:T(8,128)(2,1)}, u32[]{:S(2)}, u32[]{:S(2)}) collective-permute-start(bf16[54,80,128]{2,1,0:T(8,128)(2,1)S(1)} %laid.11.refs_2_), channel_id=1, source_target_pairs={{0,16},{1,17},{2,18},{3,19},{4,20},{5,21},{6,22},{7,23},{8,9},{9,8... | collective-permute-start | bytes 3317768 | tf_op jit(solution)/shard_map/ppermute | solution.py:488
  59.5 9.3 %collective-permute-start.13 = (bf16[2,48,384]{2,1,0:T(8,128)(2,1)S(1)}, bf16[2,48,384]{2,1,0:T(8,128)(2,1)S(1)}, u32[]{:S(2)}, u32[]{:S(2)}) collective-permute-start(bf16[2,48,384]{2,1,0:T(8,128)(2,1)S(1)} %get-tuple-element.38.own), channel_id=1, source_target_pairs={{0,2},{2,4},{4,6},{6,0},{1,3},{3,5},{5,7},{7,1},{8,10},{10,12},{12... | collective-permute-start | bytes 221192 | tf_op jit(solution)/shard_map/ppermute | solution.py:531
  64.6 6.6 %collective-permute-start.14 = (bf16[2,48,384]{2,1,0:T(8,128)(2,1)S(1)}, bf16[2,48,384]{2,1,0:T(8,128)(2,1)S(1)}, u32[]{:S(2)}, u32[]{:S(2)}) collective-permute-start(bf16[2,48,384]{2,1,0:T(8,128)(2,1)S(1)} %get-tuple-element.38.own), channel_id=1, source_target_pairs={{0,4},{2,6},{4,0},{6,2},{1,5},{3,7},{5,1},{7,3},{8,12},{10,14},{12... | collective-permute-start | bytes 221192 | tf_op jit(solution)/shard_map/ppermute | solution.py:531
  65.6 5.7 %collective-permute-start.15 = (bf16[2,48,384]{2,1,0:T(8,128)(2,1)S(1)}, bf16[2,48,384]{2,1,0:T(8,128)(2,1)S(1)}, u32[]{:S(2)}, u32[]{:S(2)}) collective-permute-start(bf16[2,48,384]{2,1,0:T(8,128)(2,1)S(1)} %get-tuple-element.38.own), channel_id=1, source_target_pairs={{0,6},{2,0},{4,2},{6,4},{1,7},{3,1},{5,3},{7,5},{8,14},{10,8},{12,... | collective-permute-start | bytes 221192 | tf_op jit(solution)/shard_map/ppermute | solution.py:531
  68.1 10.5 %collective-permute-start.21 = (bf16[9,80,128]{2,1,0:T(8,128)(2,1)S(1)}, bf16[9,80,128]{2,1,0:T(8,128)(2,1)S(1)}, u32[]{:S(2)}, u32[]{:S(2)}) collective-permute-start(bf16[9,80,128]{2,1,0:T(8,128)(2,1)S(1)} %laid.12.refs_0_), channel_id=1, source_target_pairs={{0,1},{1,0},{2,3},{3,2},{4,5},{5,4},{6,7},{7,6},{8,24},{9,25},{10,... | collective-permute-start | bytes 552968 | tf_op jit(solution)/shard_map/ppermute | solution.py:488
  74.4 7.6 %collective-permute-start.16 = (bf16[4,48,256]{2,1,0:T(8,128)(2,1)S(1)}, bf16[4,48,256]{2,1,0:T(8,128)(2,1)S(1)}, u32[]{:S(2)}, u32[]{:S(2)}) collective-permute-start(bf16[4,48,256]{2,1,0:T(8,128)(2,1)S(1)} %get-tuple-element.40), channel_id=1, source_target_pairs={{0,2},{2,4},{4,6},{6,0},{1,3},{3,5},{5,7},{7,1},{8,10},{10,12},{12... | collective-permute-start | bytes 294920 | tf_op jit(solution)/shard_map/ppermute | solution.py:556
  76.1 8.3 %collective-permute-start.17 = (bf16[4,48,256]{2,1,0:T(8,128)(2,1)S(1)}, bf16[4,48,256]{2,1,0:T(8,128)(2,1)S(1)}, u32[]{:S(2)}, u32[]{:S(2)}) collective-permute-start(bf16[4,48,256]{2,1,0:T(8,128)(2,1)S(1)} %get-tuple-element.41), channel_id=1, source_target_pairs={{0,4},{2,6},{4,0},{6,2},{1,5},{3,7},{5,1},{7,3},{8,12},{10,14},{12... | collective-permute-start | bytes 294920 | tf_op jit(solution)/shard_map/ppermute | solution.py:556
  77.9 6.5 %collective-permute-start.18 = (bf16[4,48,256]{2,1,0:T(8,128)(2,1)S(1)}, bf16[4,48,256]{2,1,0:T(8,128)(2,1)S(1)}, u32[]{:S(2)}, u32[]{:S(2)}) collective-permute-start(bf16[4,48,256]{2,1,0:T(8,128)(2,1)S(1)} %get-tuple-element.42), channel_id=1, source_target_pairs={{0,6},{2,0},{4,2},{6,4},{1,7},{3,1},{5,3},{7,5},{8,14},{10,8},{12,... | collective-permute-start | bytes 294920 | tf_op jit(solution)/shard_map/ppermute | solution.py:556
  78.6 8.2 %collective-permute-start.22 = (bf16[54,80,128]{2,1,0:T(8,128)(2,1)S(1)}, bf16[54,80,128]{2,1,0:T(8,128)(2,1)S(1)}, u32[]{:S(2)}, u32[]{:S(2)}) collective-permute-start(bf16[54,80,128]{2,1,0:T(8,128)(2,1)S(1)} %laid.11.refs_2_), channel_id=1, source_target_pairs={{0,8},{8,0},{1,9},{9,1},{2,10},{10,2},{3,11},{11,3},{4,12},{12,4},... | collective-permute-start | bytes 3317768 | tf_op jit(solution)/shard_map/ppermute | solution.py:195
  79.2 7.6 %collective-permute-start.24 = (bf16[18,80,128]{2,1,0:T(8,128)(2,1)S(1)}, bf16[18,80,128]{2,1,0:T(8,128)(2,1)S(1)}, u32[]{:S(2)}, u32[]{:S(2)}) collective-permute-start(bf16[18,80,128]{2,1,0:T(8,128)(2,1)S(1)} %laid.13.refs_1_), channel_id=1, source_target_pairs={{0,16},{1,17},{2,18},{3,19},{4,20},{5,21},{6,22},{7,23},{8,9},{9,8... | collective-permute-start | bytes 1105928 | tf_op jit(solution)/shard_map/ppermute | solution.py:488
  82.0 12.4 %collective-permute-start.25 = (bf16[18,80,128]{2,1,0:T(8,128)(2,1)S(1)}, bf16[18,80,128]{2,1,0:T(8,128)(2,1)S(1)}, u32[]{:S(2)}, u32[]{:S(2)}) collective-permute-start(bf16[18,80,128]{2,1,0:T(8,128)(2,1)S(1)} %laid.13.refs_1_), channel_id=1, source_target_pairs={{0,8},{8,0},{1,9},{9,1},{2,10},{10,2},{3,11},{11,3},{4,12},{12,4},... | collective-permute-start | bytes 1105928 | tf_op jit(solution)/shard_map/ppermute | solution.py:195
  84.4 3.0 %collective-permute-start.23 = (bf16[54,80,128]{2,1,0:T(8,128)(2,1)}, bf16[54,80,128]{2,1,0:T(8,128)(2,1)S(1)}, u32[]{:S(2)}, u32[]{:S(2)}) collective-permute-start(bf16[54,80,128]{2,1,0:T(8,128)(2,1)} %collective-permute-done.20.refs_3_), channel_id=1, source_target_pairs={{0,8},{8,0},{1,9},{9,1},{2,10},{10,2},{3,11},{11,3},{4,12},{12,4},... | collective-permute-start | bytes 3317768 | tf_op jit(solution)/shard_map/ppermute | solution.py:195
  86.7 7.7 %collective-permute-start.26 = (bf16[18,80,128]{2,1,0:T(8,128)(2,1)S(1)}, bf16[18,80,128]{2,1,0:T(8,128)(2,1)S(1)}, u32[]{:S(2)}, u32[]{:S(2)}) collective-permute-start(bf16[18,80,128]{2,1,0:T(8,128)(2,1)S(1)} %collective-permute-done.24.refs_2_), channel_id=1, source_target_pairs={{0,8},{8,0},{1,9},{9,1},{2,10},{10,2},{3,11},{11,3},{4,12},{12,4},... | collective-permute-start | bytes 1105928 | tf_op jit(solution)/shard_map/ppermute | solution.py:195
  (11 other events, 45.7 us)
